TPU v7x, 32 devices: a whole 2x2x4 slice. The times are simulated.
32 devices in a mesh: dp: 16 (over z, y, core), seq: 2 (over x).
Axes of the slice: x: 2, y: 2, z: 4, core: 2. Of those that a mesh axis runs over, the one named last changes fastest.
Arguments:
- tokens: bfloat16 [32, 1024, 768], P('dp', 'seq'), may hold values from -6 to 6
- cotangent: bfloat16 [32, 1024, 768], P('dp', 'seq'), may hold values from -6 to 6
- time_index: int32 [32], P('dp'), may hold values from 0 to 999
- span_starts: int32 [32], P('dp'), may hold values from 0 to 511, as said below
- span_lengths: int32 [32], P('dp'), may hold values from 2 to 1024, as said below
- w_ada: bfloat16 [128, 4608], replicated, may hold values from -0.5 to 0.5
- b_ada: float32 [4608], replicated, may hold values from -3 to 3
- gain_one: float32 [768], replicated, may hold values from 0.5 to 1.5
- w_qkv: bfloat16 [768, 2304], replicated, may hold values from -0.21875 to 0.21875
- w_out: bfloat16 [768, 768], replicated, may hold values from -4 to 4
- gain_two: float32 [768], replicated, may hold values from 0.5 to 1.5
- w_up: bfloat16 [768, 3072], replicated, may hold values from -0.21875 to 0.21875
- b_up: float32 [3072], replicated, may hold values from -3 to 3
- w_down: bfloat16 [3072, 768], replicated, may hold values from -0.109375 to 0.109375
- b_down: float32 [768], replicated, may hold values from -3 to 3
Outputs:
- output: bfloat16 [32, 1024, 768], P('dp', 'seq')
- grad_tokens: float32 [32, 1024, 768], P('dp', 'seq')
- grad_w_ada: float32 [128, 4608], P('dp')
- grad_b_ada: float32 [4608], P('dp')
- grad_gain_one: float32 [768], P('dp')
- grad_w_qkv: float32 [768, 2304], P('dp')
- grad_w_out: float32 [768, 768], P('dp')
- grad_gain_two: float32 [768], P('dp')
- grad_w_up: float32 [768, 3072], P('dp')
- grad_b_up: float32 [3072], P('dp')
- grad_w_down: float32 [3072, 768], P('dp')
- grad_b_down: float32 [768], P('dp')
Inputs may be any that keep to these rules, and one draw needn't show every extreme that they name: `span_starts`: each span starts in the first half of its sequence, before position 512. `span_lengths`: each span covers positions 511 and 512 and ends within its sequence.
All inputs are finite; a program needn't handle non-finite values.
Results may differ from a plain program's by a relative error of at most 0.015.
Values may be sent and summed in bfloat16 or wider, within the bound.
A program may use at most 256 MiB of HBM per device.

v0:
```python
import math

import jax
import jax.numpy as jnp
from jax import lax
from jax.sharding import PartitionSpec as P

HEADS = 12
HD = 64


PRECISE = lax.Precision.HIGHEST
NORM_EPS = 1e-05


def layer_norm(values):
    centre = values - jnp.mean(values, axis=-1, keepdims=True)
    spread = jnp.mean(centre * centre, axis=-1, keepdims=True)
    return centre * lax.rsqrt(spread + NORM_EPS)


def pre_norm(values, gain, shift, scale):
    return layer_norm(values) * gain * (1.0 + scale) + shift


def gelu_tanh(pre_act):
    return jax.nn.gelu(pre_act, approximate=True)


def time_features(time_steps, pair_count):
    frequency = jnp.exp(-math.log(10000.0) * jnp.arange(pair_count, dtype=jnp.float32) / pair_count)
    angles = time_steps.astype(jnp.float32)[:, None] * frequency[None, :]
    return jnp.concatenate([jnp.cos(angles), jnp.sin(angles)], axis=-1)


def rotary_tables(positions):
    half_dim = HD // 2
    frequency = jnp.exp(-math.log(10000.0) * jnp.arange(half_dim, dtype=jnp.float32) / half_dim)
    angles = positions[:, None] * frequency[None, :]
    return (jnp.cos(angles), jnp.sin(angles))


def rotate(vectors, cos_table, sin_table):
    half_dim = vectors.shape[-1] // 2
    leading = vectors[..., :half_dim]
    trailing = vectors[..., half_dim:]
    cosine = cos_table[:, None, :]
    sine_part = sin_table[:, None, :]
    return jnp.concatenate(
        [leading * cosine - trailing * sine_part, trailing * cosine + leading * sine_part], axis=-1
    )


def unrotate(vectors, cos_table, sin_table):
    half_dim = vectors.shape[-1] // 2
    leading = vectors[..., :half_dim]
    trailing = vectors[..., half_dim:]
    cosine = cos_table[:, None, :]
    sine_part = sin_table[:, None, :]
    return jnp.concatenate(
        [leading * cosine + trailing * sine_part, trailing * cosine - leading * sine_part], axis=-1
    )


def attend(entries):
    queries, keys_all, values_all = entries
    scores = jnp.einsum(
        "qhd,khd->hqk", queries, keys_all, preferred_element_type=jnp.float32
    ) * HD ** (-0.5)
    row_top = jnp.max(scores, axis=-1, keepdims=True)
    exponent = jnp.exp(scores - row_top)
    row_total = jnp.sum(exponent, axis=-1, keepdims=True)
    soft_out = (exponent / row_total).astype(jnp.bfloat16)
    mixture = jnp.einsum("hqk,khd->qhd", soft_out, values_all, preferred_element_type=jnp.float32)
    return (mixture.astype(jnp.bfloat16), row_top + jnp.log(row_total))


def attend_back(entries):
    queries, keys_all, values_all, log_total, d_attended = entries
    scores = jnp.einsum(
        "qhd,khd->hqk", queries, keys_all, preferred_element_type=jnp.float32
    ) * HD ** (-0.5)
    soft_full = jnp.exp(scores - log_total)
    d_probs = jnp.einsum("qhd,khd->hqk", d_attended, values_all, preferred_element_type=jnp.float32)
    d_scores = (
        soft_full * (d_probs - jnp.sum(soft_full * d_probs, axis=-1, keepdims=True))
    ).astype(jnp.bfloat16)
    d_queries = jnp.einsum(
        "hqk,khd->qhd", d_scores, keys_all, preferred_element_type=jnp.float32
    ) * HD ** (-0.5)
    d_keys = jnp.einsum(
        "hqk,qhd->khd", d_scores, queries, preferred_element_type=jnp.float32
    ) * HD ** (-0.5)
    d_values = jnp.einsum(
        "hqk,qhd->khd",
        soft_full.astype(jnp.bfloat16),
        d_attended,
        preferred_element_type=jnp.float32,
    )
    return (d_queries, d_keys, d_values)


def per_device(
    tokens,
    cotangent,
    time_index,
    span_starts,
    span_lengths,
    w_ada,
    b_ada,
    gain_one,
    w_qkv,
    w_out,
    gain_two,
    w_up,
    b_up,
    w_down,
    b_down,
):
    seqs_dev, half_len, model_width = tokens.shape
    head_shape = (seqs_dev, half_len, HEADS, HD)
    rank = lax.axis_index("seq")
    place_int = rank * half_len + jnp.arange(half_len, dtype=jnp.int32)
    cos_table, sin_table = rotary_tables(place_int.astype(jnp.float32))
    cond_act = jax.nn.silu(time_features(time_index, w_ada.shape[0] // 2))
    modulation = jnp.dot(cond_act, w_ada.astype(jnp.float32), precision=PRECISE) + b_ada
    pieces = [piece[:, None, :] for piece in jnp.split(modulation, 6, axis=-1)]
    shift_one, scale_one, gate_one, shift_two, scale_two, gate_two = pieces
    resid_in = tokens.astype(jnp.float32)
    mixed_one, norm_pull_one = jax.vjp(pre_norm, resid_in, gain_one, shift_one, scale_one)
    act_one = mixed_one.astype(jnp.bfloat16)
    projected = jnp.einsum("std,de->ste", act_one, w_qkv, preferred_element_type=jnp.float32)
    q_part, k_part, v_part = jnp.split(projected, 3, axis=-1)
    queries = rotate(q_part.reshape(head_shape), cos_table, sin_table).astype(jnp.bfloat16)
    keys_rot = rotate(k_part.reshape(head_shape), cos_table, sin_table).astype(jnp.bfloat16)
    values_rot = v_part.reshape(head_shape).astype(jnp.bfloat16)
    keys_all, values_all = (
        lax.all_gather(keys_rot, "seq", axis=1, tiled=True),
        lax.all_gather(values_rot, "seq", axis=1, tiled=True),
    )
    mixture, log_total = lax.map(attend, (queries, keys_all, values_all))
    attended = mixture.reshape(seqs_dev, half_len, model_width)
    branch = jnp.einsum("std,de->ste", attended, w_out, preferred_element_type=jnp.float32)
    x_one = resid_in + gate_one * branch
    mixed_two, norm_pull_two = jax.vjp(pre_norm, x_one, gain_two, shift_two, scale_two)
    act_two = mixed_two.astype(jnp.bfloat16)
    up_proj = jnp.einsum("std,df->stf", act_two, w_up, preferred_element_type=jnp.float32) + b_up
    hidden_full, gelu_pull = jax.vjp(gelu_tanh, up_proj)
    hidden = hidden_full.astype(jnp.bfloat16)
    down_proj = (
        jnp.einsum("stf,fd->std", hidden, w_down, preferred_element_type=jnp.float32) + b_down
    )
    result = x_one + gate_two * down_proj
    output = result.astype(jnp.bfloat16)
    inside = (place_int[None, :] >= span_starts[:, None]) & (
        place_int[None, :] < (span_starts + span_lengths)[:, None]
    )
    span_weight = jnp.where(inside, 2.0, 0.5).astype(jnp.float32)
    grad_out = cotangent.astype(jnp.float32) * span_weight[:, :, None]
    d_gate_two = jnp.sum(grad_out * down_proj, axis=1)
    d_down = (gate_two * grad_out).astype(jnp.bfloat16)
    g_w_down = jnp.einsum("stf,std->fd", hidden, d_down, preferred_element_type=jnp.float32)
    g_b_down = jnp.sum(d_down.astype(jnp.float32), axis=(0, 1))
    d_hidden = jnp.einsum("std,fd->stf", d_down, w_down, preferred_element_type=jnp.float32)
    d_up = gelu_pull(d_hidden)[0].astype(jnp.bfloat16)
    g_w_up = jnp.einsum("std,stf->df", act_two, d_up, preferred_element_type=jnp.float32)
    g_b_up = jnp.sum(d_up.astype(jnp.float32), axis=(0, 1))
    d_act_two = jnp.einsum("stf,df->std", d_up, w_up, preferred_element_type=jnp.float32)
    d_x_part, g_gain_two, d_shift_two, d_scale_two = norm_pull_two(d_act_two)
    d_x_one = grad_out + d_x_part
    d_gate_one = jnp.sum(d_x_one * branch, axis=1)
    d_branch = (gate_one * d_x_one).astype(jnp.bfloat16)
    g_w_out = jnp.einsum("std,ste->de", attended, d_branch, preferred_element_type=jnp.float32)
    d_attended = jnp.einsum(
        "ste,de->std", d_branch, w_out, preferred_element_type=jnp.float32
    ).astype(jnp.bfloat16)
    keys_back, values_back = (
        lax.all_gather(keys_rot, "seq", axis=1, tiled=True),
        lax.all_gather(values_rot, "seq", axis=1, tiled=True),
    )
    d_queries, d_keys_part, d_values_part = lax.map(
        attend_back, (queries, keys_back, values_back, log_total, d_attended.reshape(head_shape))
    )
    d_keys_sum, d_values_sum = (
        lax.psum_scatter(
            d_keys_part.astype(jnp.bfloat16), "seq", scatter_dimension=1, tiled=True
        ).astype(jnp.float32),
        lax.psum_scatter(
            d_values_part.astype(jnp.bfloat16), "seq", scatter_dimension=1, tiled=True
        ).astype(jnp.float32),
    )
    d_queries_low = d_queries.astype(jnp.bfloat16).astype(jnp.float32)
    d_keys_low = d_keys_sum.astype(jnp.bfloat16).astype(jnp.float32)
    d_values_low = d_values_sum.astype(jnp.bfloat16)
    d_projected = jnp.concatenate(
        [
            unrotate(d_queries_low, cos_table, sin_table)
            .astype(jnp.bfloat16)
            .reshape(seqs_dev, half_len, model_width),
            unrotate(d_keys_low, cos_table, sin_table)
            .astype(jnp.bfloat16)
            .reshape(seqs_dev, half_len, model_width),
            d_values_low.reshape(seqs_dev, half_len, model_width),
        ],
        axis=-1,
    )
    g_w_qkv = jnp.einsum("std,ste->de", act_one, d_projected, preferred_element_type=jnp.float32)
    d_act_one = jnp.einsum("ste,de->std", d_projected, w_qkv, preferred_element_type=jnp.float32)
    d_in_part, g_gain_one, d_shift_one, d_scale_one = norm_pull_one(d_act_one)
    grad_tokens = d_x_one + d_in_part
    d_modulation = jnp.concatenate(
        [
            d_shift_one[:, 0, :],
            d_scale_one[:, 0, :],
            d_gate_one,
            d_shift_two[:, 0, :],
            d_scale_two[:, 0, :],
            d_gate_two,
        ],
        axis=-1,
    )
    g_w_ada = jnp.dot(cond_act.T, d_modulation, precision=PRECISE)
    g_b_ada = jnp.sum(d_modulation, axis=0)
    shard_list = tuple(
        (
            lax.psum_scatter(g_w_ada, "dp", scatter_dimension=0, tiled=True),
            lax.psum_scatter(g_b_ada, "dp", scatter_dimension=0, tiled=True),
            lax.psum_scatter(g_gain_one, "dp", scatter_dimension=0, tiled=True),
            lax.psum_scatter(g_w_qkv, "dp", scatter_dimension=0, tiled=True),
            lax.psum_scatter(g_w_out, "dp", scatter_dimension=0, tiled=True),
            lax.psum_scatter(g_gain_two, "dp", scatter_dimension=0, tiled=True),
            lax.psum_scatter(g_w_up, "dp", scatter_dimension=0, tiled=True),
            lax.psum_scatter(g_b_up, "dp", scatter_dimension=0, tiled=True),
            lax.psum_scatter(g_w_down, "dp", scatter_dimension=0, tiled=True),
            lax.psum_scatter(g_b_down, "dp", scatter_dimension=0, tiled=True),
        )
    )
    (
        s_w_ada,
        s_b_ada,
        s_gain_one,
        s_w_qkv,
        s_w_out,
        s_gain_two,
        s_w_up,
        s_b_up,
        s_w_down,
        s_b_down,
    ) = shard_list
    summed = (
        lax.psum(s_w_ada.astype(jnp.bfloat16), "seq").astype(jnp.float32),
        lax.psum(s_b_ada.astype(jnp.bfloat16), "seq").astype(jnp.float32),
        lax.psum(s_gain_one.astype(jnp.bfloat16), "seq").astype(jnp.float32),
        lax.psum(s_w_qkv.astype(jnp.bfloat16), "seq").astype(jnp.float32),
        lax.psum(s_w_out.astype(jnp.bfloat16), "seq").astype(jnp.float32),
        lax.psum(s_gain_two.astype(jnp.bfloat16), "seq").astype(jnp.float32),
        lax.psum(s_w_up.astype(jnp.bfloat16), "seq").astype(jnp.float32),
        lax.psum(s_b_up.astype(jnp.bfloat16), "seq").astype(jnp.float32),
        lax.psum(s_w_down.astype(jnp.bfloat16), "seq").astype(jnp.float32),
        lax.psum(s_b_down.astype(jnp.bfloat16), "seq").astype(jnp.float32),
    )
    return (
        output,
        grad_tokens,
        summed[0],
        summed[1],
        summed[2],
        summed[3],
        summed[4],
        summed[5],
        summed[6],
        summed[7],
        summed[8],
        summed[9],
    )


def solution(mesh):
    return jax.shard_map(
        per_device,
        mesh=mesh,
        in_specs=(
            P("dp", "seq", None),
            P("dp", "seq", None),
            P("dp"),
            P("dp"),
            P("dp"),
            P(),
            P(),
            P(),
            P(),
            P(),
            P(),
            P(),
            P(),
            P(),
            P(),
        ),
        out_specs=(
            P("dp", "seq", None),
            P("dp", "seq", None),
            P("dp", None),
            P("dp"),
            P("dp"),
            P("dp", None),
            P("dp", None),
            P("dp"),
            P("dp", None),
            P("dp"),
            P("dp", None),
            P("dp"),
        ),
        check_vma=False,
    )
```

profile of v0, /device:TPU:10, one launch (start us, length us, event | category | flops | bytes accessed | tf_op | source)
XLA Modules:
  0.0 1073.0 jit_solution(7558055883864653454)
XLA Ops:
  8.1 2.2 convert_reduce_fusion.1
  10.3 2.0 fusion.86
  14.3 4.2 fusion.78
  18.6 3.6 copy-done.11
  23.5 2.6 copy.62
  26.2 6.2 fusion.102
  32.4 3.7 copy.64
  36.1 3.7 copy.63
  40.2 5.1 subtract_convert_fusion.2
  46.8 2.7 pad_maximum_fusion.3
  50.2 21.3 %all-gather.3.cloned.1.call-done = bf16[2,1024,12,64]{1,3,2,0:T(8,128)(2,1)} async-done(((bf16[2,512,12,64]{1,3,2,0:T(8,128)(2,1)}), bf16[2,1024,12,64]{1,3,2,0:T(8,128)(2,1)}) %all-gather.3.cloned.1.call-update) | async-done | bytes 3145744 | tf_op jit(solution)/shard_map/all_gather | solution.py:139
  71.4 47.1 %all-gather.5.cloned.1.call-done = bf16[2,1024,12,64]{1,3,2,0:T(8,128)(2,1)} async-done(((bf16[2,512,12,64]{1,3,2,0:T(8,128)(2,1)}), bf16[2,1024,12,64]{1,3,2,0:T(8,128)(2,1)}) %all-gather.5.cloned.1.call-update) | async-done | bytes 3145744 | tf_op jit(solution)/shard_map/all_gather | solution.py:138
  118.5 75.3 %while.26 = (s32[]{:T(128)}, bf16[2,512,12,64]{1,3,2,0:T(8,128)(2,1)}, f32[2,12,512,1]{2,1,3,0:T(8,128)}, bf16[2,1024,12,64]{1,3,2,0:T(8,128)(2,1)}, bf16[2,512,...) while((s32[]{:T(128)}, bf16[2,512,12,64]{1,3,2,0:T(8,128)(2,1)}, ...), condition=%wide.region_5.6_spmd, body=%wide.region_2.5_spmd.sunk | while | flops 1667622912 | bytes 106014952 | solution.py:141
  118.5 13.4 %multiply_reduce_fusion.10 = (f32[12,512]{1,0:T(8,128)S(1)}, f32[12,512,1024]{2,1,0:T(8,128)}) fusion(bf16[2,1024,12,64]{1,3,2,0:T(8,128)(2,1)} %get-tuple-element.326, s32[]{:T(128)S(6)} %copy.85, bf16[2,512,12,64]{1,3,2,0:T(8,128)(2,1)} %get-tuple-element.325), kind=kOutput, calls=%fused_computation.2.clone.1 | convolution fusion | flops 817883136 | bytes 27550720 | tf_op jit(solution)/shard_map/while/body/eval_jaxpr/qhd,khd->hqk/dot_general | solution.py:67
  132.0 11.6 %fusion.125 = f32[12,512]{1,0:T(8,128)S(1)} fusion(f32[12,512,1024]{2,1,0:T(8,128)} %get-tuple-element.294, f32[12,512]{1,0:T(8,128)S(1)} %get-tuple-element.295), kind=kLoop, calls=%fused_computation.3.clone.1 | loop fusion | flops 18868224 | bytes 25214976 | tf_op jit(solution)/shard_map/while/body/eval_jaxpr/reduce_sum | solution.py:72
  143.6 10.8 %fusion.126 = bf16[2,512,12,64]{1,3,2,0:T(8,128)(2,1)S(1)} fusion(bf16[2,512,12,64]{1,3,2,0:T(8,128)(2,1)S(1)} %copy-done.17, s32[]{:T(128)S(6)} %copy.85, f32[12,512,1024]{2,1,0:T(8,128)} %get-tuple-element.294, f32[12,512]{1,0:T(8,128)S(1)} %fusion.125, f32[12,512]{1,0:T(8,128)S(1)} %get-tuple-element.295, bf16[2,1024,12,64]{1,3,2,0:T(8,128)(2,1)S(1)} %copy-done.7), kind=kOutput, calls=%fused_computation.12.clone.1 | convolution fusion | flops 830865408 | bytes 27591680 | tf_op jit(solution)/shard_map/while/body/eval_jaxpr/hqk,khd->qhd/dot_general | solution.py:74
  156.2 13.4 %multiply_reduce_fusion.10 = (f32[12,512]{1,0:T(8,128)S(1)}, f32[12,512,1024]{2,1,0:T(8,128)}) fusion(bf16[2,1024,12,64]{1,3,2,0:T(8,128)(2,1)} %get-tuple-element.326, s32[]{:T(128)S(6)} %copy.85, bf16[2,512,12,64]{1,3,2,0:T(8,128)(2,1)} %get-tuple-element.325), kind=kOutput, calls=%fused_computation.2.clone.1 | convolution fusion | flops 817883136 | bytes 27550720 | tf_op jit(solution)/shard_map/while/body/eval_jaxpr/qhd,khd->hqk/dot_general | solution.py:67
  169.6 11.6 %fusion.125 = f32[12,512]{1,0:T(8,128)S(1)} fusion(f32[12,512,1024]{2,1,0:T(8,128)} %get-tuple-element.294, f32[12,512]{1,0:T(8,128)S(1)} %get-tuple-element.295), kind=kLoop, calls=%fused_computation.3.clone.1 | loop fusion | flops 18868224 | bytes 25214976 | tf_op jit(solution)/shard_map/while/body/eval_jaxpr/reduce_sum | solution.py:72
  181.3 10.8 %fusion.126 = bf16[2,512,12,64]{1,3,2,0:T(8,128)(2,1)S(1)} fusion(bf16[2,512,12,64]{1,3,2,0:T(8,128)(2,1)S(1)} %copy-done.17, s32[]{:T(128)S(6)} %copy.85, f32[12,512,1024]{2,1,0:T(8,128)} %get-tuple-element.294, f32[12,512]{1,0:T(8,128)S(1)} %fusion.125, f32[12,512]{1,0:T(8,128)S(1)} %get-tuple-element.295, bf16[2,1024,12,64]{1,3,2,0:T(8,128)(2,1)S(1)} %copy-done.7), kind=kOutput, calls=%fused_computation.12.clone.1 | convolution fusion | flops 830865408 | bytes 27591680 | tf_op jit(solution)/shard_map/while/body/eval_jaxpr/hqk,khd->qhd/dot_general | solution.py:74
  193.9 5.6 fusion.101
  200.3 8.2 fusion.70
  208.4 17.3 %convert_reduce_fusion = (f32[3072]{0:T(1024)}, bf16[2,512,3072]{2,1,0:T(8,128)(2,1)S(1)}) fusion(f32[2,512,3072]{2,1,0:T(8,128)} %fusion.70, f32[3072]{0:T(1024)S(1)} %copy-done.67, bf16[3072,768]{1,0:T(8,128)(2,1)} %param.32, bf16[2,512,768]{2,1,0:T(8,128)(2,1)} %param.20, f32[2,512]{1,0:T(2,128)S(1)} %copy-done.64, f32[2,768]{1,0:T(2,128)S(1)} %copy-done.60), kind=kOutput, calls=%fused_computation.62 | convolution fusion | flops 4907332608 | bytes 25200640 | tf_op jit(solution)/shard_map/std,fd->stf/dot_general | solution.py:164
  225.7 10.0 multiply_reduce_fusion.6
  235.7 2.7 multiply_reduce_fusion.2
  238.5 15.1 %convert_reduce_fusion.2 = (f32[768]{0:T(1024)}, f32[2,768]{1,0:T(2,128)}, bf16[2,512,768]{2,1,0:T(8,128)(2,1)}, f32[2,768]{1,0:T(2,128)}, f32[2,512,768]{2,1,0:T(8,128)S(1)}) fusion(f32[2,512]{1,0:T(2,128)S(1)} %copy-done.64, bf16[2,512,768]{2,1,0:T(8,128)(2,1)} %param.20, f32[2,768]{1,0:T(2,128)S(1)} %copy-done.60, f32[768]{0:T(1024)S(1)} %copy-done.68, ...), kind=kOutput, calls=%fused_computation.101 | convolution fusion | flops 4881379328 | bytes 33096704 | tf_op jit(solution)/shard_map/stf,fd->std/dot_general | solution.py:151
  255.3 2.6 convolution_convert_fusion
  257.9 2.6 copy.66
  260.5 168.1 %while.27 = (s32[]{:T(128)}, bf16[2,512,12,64]{1,3,2,0:T(8,128)(2,1)}, bf16[2,1024,12,64]{1,3,2,0:T(8,128)(2,1)}, bf16[2,1024,12,64]{1,3,2,0:T(8,128)(2,1)}, bf1...) while((s32[]{:T(128)}, ...), condition=%wide.region_12.13_spmd, body=%wide.region_10.12_spmd.sunk | while | flops 4103202816 | bytes 255096096 | solution.py:181
  261.4 13.5 %fusion.135 = f32[12,512,1024]{2,1,0:T(8,128)} fusion(bf16[2,1024,12,64]{1,3,2,0:T(8,128)(2,1)} %get-tuple-element.352, s32[]{:T(128)S(6)} %copy.95, bf16[2,512,12,64]{1,3,2,0:T(8,128)(2,1)} %get-tuple-element.353), kind=kOutput, calls=%fused_computation.33.clone.1 | convolution fusion | flops 805306368 | bytes 27526144 | tf_op jit(solution)/shard_map/while/body/eval_jaxpr/qhd,khd->hqk/dot_general | solution.py:80
  275.0 11.9 %bitcast_dynamic-update-slice_fusion.11 = bf16[2,1024,12,64]{1,3,2,0:T(8,128)(2,1)} fusion(bf16[2,1024,12,64]{1,3,2,0:T(8,128)(2,1)} %get-tuple-element.341, s32[]{:T(128)S(6)} %copy.95, f32[12,512,1024]{2,1,0:T(8,128)} %fusion.135, f32[12,512]{1,0:T(8,128)S(1)} %dynamic-slice_bitcast_fusion.2, bf16[2,512,12,64]{1,3,2,0:T(8,128)(2,1)S(1)} %copy-done.3), kind=kOutput, calls=%fused_computation.26.clone.1 | convolution fusion | flops 824180736 | bytes 29131776 | tf_op jit(solution)/shard_map/while/body/eval_jaxpr/hqk,qhd->khd/dot_general | solution.py:94
  286.9 17.5 %multiply_reduce_fusion.11 = (f32[12,512]{1,0:T(8,128)}, f32[12,512,1024]{2,1,0:T(8,128)}) fusion(f32[12,512,1024]{2,1,0:T(8,128)} %fusion.135, f32[12,512]{1,0:T(8,128)} %copy-done.8, bf16[2,1024,12,64]{1,3,2,0:T(8,128)(2,1)} %get-tuple-element.356, s32[]{:T(128)S(6)} %copy.95, bf16[2,512,12,64]{1,3,2,0:T(8,128)(2,1)} %get-tuple-element.355), kind=kOutput, calls=%fused_computation.20.clone.1 | convolution fusion | flops 830466048 | bytes 52749312 | tf_op jit(solution)/shard_map/while/body/eval_jaxpr/qhd,khd->hqk/dot_general | solution.py:84
  304.4 21.8 %multiply_convert_fusion.11 = bf16[12,512,1024]{2,1,0:T(8,128)(2,1)} fusion(f32[12,512,1024]{2,1,0:T(8,128)} %get-tuple-element.305, f32[12,512,1024]{2,1,0:T(8,128)} %fusion.135, f32[12,512]{1,0:T(8,128)} %get-tuple-element.306, f32[12,512]{1,0:T(8,128)} %copy-done.8), kind=kLoop, calls=%fused_computation.19.clone.1 | loop fusion | flops 31457280 | bytes 62963712 | tf_op jit(solution)/shard_map/while/body/eval_jaxpr/convert_element_type | solution.py:87
  326.2 9.5 bitcast_dynamic-update-slice_fusion.9
  335.8 6.9 bitcast_dynamic-update-slice_fusion.10
  345.2 13.5 %fusion.135 = f32[12,512,1024]{2,1,0:T(8,128)} fusion(bf16[2,1024,12,64]{1,3,2,0:T(8,128)(2,1)} %get-tuple-element.352, s32[]{:T(128)S(6)} %copy.95, bf16[2,512,12,64]{1,3,2,0:T(8,128)(2,1)} %get-tuple-element.353), kind=kOutput, calls=%fused_computation.33.clone.1 | convolution fusion | flops 805306368 | bytes 27526144 | tf_op jit(solution)/shard_map/while/body/eval_jaxpr/qhd,khd->hqk/dot_general | solution.py:80
  358.7 12.0 %bitcast_dynamic-update-slice_fusion.11 = bf16[2,1024,12,64]{1,3,2,0:T(8,128)(2,1)} fusion(bf16[2,1024,12,64]{1,3,2,0:T(8,128)(2,1)} %get-tuple-element.341, s32[]{:T(128)S(6)} %copy.95, f32[12,512,1024]{2,1,0:T(8,128)} %fusion.135, f32[12,512]{1,0:T(8,128)S(1)} %dynamic-slice_bitcast_fusion.2, bf16[2,512,12,64]{1,3,2,0:T(8,128)(2,1)S(1)} %copy-done.3), kind=kOutput, calls=%fused_computation.26.clone.1 | convolution fusion | flops 824180736 | bytes 29131776 | tf_op jit(solution)/shard_map/while/body/eval_jaxpr/hqk,qhd->khd/dot_general | solution.py:94
  370.6 17.5 %multiply_reduce_fusion.11 = (f32[12,512]{1,0:T(8,128)}, f32[12,512,1024]{2,1,0:T(8,128)}) fusion(f32[12,512,1024]{2,1,0:T(8,128)} %fusion.135, f32[12,512]{1,0:T(8,128)} %copy-done.8, bf16[2,1024,12,64]{1,3,2,0:T(8,128)(2,1)} %get-tuple-element.356, s32[]{:T(128)S(6)} %copy.95, bf16[2,512,12,64]{1,3,2,0:T(8,128)(2,1)} %get-tuple-element.355), kind=kOutput, calls=%fused_computation.20.clone.1 | convolution fusion | flops 830466048 | bytes 52749312 | tf_op jit(solution)/shard_map/while/body/eval_jaxpr/qhd,khd->hqk/dot_general | solution.py:84
  388.1 21.8 %multiply_convert_fusion.11 = bf16[12,512,1024]{2,1,0:T(8,128)(2,1)} fusion(f32[12,512,1024]{2,1,0:T(8,128)} %get-tuple-element.305, f32[12,512,1024]{2,1,0:T(8,128)} %fusion.135, f32[12,512]{1,0:T(8,128)} %get-tuple-element.306, f32[12,512]{1,0:T(8,128)} %copy-done.8), kind=kLoop, calls=%fused_computation.19.clone.1 | loop fusion | flops 31457280 | bytes 62963712 | tf_op jit(solution)/shard_map/while/body/eval_jaxpr/convert_element_type | solution.py:87
  410.0 9.6 bitcast_dynamic-update-slice_fusion.9
  419.6 6.9 bitcast_dynamic-update-slice_fusion.10
  429.3 5.2 convolution_bitcast_fusion.3
  434.6 3.6 convert_element_type.297
  438.1 34.0 %reduce-scatter.10.cloned.1.call-done = bf16[2,512,12,64]{1,3,2,0:T(8,128)(2,1)} async-done(((bf16[2,1024,12,64]{1,3,2,0:T(8,128)(2,1)}), bf16[2,512,12,64]{1,3,2,0:T(8,128)(2,1)}) %reduce-scatter.10.cloned.1.call-update) | async-done | bytes 1572880 | tf_op jit(solution)/shard_map/reduce_scatter | solution.py:188
  472.1 2.6 copy.69
  474.7 43.0 %reduce-scatter.8.cloned.1.call-done = bf16[2,512,12,64]{1,3,2,0:T(8,128)(2,1)} async-done(((bf16[2,1024,12,64]{1,3,2,0:T(8,128)(2,1)}), bf16[2,512,12,64]{1,3,2,0:T(8,128)(2,1)}) %reduce-scatter.8.cloned.1.call-update) | async-done | bytes 1572880 | tf_op jit(solution)/shard_map/reduce_scatter | solution.py:185
  517.7 2.0 convert_element_type.174
  520.1 2.3 add_convert_fusion.3
  523.6 2.6 copy.67
  526.3 2.7 pad_maximum_fusion.6
  529.0 2.6 copy.68
  531.7 7.2 fusion.87
  539.0 2.7 fusion.85
  542.5 3.5 fusion.100
  546.1 11.0 %convolution_bitcast_fusion.1 = f32[768,3072]{1,0:T(8,128)} fusion(bf16[2,512,3072]{2,1,0:T(8,128)(2,1)} %copy-done.12, f32[2,512,768]{2,1,0:T(8,128)} %copy-done.4, f32[2,768]{1,0:T(2,128)S(1)} %copy-done.28, f32[2,768]{1,0:T(2,128)S(1)} %copy-done.22, f32[768]{0:T(1024)} %param.29, f32[2,512]{1,0:T(2,128)} %copy-done.37, f32[2,512]{1,0:T(2,128)} %copy-done.33), kind=kOutput, calls=%fused_computation.65 | convolution fusion | flops 4836556800 | bytes 18897920 | tf_op jit(solution)/shard_map/std,stf->df/dot_general | solution.py:166
  557.8 13.8 %convolution_bitcast_fusion = f32[3072,768]{1,0:T(8,128)} fusion(bf16[2,512,768]{2,1,0:T(8,128)(2,1)} %param.20, f32[2,512]{1,0:T(2,128)S(1)} %copy-done.65, f32[2,768]{1,0:T(2,128)S(1)} %copy-done.61, f32[2,512,3072]{2,1,0:T(8,128)} %fusion.70, f32[3072]{0:T(1024)} %param.31), kind=kOutput, calls=%fused_computation.64 | convolution fusion | flops 4866441216 | bytes 23615488 | tf_op jit(solution)/shard_map/stf,std->fd/dot_general | solution.py:162
  572.3 10.0 convolution_bitcast_fusion.2
  582.4 2.7 reduce-scatter.16.cloned.1.call-done
  586.6 64.6 %reduce-scatter.12.cloned.1.call-done = f32[8,4608]{1,0:T(8,128)} async-done(((f32[128,4608]{1,0:T(8,128)}), f32[8,4608]{1,0:T(8,128)}) %reduce-scatter.12.cloned.1.call-update) | async-done | bytes 147472 | tf_op jit(solution)/shard_map/reduce_scatter | solution.py:226
  652.8 113.2 %reduce-scatter.18.cloned.1.call-done = f32[48,3072]{1,0:T(8,128)} async-done(((f32[768,3072]{1,0:T(8,128)}), f32[48,3072]{1,0:T(8,128)}) %reduce-scatter.18.cloned.1.call-update) | async-done | bytes 589840 | tf_op jit(solution)/shard_map/reduce_scatter | solution.py:232
  767.8 114.0 %reduce-scatter.20.cloned.1.call-done = f32[192,768]{1,0:T(8,128)} async-done(((f32[3072,768]{1,0:T(8,128)}), f32[192,768]{1,0:T(8,128)}) %reduce-scatter.20.cloned.1.call-update) | async-done | bytes 589840 | tf_op jit(solution)/shard_map/reduce_scatter | solution.py:234
  883.5 91.9 %reduce-scatter.14.cloned.1.call-done = f32[48,2304]{1,0:T(8,128)} async-done(((f32[768,2304]{1,0:T(8,128)}), f32[48,2304]{1,0:T(8,128)}) %reduce-scatter.14.cloned.1.call-update) | async-done | bytes 442384 | tf_op jit(solution)/shard_map/reduce_scatter | solution.py:229
  981.8 52.1 %all-reduce.5 = (bf16[4608]{0:T(1024)(128)(2,1)}, bf16[768]{0:T(1024)(128)(2,1)}, bf16[768]{0:T(1024)(128)(2,1)}, bf16[3072]{0:T(1024)(128)(2,1)}, bf16[768]{0:T(1024)(128)(2,1)}) all-reduce(f32[4608]{0:T(1024)} %reduce_sum.227, f32[768]{0:T(1024)} %get-tuple-element.111, ...), channel_id=5, replica_groups=mesh['dp'=16,'seq'=2] {'dp'}, use_global_device_ids=true, to_apply=%region_26.27.clone | all-reduce | flops 9984 | bytes 59904
  1040.2 5.6 all-reduce.6
  1052.5 5.0 add_add_fusion.2
  (246 shorter events, 54.7 us)
Async XLA Ops:
  7.2 7.1 copy-start
  7.2 7.1 copy-start.53
  7.2 64.2 %all-gather.3.cloned.1.call-start = ((), (), s32[]{:S(2)}) async-start(), calls=%async_computation.7 | async-start | bytes 4718592 | tf_op jit(solution)/shard_map/all_gather | solution.py:139
  7.3 5.8 copy-start.19
  7.3 5.8 copy-start.52
  7.3 7.0 copy-start.5
  10.3 8.3 copy-start.34
  12.3 6.2 copy-start.47
  14.3 4.3 copy-start.38
  14.3 4.3 copy-start.59
  18.6 3.7 copy-start.11
  26.1 92.4 %all-gather.5.cloned.1.call-start = ((), (), s32[]{:S(2)}) async-start(), calls=%async_computation.8 | async-start | bytes 4718592 | tf_op jit(solution)/shard_map/all_gather | solution.py:138
  40.1 5.1 copy-start.23
  40.1 5.1 copy-start.25
  46.5 425.6 %reduce-scatter.10.cloned.1.call-start = ((), (), s32[]{:S(2)}) async-start(), calls=%async_computation.10 | async-start | bytes 4718592 | tf_op jit(solution)/shard_map/reduce_scatter | solution.py:188
  118.5 75.3 %copy-start.41 = (f32[2,768]{1,0:T(2,128)S(1)}, f32[2,768]{1,0:T(2,128)}, u32[]{:S(2)}) copy-start(f32[2,768]{1,0:T(2,128)} %get-tuple-element.193) | copy-start | bytes 18436
  132.0 11.6 %copy-start.7 = (bf16[2,1024,12,64]{1,3,2,0:T(8,128)(2,1)S(1)}, bf16[2,1024,12,64]{1,3,2,0:T(8,128)(2,1)}, u32[]{:S(2)}) copy-start(bf16[2,1024,12,64]{1,3,2,0:T(8,128)(2,1)} %get-tuple-element.324) | copy-start | bytes 9437188 | tf_op jit(solution)/shard_map/while
  132.0 11.6 %copy-start.17 = (bf16[2,512,12,64]{1,3,2,0:T(8,128)(2,1)S(1)}, bf16[2,512,12,64]{1,3,2,0:T(8,128)(2,1)}, u32[]{:S(2)}) copy-start(bf16[2,512,12,64]{1,3,2,0:T(8,128)(2,1)} %get-tuple-element.315) | copy-start | bytes 4718596 | tf_op jit(solution)/shard_map/while
  143.6 10.9 %copy-start.29 = (f32[2,12,512,1]{2,1,3,0:T(8,128)S(1)}, f32[2,12,512,1]{2,1,3,0:T(8,128)}, u32[]{:S(2)}) copy-start(f32[2,12,512,1]{2,1,3,0:T(8,128)} %get-tuple-element.316) | copy-start | bytes 147460 | tf_op jit(solution)/shard_map/while
  169.6 11.6 %copy-start.7 = (bf16[2,1024,12,64]{1,3,2,0:T(8,128)(2,1)S(1)}, bf16[2,1024,12,64]{1,3,2,0:T(8,128)(2,1)}, u32[]{:S(2)}) copy-start(bf16[2,1024,12,64]{1,3,2,0:T(8,128)(2,1)} %get-tuple-element.324) | copy-start | bytes 9437188 | tf_op jit(solution)/shard_map/while
  169.6 11.6 %copy-start.17 = (bf16[2,512,12,64]{1,3,2,0:T(8,128)(2,1)S(1)}, bf16[2,512,12,64]{1,3,2,0:T(8,128)(2,1)}, u32[]{:S(2)}) copy-start(bf16[2,512,12,64]{1,3,2,0:T(8,128)(2,1)} %get-tuple-element.315) | copy-start | bytes 4718596 | tf_op jit(solution)/shard_map/while
  181.2 10.9 %copy-start.29 = (f32[2,12,512,1]{2,1,3,0:T(8,128)S(1)}, f32[2,12,512,1]{2,1,3,0:T(8,128)}, u32[]{:S(2)}) copy-start(f32[2,12,512,1]{2,1,3,0:T(8,128)} %get-tuple-element.316) | copy-start | bytes 147460 | tf_op jit(solution)/shard_map/while
  193.9 6.1 slice-start
  193.9 6.1 slice-start.1
  199.5 39.0 %copy-start.4 = (f32[2,512,768]{2,1,0:T(8,128)}, f32[2,512,768]{2,1,0:T(8,128)S(1)}, u32[]{:S(2)}) copy-start(f32[2,512,768]{2,1,0:T(8,128)S(1)} %get-tuple-element.166) | copy-start | bytes 9437188
  199.5 39.0 %copy-start.33 = (f32[2,512]{1,0:T(2,128)}, f32[2,512]{1,0:T(2,128)S(1)}, u32[]{:S(2)}) copy-start(f32[2,512]{1,0:T(2,128)S(1)} %broadcast_multiply_fusion) | copy-start | bytes 12292
  200.0 38.5 %copy-start.37 = (f32[2,512]{1,0:T(2,128)}, f32[2,512]{1,0:T(2,128)S(1)}, u32[]{:S(2)}) copy-start(f32[2,512]{1,0:T(2,128)S(1)} %fusion.96) | copy-start | bytes 12292
  200.3 8.2 copy-start.60
  200.3 8.2 copy-start.64
  200.3 8.2 copy-start.67
  225.7 10.0 copy-start.12
  238.5 16.8 %copy-start.20 = (bf16[768,768]{1,0:T(8,128)(2,1)S(1)}, bf16[768,768]{1,0:T(8,128)(2,1)}, u32[]{:S(2)}) copy-start(bf16[768,768]{1,0:T(8,128)(2,1)} %param.28) | copy-start | bytes 3538948
  261.4 13.5 %copy-start.8 = (f32[12,512]{1,0:T(8,128)}, f32[12,512]{1,0:T(8,128)S(1)}, u32[]{:S(2)}) copy-start(f32[12,512]{1,0:T(8,128)S(1)} %dynamic-slice_bitcast_fusion.2) | copy-start | bytes 73732 | tf_op jit(solution)/shard_map/while
  261.4 13.5 %copy-start.3 = (bf16[2,512,12,64]{1,3,2,0:T(8,128)(2,1)S(1)}, bf16[2,512,12,64]{1,3,2,0:T(8,128)(2,1)}, u32[]{:S(2)}) copy-start(bf16[2,512,12,64]{1,3,2,0:T(8,128)(2,1)} %get-tuple-element.355) | copy-start | bytes 4718596 | tf_op jit(solution)/shard_map/while
  304.4 21.8 %copy-start.1 = (bf16[2,1024,12,64]{1,3,2,0:T(8,128)(2,1)S(1)}, bf16[2,1024,12,64]{1,3,2,0:T(8,128)(2,1)}, u32[]{:S(2)}) copy-start(bf16[2,1024,12,64]{1,3,2,0:T(8,128)(2,1)} %get-tuple-element.352) | copy-start | bytes 9437188 | tf_op jit(solution)/shard_map/while
  326.2 9.6 copy-start.2
  326.2 9.6 copy-start.13
  345.2 13.5 %copy-start.8 = (f32[12,512]{1,0:T(8,128)}, f32[12,512]{1,0:T(8,128)S(1)}, u32[]{:S(2)}) copy-start(f32[12,512]{1,0:T(8,128)S(1)} %dynamic-slice_bitcast_fusion.2) | copy-start | bytes 73732 | tf_op jit(solution)/shard_map/while
  345.2 13.5 %copy-start.3 = (bf16[2,512,12,64]{1,3,2,0:T(8,128)(2,1)S(1)}, bf16[2,512,12,64]{1,3,2,0:T(8,128)(2,1)}, u32[]{:S(2)}) copy-start(bf16[2,512,12,64]{1,3,2,0:T(8,128)(2,1)} %get-tuple-element.355) | copy-start | bytes 4718596 | tf_op jit(solution)/shard_map/while
  388.1 21.8 %copy-start.1 = (bf16[2,1024,12,64]{1,3,2,0:T(8,128)(2,1)S(1)}, bf16[2,1024,12,64]{1,3,2,0:T(8,128)(2,1)}, u32[]{:S(2)}) copy-start(bf16[2,1024,12,64]{1,3,2,0:T(8,128)(2,1)} %get-tuple-element.352) | copy-start | bytes 9437188 | tf_op jit(solution)/shard_map/while
  410.0 9.6 copy-start.2
  410.0 9.6 copy-start.13
  428.6 89.1 %reduce-scatter.8.cloned.1.call-start = ((), (), s32[]{:S(2)}) async-start(), calls=%async_computation.9 | async-start | bytes 4718592 | tf_op jit(solution)/shard_map/reduce_scatter | solution.py:185
  429.2 155.9 %reduce-scatter.16.cloned.1.call-start = ((), (), s32[]{:S(2)}) async-start(), calls=%async_computation.13 | async-start | bytes 2506752 | tf_op jit(solution)/shard_map/reduce_scatter | solution.py:230
  434.5 216.7 %reduce-scatter.12.cloned.1.call-start = ((), (), s32[]{:S(2)}) async-start(), calls=%async_computation.11 | async-start | bytes 2506752 | tf_op jit(solution)/shard_map/reduce_scatter | solution.py:226
  526.2 5.4 copy-start.35
  526.3 5.4 copy-start.39
  526.3 5.4 copy-start.54
  531.6 7.3 copy-start.44
  531.6 7.3 copy-start.6
  531.7 7.3 copy-start.48
  538.9 2.9 copy-start.63
  538.9 2.9 copy-start.51
  538.9 2.9 copy-start.50
  538.9 2.9 copy-start.62
  538.9 3.5 copy-start.56
  538.9 3.5 copy-start.58
  541.7 4.3 copy-start.22
  541.7 4.4 copy-start.28
  546.0 219.9 %reduce-scatter.18.cloned.1.call-start = ((), (), s32[]{:S(2)}) async-start(), calls=%async_computation.14 | async-start | bytes 10027008 | tf_op jit(solution)/shard_map/reduce_scatter | solution.py:232
  557.1 324.6 %reduce-scatter.20.cloned.1.call-start = ((), (), s32[]{:S(2)}) async-start(), calls=%async_computation.15 | async-start | bytes 10027008 | tf_op jit(solution)/shard_map/reduce_scatter | solution.py:234
  571.6 403.8 %reduce-scatter.14.cloned.1.call-start = ((), (), s32[]{:S(2)}) async-start(), calls=%async_computation.12 | async-start | bytes 7520256 | tf_op jit(solution)/shard_map/reduce_scatter | solution.py:229
  582.3 470.2 %copy-start.46 = (f32[2,512]{1,0:T(2,128)S(1)}, f32[2,512]{1,0:T(2,128)}, u32[]{:S(2)}) copy-start(f32[2,512]{1,0:T(2,128)} %copy-done.45) | copy-start | bytes 12292
  582.3 475.2 %all-reduce.10.cloned.1.call-start = ((), (), s32[]{:S(2)}) async-start(), calls=%async_computation.16 | async-start | bytes 1916928 | tf_op jit(solution)/shard_map/psum | solution.py:251
  (29 other events, 40.1 us)
Sparse Core Ops, SparseCore 0:
  26.3 45.1 all-gather.2
  73.6 44.9 all-gather.4
  428.8 43.3 reduce-scatter.9
  474.3 43.3 reduce-scatter.7
  521.3 63.7 reduce-scatter.15
  589.2 62.0 reduce-scatter.11
  655.3 110.5 reduce-scatter.17
  770.6 111.0 reduce-scatter.19
  885.7 89.6 reduce-scatter.13
  979.2 37.5 all-reduce.9
where the time goes:
time: 1090 us; the launch traced here: 1070 us
  waiting for transfers between devices  532 us (49%)
  matrix products  282 us (26%)
  other arithmetic  130 us (12%)
  blocking collectives  57.7 us (5%)
  local copies, waits for them, and re-layouts  52.5 us (5%)
  between operations  17 us (2%)
    reduce_scatter x1, waiting for transfers between devices, per_device(): lax.psum_scatter(g_w_down, 'dp', scatter_dimension=0, tiled=True)  114 us
    reduce_scatter x1, waiting for transfers between devices, per_device(): lax.psum_scatter(g_w_up, 'dp', scatter_dimension=0, tiled=True)  113 us
    reduce_scatter x1, waiting for transfers between devices, per_device(): lax.psum_scatter(g_w_qkv, 'dp', scatter_dimension=0, tiled=True)  91.9 us
    reduce_scatter x1, waiting for transfers between devices, per_device(): lax.psum_scatter(g_w_ada, 'dp', scatter_dimension=0, tiled=True)  64.6 us
    unnamed x1, blocking collectives  52.1 us
    all_gather x1, waiting for transfers between devices, per_device(): lax.all_gather(keys_rot, 'seq', axis=1, tiled=True)  47.1 us
    convert_element_type x2, other arithmetic, attend_back(): d_scores = (soft_full * (d_probs - jnp.sum(soft_full * d_probs, axis=-1,...  43.7 us
    reduce_scatter x1, waiting for transfers between devices, per_device(): lax.psum_scatter(d_keys_part.astype(jnp.bfloat16), 'seq', scatter_dimensi...  43 us
  transfers between devices with their start and end apart: 10, of which 9 were waited for; matrix products, arithmetic and copies ran while one was open for 12% of the time, Pallas kernels for 0%

commit v1 on v0

v1 whole, which is shorter than its diff:
```python
import functools
import math

import jax
import jax.numpy as jnp
from jax import lax
from jax.experimental import pallas as pl
from jax.experimental.pallas import tpu as pltpu
from jax.sharding import PartitionSpec as P

HEADS = 12
HD = 64
PAIRS = HEADS // 2
NORM_EPS = 1e-05
LOG2E = math.log2(math.e)
BF = jnp.bfloat16
F32 = jnp.float32
MIB = 1 << 20

NN = (((1,), (0,)), ((), ()))
NT = (((1,), (1,)), ((), ()))
TN = (((0,), (0,)), ((), ()))


def mm(a, b, dims=NN):
    return lax.dot_general(a, b, dims, preferred_element_type=F32)


def norm_parts(x):
    centre = x - jnp.mean(x, axis=-1, keepdims=True)
    rstd = lax.rsqrt(jnp.mean(centre * centre, axis=-1, keepdims=True) + NORM_EPS)
    return centre * rstd, rstd


def norm_pull(n, rstd, dn):
    return rstd * (
        dn - jnp.mean(dn, axis=-1, keepdims=True) - n * jnp.mean(dn * n, axis=-1, keepdims=True)
    )


def col_sum(x):
    return jnp.sum(x, axis=0, keepdims=True)


def rows_of(size, index):
    return pl.ds(pl.multiple_of(index * size, size), size)


def params(mib=56):
    return pltpu.CompilerParams(vmem_limit_bytes=mib * MIB)


def whole(shape):
    zeros = (0,) * len(shape)
    return pl.BlockSpec(shape, lambda *_: zeros)


def project_kernel(own_ref, rem_ref, vec_ref, cos_ref, sin_ref, w_ref, act_ref, out_ref):
    step = pl.program_id(0)
    half, _ = own_ref.shape
    tile = 256

    @pl.when(step == 0)
    def _():
        scale = vec_ref[0:1, :]
        shift = vec_ref[1:2, :]
        for part, ref in enumerate((own_ref, rem_ref)):
            for t in range(half // tile):
                n, _ = norm_parts(ref[t * tile : (t + 1) * tile, :].astype(F32))
                act = (n * scale + shift).astype(BF)
                start = part * half + t * tile
                act_ref[:, start : start + tile] = act.T

    proj = mm(w_ref[...], act_ref[...])
    heads = proj.shape[0] // HD
    tokens = proj.shape[1]

    @pl.when(step < 4)
    def _():
        factor = jnp.where(step < 2, HD**-0.5, 1.0)
        cos = cos_ref[...] * factor
        sin = sin_ref[...] * factor
        for h in range(heads):
            a = proj[h * HD : h * HD + HD // 2]
            b = proj[h * HD + HD // 2 : (h + 1) * HD]
            out_ref[h * HD : h * HD + HD // 2, :] = (a * cos - b * sin).astype(BF)
            out_ref[h * HD + HD // 2 : (h + 1) * HD, :] = (b * cos + a * sin).astype(BF)

    @pl.when(step >= 4)
    def _():
        out_ref[...] = proj.astype(BF)


def project(own, rem, vec, cos_t, sin_t, w_qkv_t):
    half, width = own.shape
    tokens = 2 * half
    blk = width // 2
    return pl.pallas_call(
        project_kernel,
        grid=(6,),
        in_specs=[
            whole(own.shape),
            whole(rem.shape),
            whole(vec.shape),
            whole(cos_t.shape),
            whole(sin_t.shape),
            pl.BlockSpec((blk, width), lambda i: (i, 0)),
        ],
        out_specs=[
            whole((width, tokens)),
            pl.BlockSpec((blk, tokens), lambda i: (i, 0)),
        ],
        out_shape=[
            jax.ShapeDtypeStruct((width, tokens), BF),
            jax.ShapeDtypeStruct((3 * width, tokens), BF),
        ],
        compiler_params=params(),
        cost_estimate=pl.CostEstimate(
            flops=6 * tokens * width * width, bytes_accessed=14 << 20, transcendentals=0
        ),
        name="project",
    )(own, rem, vec, cos_t, sin_t, w_qkv_t)


def attend_kernel(q_ref, k_ref, v_ref, att_ref, e_ref, linv_ref, q_mask, v_ext):
    tokens = q_ref.shape[1]
    tile = 256
    zero = jnp.zeros((HD, tokens), BF)
    k_nat = k_ref[...].T
    q_mask[0, 0:HD, :] = q_ref[0:HD, :]
    q_mask[0, HD:, :] = zero
    q_mask[1, 0:HD, :] = zero
    q_mask[1, HD:, :] = q_ref[HD:, :]
    for h in range(2):
        v_ext[h, 0:HD, :] = v_ref[h * HD : (h + 1) * HD, :]
        v_ext[h, HD:, :] = jnp.ones((16, tokens), BF)
    for h in range(2):
        for t in range(tokens // tile):
            cols = slice(t * tile, (t + 1) * tile)
            s = mm(k_nat, q_mask[h, :, cols])
            top = jnp.max(s, axis=0, keepdims=True)
            e = jnp.exp(s - top).astype(BF)
            e_ref[h, :, cols] = e
            mix = mm(v_ext[h], e)
            linv = 1.0 / mix[HD : HD + 1, :]
            linv_ref[0, h : h + 1, cols] = linv
            att_ref[h * HD : (h + 1) * HD, cols] = (mix[0:HD, :] * linv).astype(BF)


def attend(qkv_t):
    tokens = qkv_t.shape[1]
    width = HEADS * HD

    def part(k):
        return pl.BlockSpec((2 * HD, tokens), lambda i: (i + k * PAIRS, 0))

    return pl.pallas_call(
        attend_kernel,
        grid=(PAIRS,),
        in_specs=[part(0), part(1), part(2)],
        out_specs=[
            part(0),
            pl.BlockSpec((2, tokens, tokens), lambda i: (i, 0, 0)),
            pl.BlockSpec((1, 8, tokens), lambda i: (i, 0, 0)),
        ],
        out_shape=[
            jax.ShapeDtypeStruct((width, tokens), BF),
            jax.ShapeDtypeStruct((HEADS, tokens, tokens), BF),
            jax.ShapeDtypeStruct((PAIRS, 8, tokens), F32),
        ],
        scratch_shapes=[
            pltpu.VMEM((2, 2 * HD, tokens), BF),
            pltpu.VMEM((2, HD + 16, tokens), BF),
        ],
        compiler_params=params(),
        cost_estimate=pl.CostEstimate(
            flops=16 * tokens * tokens * width,
            bytes_accessed=30 << 20,
            transcendentals=HEADS * tokens * tokens,
        ),
        name="attend",
    )(qkv_t, qkv_t, qkv_t)


def gelu_both(u):
    c = math.sqrt(2.0 / math.pi)
    u2 = u * u
    th = jnp.tanh(u * (c + (c * 0.044715) * u2))
    half = 0.5 * (1.0 + th)
    value = u * half
    slope = half + (0.5 * u) * (1.0 - th * th) * (c + (3.0 * c * 0.044715) * u2)
    return value, slope


def middle_kernel(
    att_ref,
    tok_own,
    tok_rem,
    cot_own,
    cot_rem,
    span_ref,
    vec_ref,
    b_up_ref,
    w_out_ref,
    w_up_ref,
    w_down_ref,
    out_own,
    out_rem,
    dx_ref,
    d_att_ref,
    g_out_ref,
    g_up_ref,
    g_down_ref,
    g_bup_ref,
    sums_ref,
    branch,
    x_one,
    act_two,
    d_down,
    down_acc,
    d_act,
    d_branch,
):
    step = pl.program_id(0)
    steps = pl.num_programs(0)
    tokens = att_ref.shape[1]
    half = tokens // 2
    tile = 256
    per_half = half // tile
    gate_one = vec_ref[0:1, :]
    mult_two = vec_ref[1:2, :]
    shift_two = vec_ref[2:3, :]
    gate_two = vec_ref[3:4, :]
    b_down = vec_ref[4:5, :]
    gain_two = vec_ref[5:6, :]
    scale_two = vec_ref[6:7, :]

    @pl.when(step == 0)
    def _():
        for part, (tok, cot) in enumerate(((tok_own, cot_own), (tok_rem, cot_rem))):
            for t in range(per_half):
                src = slice(t * tile, (t + 1) * tile)
                dst = slice(part * half + t * tile, part * half + (t + 1) * tile)
                br = mm(att_ref[:, dst], w_out_ref[...], TN)
                branch[dst, :] = br
                x = tok[src, :].astype(F32) + gate_one * br
                x_one[dst, :] = x
                n, _ = norm_parts(x)
                act_two[dst, :] = (n * mult_two + shift_two).astype(BF)
                grad_out = cot[src, :].astype(F32) * span_ref[dst, :]
                d_down[dst, :] = (gate_two * grad_out).astype(BF)

    up = mm(act_two[...], w_up_ref[...]) + b_up_ref[...]
    value, slope = gelu_both(up)
    hidden = value.astype(BF)
    d_hidden = mm(d_down[...], w_down_ref[...], NT)
    d_up_full = slope * d_hidden
    d_up = d_up_full.astype(BF)
    g_bup_ref[...] = col_sum(d_up.astype(F32))
    down_part = mm(hidden, w_down_ref[...])
    d_act_part = mm(d_up, w_up_ref[...], NT)
    g_down_ref[...] = mm(hidden, d_down[...], TN).astype(BF)
    g_up_ref[...] = mm(act_two[...], d_up, TN).astype(BF)

    @pl.when(step == 0)
    def _():
        down_acc[...] = down_part
        d_act[...] = d_act_part

    @pl.when(step > 0)
    def _():
        down_acc[...] += down_part
        d_act[...] += d_act_part

    @pl.when(step == steps - 1)
    def _():
        zero = jnp.zeros((1, gate_one.shape[1]), F32)
        s_gate_two, s_shift, s_pull, s_gate_one, s_bdown = zero, zero, zero, zero, zero
        for part, (cot, out) in enumerate(((cot_own, out_own), (cot_rem, out_rem))):
            for t in range(per_half):
                src = slice(t * tile, (t + 1) * tile)
                dst = slice(part * half + t * tile, part * half + (t + 1) * tile)
                x = x_one[dst, :]
                down = down_acc[dst, :] + b_down
                out[src, :] = (x + gate_two * down).astype(BF)
                grad_out = cot[src, :].astype(F32) * span_ref[dst, :]
                s_gate_two += col_sum(grad_out * down)
                s_bdown += col_sum(d_down[dst, :].astype(F32))
                n, rstd = norm_parts(x)
                da = d_act[dst, :]
                s_shift += col_sum(da)
                s_pull += col_sum(da * n)
                dx = grad_out + norm_pull(n, rstd, da * mult_two)
                dx_ref[dst, :] = dx
                s_gate_one += col_sum(dx * branch[dst, :])
                d_branch[dst, :] = (gate_one * dx).astype(BF)
        sums_ref[0:1, :] = s_gate_one
        sums_ref[1:2, :] = s_shift
        sums_ref[2:3, :] = s_pull * gain_two
        sums_ref[3:4, :] = s_gate_two
        sums_ref[4:5, :] = s_pull * (1.0 + scale_two)
        sums_ref[5:6, :] = s_bdown
        sums_ref[6:8, :] = jnp.zeros((2, gate_one.shape[1]), F32)
        g_out_ref[...] = mm(att_ref[...], d_branch[...]).astype(BF)
        d_att_ref[...] = mm(w_out_ref[...], d_branch[...], NT).astype(BF)


def middle(att_t, tok_own, tok_rem, cot_own, cot_rem, span, vec, b_up, w_out, w_up, w_down):
    width, tokens = att_t.shape
    half = tokens // 2
    ff = w_up.shape[1]
    tile = 512
    return pl.pallas_call(
        middle_kernel,
        grid=(ff // tile,),
        in_specs=[
            whole(att_t.shape),
            whole(tok_own.shape),
            whole(tok_rem.shape),
            whole(cot_own.shape),
            whole(cot_rem.shape),
            whole(span.shape),
            whole(vec.shape),
            pl.BlockSpec((1, tile), lambda i: (0, i)),
            whole(w_out.shape),
            pl.BlockSpec((width, tile), lambda i: (0, i)),
            pl.BlockSpec((tile, width), lambda i: (i, 0)),
        ],
        out_specs=[
            whole((half, width)),
            whole((half, width)),
            whole((tokens, width)),
            whole((width, tokens)),
            whole((width, width)),
            pl.BlockSpec((width, tile), lambda i: (0, i)),
            pl.BlockSpec((tile, width), lambda i: (i, 0)),
            pl.BlockSpec((1, tile), lambda i: (0, i)),
            whole((8, width)),
        ],
        out_shape=[
            jax.ShapeDtypeStruct((half, width), BF),
            jax.ShapeDtypeStruct((half, width), BF),
            jax.ShapeDtypeStruct((tokens, width), F32),
            jax.ShapeDtypeStruct((width, tokens), BF),
            jax.ShapeDtypeStruct((width, width), BF),
            jax.ShapeDtypeStruct((width, ff), BF),
            jax.ShapeDtypeStruct((ff, width), BF),
            jax.ShapeDtypeStruct((1, ff), F32),
            jax.ShapeDtypeStruct((8, width), F32),
        ],
        scratch_shapes=[
            pltpu.VMEM((tokens, width), F32),
            pltpu.VMEM((tokens, width), F32),
            pltpu.VMEM((tokens, width), BF),
            pltpu.VMEM((tokens, width), BF),
            pltpu.VMEM((tokens, width), F32),
            pltpu.VMEM((tokens, width), F32),
            pltpu.VMEM((tokens, width), BF),
        ],
        compiler_params=params(),
        cost_estimate=pl.CostEstimate(
            flops=12 * tokens * width * ff + 6 * tokens * width * width,
            bytes_accessed=40 << 20,
            transcendentals=tokens * ff,
        ),
        name="middle",
    )(att_t, tok_own, tok_rem, cot_own, cot_rem, span, vec, b_up, w_out, w_up, w_down)


def attend_back_kernel(
    q_ref, k_ref, v_ref, att_ref, d_att_ref, e_ref, linv_ref, cos_ref, sin_ref, out_ref, do_mask
):
    tokens = q_ref.shape[1]
    tile = 256
    zero = jnp.zeros((HD, tokens), BF)
    v_nat = v_ref[...].T
    cos = cos_ref[...]
    sin = sin_ref[...]

    def unrotate(x):
        low = x.astype(BF).astype(F32)
        a, b = low[0 : HD // 2], low[HD // 2 :]
        return a * cos + b * sin, b * cos - a * sin

    for h in range(2):
        rows = slice(h * HD, (h + 1) * HD)
        linv = linv_ref[0, h : h + 1, :]
        d_o = d_att_ref[rows, :].astype(F32)
        d_os = (d_o * linv).astype(BF)
        do_mask[h, rows, :] = d_os
        do_mask[h, (1 - h) * HD : (2 - h) * HD, :] = zero
        inner = col_sum(d_o * att_ref[rows, :].astype(F32)) * linv
        d_values = mm(d_os, e_ref[h], NT)
        out_ref[2, rows, :] = d_values.astype(BF)
        d_keys = jnp.zeros((HD, tokens), F32)
        d_queries = []
        for t in range(tokens // tile):
            cols = slice(t * tile, (t + 1) * tile)
            d_probs = mm(v_nat, do_mask[h, :, cols])
            d_s = (e_ref[h, :, cols].astype(F32) * (d_probs - inner[:, cols])).astype(BF)
            d_queries.append(mm(k_ref[rows, :], d_s))
            d_keys += mm(q_ref[rows, cols], d_s, NT)
        dq = jnp.concatenate(d_queries, axis=1) * HD**-0.5
        lead, trail = unrotate(dq)
        out_ref[0, h * HD : h * HD + HD // 2, :] = lead.astype(BF)
        out_ref[0, h * HD + HD // 2 : (h + 1) * HD, :] = trail.astype(BF)
        lead, trail = unrotate(d_keys)
        out_ref[1, h * HD : h * HD + HD // 2, :] = lead.astype(BF)
        out_ref[1, h * HD + HD // 2 : (h + 1) * HD, :] = trail.astype(BF)


def attend_back(qkv_t, att_t, d_att_t, e, linv, cos_t, sin_t):
    tokens = qkv_t.shape[1]
    width = HEADS * HD

    def part(k):
        return pl.BlockSpec((2 * HD, tokens), lambda i: (i + k * PAIRS, 0))

    return pl.pallas_call(
        attend_back_kernel,
        grid=(PAIRS,),
        in_specs=[
            part(0),
            part(1),
            part(2),
            part(0),
            part(0),
            pl.BlockSpec((2, tokens, tokens), lambda i: (i, 0, 0)),
            pl.BlockSpec((1, 8, tokens), lambda i: (i, 0, 0)),
            whole(cos_t.shape),
            whole(sin_t.shape),
        ],
        out_specs=pl.BlockSpec((3, 2 * HD, tokens), lambda i: (0, i, 0)),
        out_shape=jax.ShapeDtypeStruct((3, width, tokens), BF),
        scratch_shapes=[pltpu.VMEM((2, 2 * HD, tokens), BF)],
        compiler_params=params(),
        cost_estimate=pl.CostEstimate(
            flops=32 * tokens * tokens * width, bytes_accessed=36 << 20, transcendentals=0
        ),
        name="attend_back",
    )(qkv_t, qkv_t, qkv_t, att_t, d_att_t, e, linv, cos_t, sin_t)


def tail_kernel(tok_own, tok_rem, d_proj_ref, w_ref, dx_ref, vec_ref, own_ref, rem_ref, sums_ref):
    step = pl.program_id(0)
    steps = pl.num_programs(0)
    mult_one = vec_ref[0:1, :]
    gain_one = vec_ref[2:3, :]
    scale_one = vec_ref[3:4, :]
    d_act = mm(d_proj_ref[...], w_ref[...], TN)

    def finish(tok, out):
        n, rstd = norm_parts(tok[...].astype(F32))
        grad = dx_ref[...] + norm_pull(n, rstd, d_act * mult_one)
        out[...] = grad.astype(out.dtype)
        return col_sum(d_act), col_sum(d_act * n)

    @pl.when(step == 0)
    def _():
        shift, pull = finish(tok_rem, rem_ref)
        sums_ref[0:1, :] = shift
        sums_ref[1:2, :] = pull
        sums_ref[2:, :] = jnp.zeros((6, shift.shape[1]), F32)

    @pl.when(step == steps - 1)
    def _():
        shift, pull = finish(tok_own, own_ref)
        shift = sums_ref[0:1, :] + shift
        pull = sums_ref[1:2, :] + pull
        sums_ref[0:1, :] = shift
        sums_ref[1:2, :] = pull * gain_one
        sums_ref[2:3, :] = pull * (1.0 + scale_one)


def tail(tok_own, tok_rem, d_proj_t, w_qkv_t, dx, vec):
    half, width = tok_own.shape
    return pl.pallas_call(
        tail_kernel,
        grid=(2,),
        in_specs=[
            whole(tok_own.shape),
            whole(tok_rem.shape),
            pl.BlockSpec((3 * width, half), lambda i: (0, 1 - i)),
            whole(w_qkv_t.shape),
            pl.BlockSpec((half, width), lambda i: (1 - i, 0)),
            whole(vec.shape),
        ],
        out_specs=[whole((half, width)), whole((half, width)), whole((8, width))],
        out_shape=[
            jax.ShapeDtypeStruct((half, width), F32),
            jax.ShapeDtypeStruct((half, width), BF),
            jax.ShapeDtypeStruct((8, width), F32),
        ],
        compiler_params=params(),
        cost_estimate=pl.CostEstimate(
            flops=12 * half * width * width, bytes_accessed=20 << 20, transcendentals=0
        ),
        name="tail",
    )(tok_own, tok_rem, d_proj_t, w_qkv_t, dx, vec)


def weight_grad_kernel(act_ref, d_proj_ref, out_ref):
    out_ref[...] = mm(act_ref[...], d_proj_ref[...], NT).astype(BF)


def weight_grad(act_t, d_proj_t):
    width, tokens = act_t.shape
    cols = d_proj_t.shape[0]
    tile = 768
    return pl.pallas_call(
        weight_grad_kernel,
        grid=(cols // tile,),
        in_specs=[whole(act_t.shape), pl.BlockSpec((tile, tokens), lambda i: (i, 0))],
        out_specs=pl.BlockSpec((width, tile), lambda i: (0, i)),
        out_shape=jax.ShapeDtypeStruct((width, cols), BF),
        compiler_params=params(),
        cost_estimate=pl.CostEstimate(
            flops=2 * cols * width * tokens, bytes_accessed=12 << 20, transcendentals=0
        ),
        name="weight_grad",
    )(act_t, d_proj_t)


def time_features(time_steps, pair_count):
    frequency = jnp.exp(-math.log(10000.0) * jnp.arange(pair_count, dtype=F32) / pair_count)
    angles = time_steps.astype(F32)[:, None] * frequency[None, :]
    return jnp.concatenate([jnp.cos(angles), jnp.sin(angles)], axis=-1)


def per_device(
    tokens,
    cotangent,
    time_index,
    span_starts,
    span_lengths,
    w_ada,
    b_ada,
    gain_one,
    w_qkv,
    w_out,
    gain_two,
    w_up,
    b_up,
    w_down,
    b_down,
):
    seqs_dev, half, width = tokens.shape
    length = 2 * half
    rank = lax.axis_index("seq")
    swap = [(0, 1), (1, 0)]

    def pick(x, i):
        return lax.dynamic_index_in_dim(x, i, 0, keepdims=False)

    tok_own, tok_send = pick(tokens, rank), pick(tokens, 1 - rank)
    cot_own, cot_send = pick(cotangent, rank), pick(cotangent, 1 - rank)
    tok_rem = lax.ppermute(tok_send, "seq", swap)
    cot_rem = lax.ppermute(cot_send, "seq", swap)

    here = jnp.arange(half, dtype=jnp.int32)
    place = jnp.concatenate([rank * half + here, (1 - rank) * half + here])
    frequency = jnp.exp(-math.log(10000.0) * jnp.arange(HD // 2, dtype=F32) / (HD // 2))
    angles = frequency[:, None] * place.astype(F32)[None, :]
    cos_t, sin_t = jnp.cos(angles), jnp.sin(angles)
    start, extent = pick(span_starts, rank), pick(span_lengths, rank)
    span = jnp.where((place >= start) & (place < start + extent), 2.0, 0.5).astype(F32)[:, None]

    time_own = lax.dynamic_slice_in_dim(time_index, rank, 1)
    cond_act = jax.nn.silu(time_features(time_own, w_ada.shape[0] // 2))
    modulation = (
        jnp.dot(cond_act, w_ada.astype(F32), precision=lax.Precision.HIGHEST)[0] + b_ada
    )
    shift_one, scale_one, gate_one, shift_two, scale_two, gate_two = jnp.split(modulation, 6)
    zeros = jnp.zeros_like(shift_one)
    vec_one = jnp.stack(
        [gain_one * (1.0 + scale_one), shift_one, gain_one, scale_one, zeros, zeros, zeros, zeros]
    )
    vec_two = jnp.stack(
        [
            gate_one,
            gain_two * (1.0 + scale_two),
            shift_two,
            gate_two,
            b_down,
            gain_two,
            scale_two,
            zeros,
        ]
    )
    w_qkv_t = w_qkv.T

    act_t, qkv_t = project(tok_own, tok_rem, vec_one, cos_t, sin_t, w_qkv_t)
    att_t, e, linv = attend(qkv_t)
    out_own, out_rem, dx, d_att_t, g_out, g_up, g_down, g_bup, sums_two = middle(
        att_t, tok_own, tok_rem, cot_own, cot_rem, span, vec_two, b_up[None], w_out, w_up, w_down
    )
    d_proj = attend_back(qkv_t, att_t, d_att_t, e, linv, cos_t, sin_t)
    d_proj_t = d_proj.reshape(3 * width, length)
    g_own, g_rem, sums_one = tail(tok_own, tok_rem, d_proj_t, w_qkv_t, dx, vec_one)
    g_qkv = weight_grad(act_t, d_proj_t)

    def spread(own, other):
        first = jnp.where(rank == 0, own, other)
        second = jnp.where(rank == 0, other, own)
        return jnp.stack([first, second])

    output = spread(out_own, lax.ppermute(out_rem, "seq", swap))
    grad_tokens = spread(g_own, lax.ppermute(g_rem, "seq", swap).astype(F32))

    gate_sums = jnp.concatenate([sums_two[:6].reshape(-1), g_bup[0], time_own.astype(F32)])
    early = lax.all_gather(gate_sums, ("dp", "seq"))
    late = lax.all_gather(sums_one[:3].reshape(-1), ("dp", "seq"))
    everyone = early[:, -1]
    ff = w_up.shape[1]
    features = jax.nn.silu(time_features(everyone, w_ada.shape[0] // 2))
    d_mod = jnp.concatenate([late[:, : 2 * width], early[:, : 4 * width]], axis=1)
    dp = lax.axis_index("dp")

    def mine(x, axis=0):
        size = x.shape[axis] // lax.axis_size("dp")
        return lax.dynamic_slice_in_dim(x, dp * size, size, axis)

    s_w_ada = jnp.dot(mine(features, 1).T, d_mod, precision=lax.Precision.HIGHEST)
    s_b_ada = jnp.sum(mine(d_mod, 1), axis=0)
    s_gain_one = jnp.sum(mine(late[:, 2 * width :], 1), axis=0)
    s_gain_two = jnp.sum(mine(early[:, 4 * width : 5 * width], 1), axis=0)
    s_b_down = jnp.sum(mine(early[:, 5 * width : 6 * width], 1), axis=0)
    s_b_up = jnp.sum(mine(early[:, 6 * width : 6 * width + ff], 1), axis=0)

    def reduce_rows(g):
        part = lax.psum_scatter(g, "dp", scatter_dimension=0, tiled=True)
        return lax.psum(part, "seq").astype(F32)

    return (
        output,
        grad_tokens,
        s_w_ada,
        s_b_ada,
        s_gain_one,
        reduce_rows(g_qkv),
        reduce_rows(g_out),
        s_gain_two,
        reduce_rows(g_up),
        s_b_up,
        reduce_rows(g_down),
        s_b_down,
    )


def solution(mesh):
    rows = P("dp", "seq", None)
    return jax.shard_map(
        per_device,
        mesh=mesh,
        in_specs=(rows, rows, P("dp"), P("dp"), P("dp")) + (P(),) * 10,
        out_specs=(
            rows,
            rows,
            P("dp", None),
            P("dp"),
            P("dp"),
            P("dp", None),
            P("dp", None),
            P("dp"),
            P("dp", None),
            P("dp"),
            P("dp", None),
            P("dp"),
        ),
        check_vma=False,
    )
```

time: 1090 us -> 483 us (0.44); the launches traced: 1070 us -> 480 us
  waiting for transfers between devices: 532 us -> 204 us
  matrix products: 282 us -> 1.87 us
  Pallas kernels: 0 us -> 159 us
  other arithmetic: 130 us -> 19.9 us
  local copies, waits for them, and re-layouts: 52.5 us -> 17.7 us
    reduce_scatter x7 -> x4, waiting for transfers between devices: 463 us -> 148 us  [reduce_rows(): part = lax.psum_scatter(g, 'dp', scatter_dimension=0, tiled=True)]
    dot_general x28 -> x2, matrix products: 282 us -> 1.87 us  [the longest x1 1.22 us: per_device(): jnp.dot(mine(features, 1).T, d_mod, precision=lax.Precision.HIGHEST)]
    pallas_call x0 -> x6, Pallas kernels: none -> 159 us  [the longest x1 50.8 us: middle(): pl.pallas_call(middle_kernel, grid=(ff // tile,), in_specs=[whole(att_t.s...]
    all_gather x2 -> x0, waiting for transfers between devices: 68.3 us -> none  [the longest x1 47.1 us: per_device(): lax.all_gather(keys_rot, 'seq', axis=1, tiled=True)]
    convert_element_type x20 -> x6, other arithmetic: 72.9 us -> 5.73 us  [the longest x4 5.14 us: reduce_rows(): return lax.psum(part, 'seq').astype(F32)]
    all_gather x0 -> x1, blocking collectives: none -> 53.9 us  [per_device(): late = lax.all_gather(sums_one[:3].reshape(-1), ('dp', 'seq'))]
    unnamed x1 -> x0, blocking collectives: 52.1 us -> none
    psum x1, waiting for transfers between devices: 0.01 us -> 31.6 us  [reduce_rows(): return lax.psum(part, 'seq').astype(F32)]
  transfers between devices with their start and end apart: 10 -> 10, of which waited for: 9 -> 5; matrix products, arithmetic and copies ran while one was open for 12% -> 6% of each run, Pallas kernels for 0% -> 23%
where the time goes in v1:
time: 483 us; the launch traced here: 480 us
  waiting for transfers between devices  204 us (42%)
  Pallas kernels  159 us (33%)
  blocking collectives  53.9 us (11%)
  other arithmetic  19.9 us (4%)
  local copies, waits for them, and re-layouts  17.7 us (4%)
  between operations  17.4 us (4%)
  starting transfers between devices  5.64 us (1%)
    reduce_scatter x4, waiting for transfers between devices, reduce_rows(): part = lax.psum_scatter(g, 'dp', scatter_dimension=0, tiled=True)  148 us
    all_gather x1, blocking collectives, per_device(): late = lax.all_gather(sums_one[:3].reshape(-1), ('dp', 'seq'))  53.9 us
    pallas_call x1, Pallas kernels, middle(): pl.pallas_call(middle_kernel, grid=(ff // tile,), in_specs=[whole(att_t.s...  50.8 us
    pallas_call x1, Pallas kernels, attend(): pl.pallas_call(attend_kernel, grid=(PAIRS,), in_specs=[part(0), part(1),...  39.7 us
    pallas_call x1, Pallas kernels, attend_back(): pl.pallas_call(attend_back_kernel, grid=(PAIRS,), in_specs=[part(0), part...  38.4 us
    psum x1, waiting for transfers between devices, reduce_rows(): return lax.psum(part, 'seq').astype(F32)  31.6 us
    unnamed x7, waiting for transfers between devices  22.1 us
    pallas_call x1, Pallas kernels, tail(): pl.pallas_call(tail_kernel, grid=(2,), in_specs=[whole(tok_own.shape), wh...  11.6 us
  transfers between devices with their start and end apart: 10, of which 5 were waited for; matrix products, arithmetic and copies ran while one was open for 6% of the time, Pallas kernels for 23%

profile of v1, /device:TPU:10, one launch (start us, length us, event | category | flops | bytes accessed | tf_op | source)
XLA Modules:
  0.0 480.1 jit_solution(3406056316529023402)
XLA Ops:
  8.0 0.0 all-reduce.5.cloned.1.call-start
  8.1 2.5 dynamic-slice_bitcast_fusion.2
  10.6 0.6 collective-permute-start
  11.2 1.0 dynamic-slice_bitcast_fusion
  12.2 1.5 collective-permute-start.1
  13.7 0.6 dynamic-slice_convert_fusion
  14.3 0.7 multiply_sine_fusion.2
  15.0 0.7 convolution_reduce_fusion
  15.8 5.8 %copy.42 = bf16[768,2304]{0,1:T(8,128)(2,1)} copy(bf16[768,2304]{1,0:T(8,128)(2,1)} %param.23) | data formatting | bytes 7077888 | tf_op args[8]
  21.6 0.6 dynamic_slice.46
  22.2 0.6 dynamic_slice.47
  24.1 0.7 broadcast_compare_fusion
  24.7 0.3 copy.43
  25.0 0.3 copy.44
  25.4 0.6 stack.65.vec_ref
  26.1 0.6 stack.73.vec_ref
  26.7 1.2 multiply_sine_fusion
  28.0 0.9 and_select_fusion.span_ref
  28.8 2.4 collective-permute-done.rem_ref.tok_rem
  31.2 11.0 %project.1 = (bf16[768,1024]{1,0:T(8,128)(2,1)}, bf16[2304,1024]{1,0:T(8,128)(2,1)}) custom-call(bf16[512,768]{1,0:T(8,128)(2,1)} %get-tuple-element.57.own_ref.tok_own, bf16[512,768]{1,0:T(8,128)(2,1)} %collective-permute-done.rem_ref.tok_rem, f32[8,768]{1,0:T(8,128)} %stack.65.vec_ref, f32[32,1024]{1,0:T(8,128)} %get-tuple-element.71.cos_ref, ...), custom_call_target="tpu_custom_call" | custom-call | flops 3623878656 | bytes 14680064 | tf_op jit(solution)/shard_map/project/pallas_call | solution.py:98
  42.2 39.7 %attend.1 = (bf16[768,1024]{1,0:T(8,128)(2,1)}, bf16[12,1024,1024]{2,1,0:T(8,128)(2,1)}, f32[6,8,1024]{2,1,0:T(8,128)}) custom-call(bf16[2304,1024]{1,0:T(8,128)(2,1)} %get-tuple-element.29.q_ref.k_ref.v_ref, bf16[2304,1024]{1,0:T(8,128)(2,1)} %get-tuple-element.29.q_ref.k_ref.v_ref, bf16[2304,1024]{1,0:T(8,128)(2,1)} %get-tuple-element.29.q_ref.k_ref.v_ref), custom_call_target="tpu_custom_call" | custom-call | flops 12884901888 | bytes 31457280 | tf_op jit(solution)/shard_map/attend/pallas_call | solution.py:157
  82.0 50.8 %middle.1 = (bf16[512,768]{1,0:T(8,128)(2,1)}, bf16[512,768]{1,0:T(8,128)(2,1)}, f32[1024,768]{1,0:T(8,128)}, bf16[768,1024]{1,0:T(8,128)(2,1)}, bf16[768,768]{1...) custom-call(bf16[768,1024]{1,0:T(8,128)(2,1)} %get-tuple-element.30., ...), custom_call_target="tpu_custom_call" | custom-call | flops 32614907904 | bytes 41943040 | tf_op jit(solution)/shard_map/middle/pallas_call | solution.py:313
  132.8 0.7 reshape.130
  133.6 0.1 broadcast.104
  133.6 1.6 maximum_dynamic-update-slice_fusion
  135.2 0.9 copy-done.2
  136.2 0.0 reduce-scatter.7.cloned.1.call-start
  136.2 0.5 reduce-scatter.7.cloned.1.call-update
  136.8 0.0 reduce-scatter.5.cloned.1.call-start
  136.8 38.4 %attend_back.1 = bf16[3,768,1024]{2,1,0:T(8,128)(2,1)} custom-call(bf16[2304,1024]{1,0:T(8,128)(2,1)} %get-tuple-element.29.q_ref.k_ref.v_ref, bf16[2304,1024]{1,0:T(8,128)(2,1)} %get-tuple-element.29.q_ref.k_ref.v_ref, bf16[2304,1024]{1,0:T(8,128)(2,1)} %get-tuple-element.29.q_ref.k_ref.v_ref, bf16[768,1024]{1,0:T(8,128)(2,1)} %get-tuple-element.30.att_ref, ...), custom_call_target="tpu_custom_call" | custom-call | flops 25769803776 | bytes 37748736 | tf_op jit(solution)/shard_map/attend_back/pallas_call | solution.py:419
  175.2 7.7 %weight_grad.1 = bf16[768,2304]{1,0:T(8,128)(2,1)} custom-call(bf16[768,1024]{1,0:T(8,128)(2,1)} %get-tuple-element.42.act_ref, bf16[2304,1024]{1,0:T(8,128)(2,1)} %bitcast.42), custom_call_target="tpu_custom_call" | custom-call | flops 3623878656 | bytes 12582912 | tf_op jit(solution)/shard_map/weight_grad/pallas_call | solution.py:510
  182.9 0.0 reduce-scatter.11.cloned.1.call-start
  183.0 0.5 reduce-scatter.11.cloned.1.call-update
  183.5 0.0 reduce-scatter.9.cloned.1.call-start
  183.5 0.7 reduce-scatter.9.cloned.1.call-update
  184.2 0.0 all-reduce.7.cloned.1.call-start
  184.3 11.6 %tail.1 = (f32[512,768]{1,0:T(8,128)}, bf16[512,768]{1,0:T(8,128)(2,1)}, f32[8,768]{1,0:T(8,128)}) custom-call(bf16[512,768]{1,0:T(8,128)(2,1)} %get-tuple-element.57.own_ref.tok_own, bf16[512,768]{1,0:T(8,128)(2,1)} %collective-permute-done.rem_ref.tok_rem, bf16[2304,1024]{1,0:T(8,128)(2,1)} %bitcast.43, bf16[2304,768]{1,0:T(8,128)(2,1)} %bitcast.34, ...), custom_call_target="tpu_custom_call" | custom-call | flops 3623878656 | bytes 20971520 | tf_op jit(solution)/shard_map/tail/pallas_call | solution.py:477
  195.8 0.7 slice.29
  196.6 53.9 %all-gather.1 = f32[32,1,2304]{2,1,0:T(1,128)S(1)} all-gather(f32[1,1,2304]{2,1,0:T(1,128)S(1)} %reshape.134), channel_id=1, replica_groups=mesh['dp'=16,'seq'=2] {'dp','seq'}, dimensions={0}, use_global_device_ids=true | all-gather | bytes 304128 | tf_op jit(solution)/shard_map/all_gather | solution.py:612
  250.5 3.2 collective-permute-start.3
  253.8 0.1 collective-permute-start.2
  253.8 0.6 dynamic-slice_reduce_fusion.3
  254.4 20.3 %all-reduce.5.cloned.1.call-done = f32[245792]{0:T(1024)} async-done(((f32[245792]{0:T(1024)}), f32[245792]{0:T(1024)}) %all-reduce.5.cloned.1.call-update) | async-done | bytes 983184
  274.8 1.9 reshape.131
  276.6 0.1 fusion.21
  276.7 0.6 dynamic-slice_reduce_fusion.1
  277.3 0.6 dynamic-slice_reduce_fusion.2
  277.9 0.7 dynamic-slice_reduce_fusion
  278.6 0.7 fusion.4
  279.3 0.1 slice_reduce_fusion
  279.4 0.1 multiply_cosine_fusion.1
  279.5 1.2 fusion.2
  280.8 70.1 %reduce-scatter.11.cloned.1.call-done = bf16[192,768]{1,0:T(8,128)(2,1)} async-done(((bf16[3072,768]{1,0:T(8,128)(2,1)}), bf16[192,768]{1,0:T(8,128)(2,1)}) %reduce-scatter.11.cloned.1.call-update) | async-done | bytes 294928 | tf_op jit(solution)/shard_map/reduce_scatter | solution.py:631
  350.8 78.3 %reduce-scatter.9.cloned.1.call-done = bf16[48,3072]{1,0:T(8,128)(2,1)} async-done(((bf16[768,3072]{1,0:T(8,128)(2,1)}), bf16[48,3072]{1,0:T(8,128)(2,1)}) %reduce-scatter.9.cloned.1.call-update) | async-done | bytes 294928 | tf_op jit(solution)/shard_map/reduce_scatter | solution.py:631
  429.2 1.2 select_bitcast_fusion.1
  430.5 1.3 pad_maximum_fusion.1
  431.7 0.7 copy-done.4
  432.4 1.4 fusion
  433.9 1.9 pad_maximum_fusion
  435.7 31.6 %all-reduce.7.cloned.1.call-done = (bf16[48,2304]{1,0:T(8,128)(2,1)}, bf16[48,768]{1,0:T(8,128)(2,1)}, bf16[48,3072]{1,0:T(8,128)(2,1)}, bf16[192,768]{1,0:T(8,128)(2,1)}) async-done(((bf16[48,2304]{1,0:T(8,128)(2,1)}, bf16[48,768]{1,0:T(8,128)(2,1)}, bf16[48,3072]{1,0:T(8,128)(2,1)}, bf16[192,768]{1,0:T(8,128)(2,1)}), (bf16[48,2304]{1,0:T(8,128)(2,1)}, bf16[48,768]{1,0:T(8,128)(2,1)}, ...) | async-done | bytes 884752 | tf_op jit(solution)/shard_map/psum | solution.py:632
  467.3 1.9 convert_element_type.32
  469.2 1.8 convert_element_type.33
  471.0 0.8 convert_element_type.30
  471.8 0.7 convert_element_type.31
  (60 shorter events, 0.3 us)
Async XLA Ops:
  8.0 7.0 %copy-start = (bf16[128,4608]{1,0:T(8,128)(2,1)S(1)}, bf16[128,4608]{1,0:T(8,128)(2,1)}, u32[]{:S(2)}) copy-start(bf16[128,4608]{1,0:T(8,128)(2,1)} %param.20) | copy-start | bytes 3538948
  8.0 266.7 %all-reduce.5.cloned.1.call-start = ((), (), s32[]{:S(2)}) async-start(), calls=%async_computation.8 | async-start | bytes 1974272
  8.1 3.1 copy-start.3
  10.6 3.1 copy-start.12
  10.6 4.4 copy-start.9
  10.6 4.4 copy-start.10
  10.6 5.1 %copy-start.8 = (f32[4608]{0:T(1024)S(1)}, f32[4608]{0:T(1024)}, u32[]{:S(2)}) copy-start(f32[4608]{0:T(1024)} %param.21) | copy-start | bytes 55300
  10.6 20.6 %collective-permute-start = (bf16[512,768]{1,0:T(8,128)(2,1)S(1)}, bf16[512,768]{1,0:T(8,128)(2,1)}, u32[]{:S(2)}, u32[]{:S(2)}) collective-permute-start(bf16[512,768]{1,0:T(8,128)(2,1)S(1)} %get-tuple-element.56), channel_id=1, source_target_pairs={{0,1},{1,0},{2,3},{3,2},{4,5},{5,4},{6,7},{7,6},{8,9},{9,8},{10,11... | collective-permute-start | bytes 2359304 | tf_op jit(solution)/shard_map/ppermute | solution.py:557
  12.2 69.8 %collective-permute-start.1 = (bf16[512,768]{1,0:T(8,128)(2,1)S(1)}, bf16[512,768]{1,0:T(8,128)(2,1)}, u32[]{:S(2)}, u32[]{:S(2)}) collective-permute-start(bf16[512,768]{1,0:T(8,128)(2,1)S(1)} %get-tuple-element.54), channel_id=1, source_target_pairs={{0,1},{1,0},{2,3},{3,2},{4,5},{5,4},{6,7},{7,6},{8,9},{9,8},{10,11... | collective-permute-start | bytes 2359304 | tf_op jit(solution)/shard_map/ppermute | solution.py:558
  15.8 5.8 %copy-start.13 = (s32[2]{0:T(128)S(1)}, s32[2]{0:T(128)}, u32[]{:S(2)}) copy-start(s32[2]{0:T(128)} %param.18) | copy-start | bytes 28
  15.8 6.4 %copy-start.14 = (s32[2]{0:T(128)S(1)}, s32[2]{0:T(128)}, u32[]{:S(2)}) copy-start(s32[2]{0:T(128)} %param.19) | copy-start | bytes 28
  15.8 9.6 %copy-start.11 = (f32[768]{0:T(1024)S(1)}, f32[768]{0:T(1024)}, u32[]{:S(2)}) copy-start(f32[768]{0:T(1024)} %param.29) | copy-start | bytes 9220
  135.2 0.9 copy-start.2
  136.2 144.6 %reduce-scatter.7.cloned.1.call-start = ((), (), s32[]{:S(2)}) async-start(), calls=%async_computation.5 | async-start | bytes 1253376 | tf_op jit(solution)/shard_map/reduce_scatter | solution.py:631
  136.8 144.0 %reduce-scatter.5.cloned.1.call-start = ((), (), s32[]{:S(2)}) async-start(), calls=%async_computation.4 | async-start | bytes 3760128 | tf_op jit(solution)/shard_map/reduce_scatter | solution.py:631
  182.9 167.9 %reduce-scatter.11.cloned.1.call-start = ((), (), s32[]{:S(2)}) async-start(), calls=%async_computation.7 | async-start | bytes 5013504 | tf_op jit(solution)/shard_map/reduce_scatter | solution.py:631
  183.5 245.7 %reduce-scatter.9.cloned.1.call-start = ((), (), s32[]{:S(2)}) async-start(), calls=%async_computation.6 | async-start | bytes 5013504 | tf_op jit(solution)/shard_map/reduce_scatter | solution.py:631
  184.2 283.1 %all-reduce.7.cloned.1.call-start = ((), (), s32[]{:S(2)}) async-start(), calls=%async_computation.9 | async-start | bytes 1769472 | tf_op jit(solution)/shard_map/psum | solution.py:632
  250.5 181.2 %collective-permute-start.3 = (bf16[512,768]{1,0:T(8,128)(2,1)}, bf16[512,768]{1,0:T(8,128)(2,1)}, u32[]{:S(2)}, u32[]{:S(2)}) collective-permute-start(bf16[512,768]{1,0:T(8,128)(2,1)} %get-tuple-element.38), channel_id=1, source_target_pairs={{0,1},{1,0},{2,3},{3,2},{4,5},{5,4},{6,7},{7,6},{8,9},{9,8},{10,11... | collective-permute-start | bytes 2359304 | tf_op jit(solution)/shard_map/ppermute | solution.py:608
  253.8 175.4 %collective-permute-start.2 = (bf16[512,768]{1,0:T(8,128)(2,1)}, bf16[512,768]{1,0:T(8,128)(2,1)}, u32[]{:S(2)}, u32[]{:S(2)}) collective-permute-start(bf16[512,768]{1,0:T(8,128)(2,1)} %get-tuple-element.32), channel_id=1, source_target_pairs={{0,1},{1,0},{2,3},{3,2},{4,5},{5,4},{6,7},{7,6},{8,9},{9,8},{10,11... | collective-permute-start | bytes 2359304 | tf_op jit(solution)/shard_map/ppermute | solution.py:607
  276.7 152.5 %copy-start.5 = (bf16[512,768]{1,0:T(8,128)(2,1)S(1)}, bf16[512,768]{1,0:T(8,128)(2,1)}, u32[]{:S(2)}) copy-start(bf16[512,768]{1,0:T(8,128)(2,1)} %get-tuple-element.31) | copy-start | bytes 2359300
  430.4 2.0 copy-start.4
  433.8 38.6 %copy-start.1 = (bf16[128,4608]{1,0:T(8,128)(2,1)S(1)}, bf16[128,4608]{1,0:T(8,128)(2,1)}, u32[]{:S(2)}) copy-start(bf16[128,4608]{1,0:T(8,128)(2,1)} %param.20) | copy-start | bytes 3538948
  467.3 3.7 copy-start.6
  467.3 4.5 copy-start.7
Sparse Core Ops, SparseCore 0:
  136.3 138.4 all-reduce.4
Sparse Core Ops, SparseCore 1:
  140.7 59.2 reduce-scatter.6
  204.2 68.1 reduce-scatter.4
  276.6 74.2 reduce-scatter.10
  354.7 74.4 reduce-scatter.8
  431.8 35.4 all-reduce.6

commit v2 on v1

--- a/solution.py
+++ b/solution.py
@@ -46,13 +46,49 @@
     return pl.ds(pl.multiple_of(index * size, size), size)
 
 
-def params(mib=56):
-    return pltpu.CompilerParams(vmem_limit_bytes=mib * MIB)
+def params(mib=56, collective_id=None):
+    if collective_id is None:
+        return pltpu.CompilerParams(vmem_limit_bytes=mib * MIB)
+    return pltpu.CompilerParams(
+        vmem_limit_bytes=mib * MIB, collective_id=collective_id, has_side_effects=True
+    )
 
 
 def whole(shape):
     zeros = (0,) * len(shape)
     return pl.BlockSpec(shape, lambda *_: zeros)
+
+
+MESH = pl.DeviceIdType.MESH
+ANY = pl.BlockSpec(memory_space=pl.ANY)
+SEMS = [pltpu.SemaphoreType.DMA, pltpu.SemaphoreType.DMA]
+
+
+def greet(*partners):
+    barrier = pltpu.get_barrier_semaphore()
+    for partner in partners:
+        pl.semaphore_signal(barrier, inc=1, device_id=partner, device_id_type=MESH)
+    pl.semaphore_wait(barrier, len(partners))
+
+
+def remote(src, dst, send, recv, device):
+    return pltpu.make_async_remote_copy(
+        src_ref=src, dst_ref=dst, send_sem=send, recv_sem=recv, device_id=device, device_id_type=MESH
+    )
+
+
+def seq_partner():
+    return (lax.axis_index("dp"), 1 - lax.axis_index("seq"))
+
+
+def swap_start(src, dst, send, recv):
+    partner = seq_partner()
+    greet(partner)
+    remote(src, dst, send, recv, partner).start()
+
+
+def swap_wait(src, dst, send, recv):
+    remote(src, dst, send, recv, seq_partner()).wait()
 
 
 def project_kernel(own_ref, rem_ref, vec_ref, cos_ref, sin_ref, w_ref, act_ref, out_ref):
@@ -122,7 +158,16 @@
     )(own, rem, vec, cos_t, sin_t, w_qkv_t)
 
 
-def attend_kernel(q_ref, k_ref, v_ref, att_ref, e_ref, linv_ref, q_mask, v_ext):
+def attend_kernel(
+    q_ref, k_ref, v_ref, cot_ref, att_ref, e_ref, linv_ref, cot_rem, q_mask, v_ext, send, recv
+):
+    step = pl.program_id(0)
+    cot_send = cot_ref.at[1 - lax.axis_index("seq")]
+
+    @pl.when(step == 0)
+    def _():
+        swap_start(cot_send, cot_rem, send, recv)
+
     tokens = q_ref.shape[1]
     tile = 256
     zero = jnp.zeros((HD, tokens), BF)
@@ -146,8 +191,12 @@
             linv_ref[0, h : h + 1, cols] = linv
             att_ref[h * HD : (h + 1) * HD, cols] = (mix[0:HD, :] * linv).astype(BF)
 
-
-def attend(qkv_t):
+    @pl.when(step == pl.num_programs(0) - 1)
+    def _():
+        swap_wait(cot_send, cot_rem, send, recv)
+
+
+def attend(qkv_t, cotangent):
     tokens = qkv_t.shape[1]
     width = HEADS * HD
 
@@ -157,29 +206,32 @@
     return pl.pallas_call(
         attend_kernel,
         grid=(PAIRS,),
-        in_specs=[part(0), part(1), part(2)],
+        in_specs=[part(0), part(1), part(2), ANY],
         out_specs=[
             part(0),
             pl.BlockSpec((2, tokens, tokens), lambda i: (i, 0, 0)),
             pl.BlockSpec((1, 8, tokens), lambda i: (i, 0, 0)),
+            ANY,
         ],
         out_shape=[
             jax.ShapeDtypeStruct((width, tokens), BF),
             jax.ShapeDtypeStruct((HEADS, tokens, tokens), BF),
             jax.ShapeDtypeStruct((PAIRS, 8, tokens), F32),
+            jax.ShapeDtypeStruct(cotangent.shape[1:], BF),
         ],
         scratch_shapes=[
             pltpu.VMEM((2, 2 * HD, tokens), BF),
             pltpu.VMEM((2, HD + 16, tokens), BF),
-        ],
-        compiler_params=params(),
+        ]
+        + SEMS,
+        compiler_params=params(collective_id=1),
         cost_estimate=pl.CostEstimate(
             flops=16 * tokens * tokens * width,
             bytes_accessed=30 << 20,
             transcendentals=HEADS * tokens * tokens,
         ),
         name="attend",
-    )(qkv_t, qkv_t, qkv_t)
+    )(qkv_t, qkv_t, qkv_t, cotangent)
 
 
 def gelu_both(u):
@@ -368,8 +420,28 @@
 
 
 def attend_back_kernel(
-    q_ref, k_ref, v_ref, att_ref, d_att_ref, e_ref, linv_ref, cos_ref, sin_ref, out_ref, do_mask
+    q_ref,
+    k_ref,
+    v_ref,
+    att_ref,
+    d_att_ref,
+    e_ref,
+    linv_ref,
+    cos_ref,
+    sin_ref,
+    give_ref,
+    out_ref,
+    take_ref,
+    do_mask,
+    send,
+    recv,
 ):
+    step = pl.program_id(0)
+
+    @pl.when(step == 0)
+    def _():
+        swap_start(give_ref, take_ref, send, recv)
+
     tokens = q_ref.shape[1]
     tile = 256
     zero = jnp.zeros((HD, tokens), BF)
@@ -408,8 +480,12 @@
         out_ref[1, h * HD : h * HD + HD // 2, :] = lead.astype(BF)
         out_ref[1, h * HD + HD // 2 : (h + 1) * HD, :] = trail.astype(BF)
 
-
-def attend_back(qkv_t, att_t, d_att_t, e, linv, cos_t, sin_t):
+    @pl.when(step == pl.num_programs(0) - 1)
+    def _():
+        swap_wait(give_ref, take_ref, send, recv)
+
+
+def attend_back(qkv_t, att_t, d_att_t, e, linv, cos_t, sin_t, give):
     tokens = qkv_t.shape[1]
     width = HEADS * HD
 
@@ -429,16 +505,20 @@
             pl.BlockSpec((1, 8, tokens), lambda i: (i, 0, 0)),
             whole(cos_t.shape),
             whole(sin_t.shape),
-        ],
-        out_specs=pl.BlockSpec((3, 2 * HD, tokens), lambda i: (0, i, 0)),
-        out_shape=jax.ShapeDtypeStruct((3, width, tokens), BF),
-        scratch_shapes=[pltpu.VMEM((2, 2 * HD, tokens), BF)],
-        compiler_params=params(),
+            ANY,
+        ],
+        out_specs=[pl.BlockSpec((3, 2 * HD, tokens), lambda i: (0, i, 0)), ANY],
+        out_shape=[
+            jax.ShapeDtypeStruct((3, width, tokens), BF),
+            jax.ShapeDtypeStruct(give.shape, give.dtype),
+        ],
+        scratch_shapes=[pltpu.VMEM((2, 2 * HD, tokens), BF)] + SEMS,
+        compiler_params=params(collective_id=2),
         cost_estimate=pl.CostEstimate(
             flops=32 * tokens * tokens * width, bytes_accessed=36 << 20, transcendentals=0
         ),
         name="attend_back",
-    )(qkv_t, qkv_t, qkv_t, att_t, d_att_t, e, linv, cos_t, sin_t)
+    )(qkv_t, qkv_t, qkv_t, att_t, d_att_t, e, linv, cos_t, sin_t, give)
 
 
 def tail_kernel(tok_own, tok_rem, d_proj_ref, w_ref, dx_ref, vec_ref, own_ref, rem_ref, sums_ref):
@@ -519,6 +599,178 @@
         ),
         name="weight_grad",
     )(act_t, d_proj_t)
+
+
+def reduce_kernel(count, *refs):
+    grads, mod_ref, sum_ref = refs[:count], refs[count], refs[count + 1]
+    refs = refs[count + 2 :]
+    outs, mod_out, sum_out = refs[:count], refs[count], refs[count + 1]
+    refs = refs[count + 2 :]
+    own, from_core, from_y, from_z, last, from_x = (
+        refs[k * count : (k + 1) * count] for k in range(6)
+    )
+    sum_own, sum_core, sum_y, sum_z, sum_x, mod_all, sems, z_send, z_recv = refs[6 * count :]
+    dp, x = lax.axis_index("dp"), lax.axis_index("seq")
+    z, y, c = dp // 4, lax.rem(dp // 2, 2), lax.rem(dp, 2)
+    zs = mod_all.shape[0]
+    core = (dp + 1 - 2 * c, x)
+    across = (dp + 2 - 4 * y, x)
+    facing = (dp, 1 - x)
+    far = [lax.rem(z + k, zs) for k in range(1, zs)]
+    far_devices = [(f * 4 + 2 * y + c, x) for f in far]
+
+    for i in range(count):
+        pltpu.make_async_copy(grads[i].at[:, :, c], own[i], sems.at[i, 8]).start()
+    mine = (z, y, c, x)
+    pltpu.make_async_copy(mod_ref, mod_all.at[mine], sems.at[count, 8]).start()
+    pltpu.make_async_copy(sum_ref, sum_own, sems.at[count + 1, 8]).start()
+
+    greet(core, across, facing, *far_devices)
+
+    def over(stage, i, src, dst, device):
+        return remote(src, dst, sems.at[i, 2 * stage], sems.at[i, 2 * stage + 1], device)
+
+    def to_core(i):
+        return over(0, i, grads[i].at[:, :, 1 - c], from_core[i], core)
+
+    def to_across(i):
+        return over(1, i, own[i].at[:, 1 - y], from_y[i], across)
+
+    def to_facing(i):
+        return over(2, i, last[i], from_x[i], facing)
+
+    def to_far(i, k, incoming):
+        f = far[k]
+        return remote(
+            own[i].at[f, y] if i < count else sum_own if i > count else mod_all.at[z, :, :, x],
+            (from_z[i] if i < count else sum_z).at[f if incoming else z]
+            if i != count
+            else mod_all.at[f if incoming else z, :, :, x],
+            z_send.at[i, k],
+            z_recv.at[i, f if incoming else z],
+            far_devices[k],
+        )
+
+    def far_start(i):
+        for k in range(zs - 1):
+            to_far(i, k, False).start()
+
+    def far_wait(i):
+        for k in range(zs - 1):
+            to_far(i, k, False).wait_send()
+            to_far(i, k, True).wait_recv()
+
+    def mod_core():
+        return over(0, count, mod_all.at[mine], mod_all.at[mine], core)
+
+    def mod_core_in():
+        slot = mod_all.at[z, y, 1 - c, x]
+        return over(0, count, slot, slot, core)
+
+    def mod_across(row):
+        slot = mod_all.at[z, row, :, x]
+        return over(1, count, slot, slot, across)
+
+    def mod_facing(side):
+        slot = mod_all.at[:, :, :, side]
+        return over(2, count, slot, slot, facing)
+
+    def sum_swap(stage, dst, device):
+        return over(stage, count + 1, sum_own, dst, device)
+
+    for i in range(count):
+        to_core(i).start()
+    pltpu.make_async_copy(mod_ref, mod_all.at[mine], sems.at[count, 8]).wait()
+    pltpu.make_async_copy(sum_ref, sum_own, sems.at[count + 1, 8]).wait()
+    mod_core().start()
+    sum_swap(0, sum_core, core).start()
+
+    for i in range(count):
+        pltpu.make_async_copy(grads[i].at[:, :, c], own[i], sems.at[i, 8]).wait()
+        to_core(i).wait()
+        for a in range(zs):
+            for b in range(2):
+                own[i][a, b] = own[i][a, b] + from_core[i][a, b]
+        to_across(i).start()
+    mod_core().wait_send()
+    mod_core_in().wait_recv()
+    mod_across(y).start()
+    sum_swap(0, sum_core, core).wait()
+    sum_own[...] += sum_core[...]
+    sum_swap(1, sum_y, across).start()
+
+    mod_across(y).wait_send()
+    mod_across(1 - y).wait_recv()
+    far_start(count)
+    sum_swap(1, sum_y, across).wait()
+    sum_own[...] += sum_y[...]
+    far_start(count + 1)
+    for i in range(count):
+        to_across(i).wait()
+        for a in range(zs):
+            own[i][a, y] = own[i][a, y] + from_y[i][a]
+        far_start(i)
+    far_wait(count)
+    mod_facing(x).start()
+    far_wait(count + 1)
+    sum_z[z] = sum_own[...]
+    total = sum_z[0]
+    for a in range(1, zs):
+        total += sum_z[a]
+    sum_own[...] = total
+    sum_swap(2, sum_x, facing).start()
+    for i in range(count):
+        far_wait(i)
+        from_z[i][z] = own[i][z, y]
+        total = from_z[i][0].astype(F32)
+        for a in range(1, zs):
+            total += from_z[i][a].astype(F32)
+        last[i][...] = total.astype(BF)
+        to_facing(i).start()
+    mod_facing(x).wait_send()
+    mod_facing(1 - x).wait_recv()
+    mod_out[...] = mod_all[...]
+    sum_swap(2, sum_x, facing).wait()
+    sum_out[...] = sum_own[...] + sum_x[...]
+    for i in range(count):
+        to_facing(i).wait()
+        outs[i][...] = last[i][...].astype(F32) + from_x[i][...].astype(F32)
+
+
+def reduce_all(grads, mod, sums, dp):
+    zs = dp // 4
+    grads = [g.reshape(zs, 2, 2, g.shape[0] // dp, g.shape[1]) for g in grads]
+    tails = [g.shape[3:] for g in grads]
+    count = len(grads)
+
+    def scratch(*lead):
+        return [pltpu.VMEM(lead + t, BF) for t in tails]
+
+    everyone = (zs, 2, 2, 2) + mod.shape
+    return pl.pallas_call(
+        functools.partial(reduce_kernel, count),
+        in_specs=[ANY] * (count + 2),
+        out_specs=[pl.BlockSpec(memory_space=pltpu.VMEM)] * (count + 2),
+        out_shape=[jax.ShapeDtypeStruct(t, F32) for t in tails]
+        + [jax.ShapeDtypeStruct(everyone, BF), jax.ShapeDtypeStruct(sums.shape, F32)],
+        scratch_shapes=scratch(zs, 2)
+        + scratch(zs, 2)
+        + scratch(zs)
+        + scratch(zs)
+        + scratch()
+        + scratch()
+        + [pltpu.VMEM(sums.shape, F32)] * 3
+        + [
+            pltpu.VMEM((zs,) + sums.shape, F32),
+            pltpu.VMEM(sums.shape, F32),
+            pltpu.VMEM(everyone, BF),
+            pltpu.SemaphoreType.DMA((count + 2, 9)),
+            pltpu.SemaphoreType.DMA((count + 2, zs)),
+            pltpu.SemaphoreType.DMA((count + 2, zs)),
+        ],
+        compiler_params=params(collective_id=3),
+        name="reduce_all",
+    )(*grads, mod, sums)
 
 
 def time_features(time_steps, pair_count):
@@ -553,9 +805,8 @@
         return lax.dynamic_index_in_dim(x, i, 0, keepdims=False)
 
     tok_own, tok_send = pick(tokens, rank), pick(tokens, 1 - rank)
-    cot_own, cot_send = pick(cotangent, rank), pick(cotangent, 1 - rank)
+    cot_own = pick(cotangent, rank)
     tok_rem = lax.ppermute(tok_send, "seq", swap)
-    cot_rem = lax.ppermute(cot_send, "seq", swap)
 
     here = jnp.arange(half, dtype=jnp.int32)
     place = jnp.concatenate([rank * half + here, (1 - rank) * half + here])
@@ -590,11 +841,11 @@
     w_qkv_t = w_qkv.T
 
     act_t, qkv_t = project(tok_own, tok_rem, vec_one, cos_t, sin_t, w_qkv_t)
-    att_t, e, linv = attend(qkv_t)
+    att_t, e, linv, cot_rem = attend(qkv_t, cotangent)
     out_own, out_rem, dx, d_att_t, g_out, g_up, g_down, g_bup, sums_two = middle(
         att_t, tok_own, tok_rem, cot_own, cot_rem, span, vec_two, b_up[None], w_out, w_up, w_down
     )
-    d_proj = attend_back(qkv_t, att_t, d_att_t, e, linv, cos_t, sin_t)
+    d_proj, out_back = attend_back(qkv_t, att_t, d_att_t, e, linv, cos_t, sin_t, out_rem)
     d_proj_t = d_proj.reshape(3 * width, length)
     g_own, g_rem, sums_one = tail(tok_own, tok_rem, d_proj_t, w_qkv_t, dx, vec_one)
     g_qkv = weight_grad(act_t, d_proj_t)
@@ -604,32 +855,47 @@
         second = jnp.where(rank == 0, other, own)
         return jnp.stack([first, second])
 
-    output = spread(out_own, lax.ppermute(out_rem, "seq", swap))
+    output = spread(out_own, out_back)
     grad_tokens = spread(g_own, lax.ppermute(g_rem, "seq", swap).astype(F32))
 
-    gate_sums = jnp.concatenate([sums_two[:6].reshape(-1), g_bup[0], time_own.astype(F32)])
-    early = lax.all_gather(gate_sums, ("dp", "seq"))
-    late = lax.all_gather(sums_one[:3].reshape(-1), ("dp", "seq"))
-    everyone = early[:, -1]
+    dp, dps = lax.axis_index("dp"), lax.axis_size("dp")
     ff = w_up.shape[1]
-    features = jax.nn.silu(time_features(everyone, w_ada.shape[0] // 2))
-    d_mod = jnp.concatenate([late[:, : 2 * width], early[:, : 4 * width]], axis=1)
-    dp = lax.axis_index("dp")
+    d_mod = jnp.concatenate([sums_one[:2].reshape(-1), sums_two[:4].reshape(-1)])
+    small = jnp.concatenate([sums_one[2], sums_two[4], sums_two[5], g_bup[0]])
+    grads = (g_qkv, g_out, g_up, g_down)
+    if dps % 4 == 0 and all(g.shape[0] % (16 * dps) == 0 for g in grads):
+        time_parts = jnp.concatenate([time_own // 32, time_own % 32]).astype(F32)
+        mod_rows = -(-(d_mod.size + 2) // 2048) * 16
+        mod = jnp.concatenate([d_mod, time_parts])
+        mod = jnp.pad(mod, (0, mod_rows * 128 - mod.size)).astype(BF).reshape(mod_rows, 128)
+        sum_rows = -(-small.size // 1024) * 8
+        sums = jnp.pad(small, (0, sum_rows * 128 - small.size)).reshape(sum_rows, 128)
+        *shards, mod_all, sums = reduce_all(grads, mod, sums, dps)
+        mod_all = mod_all.reshape(-1, mod_rows * 128).astype(F32)
+        d_mod_all = mod_all[:, : d_mod.size]
+        time_all = 32.0 * mod_all[:, d_mod.size] + mod_all[:, d_mod.size + 1]
+        small = sums.reshape(-1)[: small.size]
+    else:
+        shards = [
+            lax.psum(lax.psum_scatter(g, "dp", scatter_dimension=0, tiled=True), "seq").astype(F32)
+            for g in grads
+        ]
+        d_mod_all = lax.all_gather(d_mod, ("dp", "seq"))
+        time_all = lax.all_gather(time_own[0].astype(F32), ("dp", "seq"))
+        small = lax.psum(small, ("dp", "seq"))
 
     def mine(x, axis=0):
-        size = x.shape[axis] // lax.axis_size("dp")
+        size = x.shape[axis] // dps
         return lax.dynamic_slice_in_dim(x, dp * size, size, axis)
 
-    s_w_ada = jnp.dot(mine(features, 1).T, d_mod, precision=lax.Precision.HIGHEST)
-    s_b_ada = jnp.sum(mine(d_mod, 1), axis=0)
-    s_gain_one = jnp.sum(mine(late[:, 2 * width :], 1), axis=0)
-    s_gain_two = jnp.sum(mine(early[:, 4 * width : 5 * width], 1), axis=0)
-    s_b_down = jnp.sum(mine(early[:, 5 * width : 6 * width], 1), axis=0)
-    s_b_up = jnp.sum(mine(early[:, 6 * width : 6 * width + ff], 1), axis=0)
-
-    def reduce_rows(g):
-        part = lax.psum_scatter(g, "dp", scatter_dimension=0, tiled=True)
-        return lax.psum(part, "seq").astype(F32)
+    features = jax.nn.silu(time_features(time_all, w_ada.shape[0] // 2))
+    s_w_ada = jnp.dot(mine(features, 1).T, d_mod_all, precision=lax.Precision.HIGHEST)
+    s_b_ada = jnp.sum(mine(d_mod_all, 1), axis=0)
+    s_gain_one = mine(small[:width])
+    s_gain_two = mine(small[width : 2 * width])
+    s_b_down = mine(small[2 * width : 3 * width])
+    s_b_up = mine(small[3 * width :])
+    s_qkv, s_out, s_up, s_down = shards
 
     return (
         output,
@@ -637,12 +903,12 @@
         s_w_ada,
         s_b_ada,
         s_gain_one,
-        reduce_rows(g_qkv),
-        reduce_rows(g_out),
+        s_qkv,
+        s_out,
         s_gain_two,
-        reduce_rows(g_up),
+        s_up,
         s_b_up,
-        reduce_rows(g_down),
+        s_down,
         s_b_down,
     )
 

time: 483 us -> 404 us (0.84)
  waiting for transfers between devices: 204 us -> 14.9 us
  Pallas kernels: 159 us -> 342 us
  blocking collectives: 53.9 us -> 0 us
  between operations: 17.4 us -> 6.14 us
  other arithmetic: 19.9 us -> 8.74 us
  starting transfers between devices: 5.64 us -> 0.54 us
  local copies, waits for them, and re-layouts: 17.7 us -> 22.7 us
    pallas_call x0 -> x1, Pallas kernels: none -> 180 us  [reduce_all(): pl.pallas_call(functools.partial(reduce_kernel, count), in_specs=[ANY] *...]
    reduce_scatter x4 -> x0, waiting for transfers between devices: 148 us -> none  [reduce_rows(): part = lax.psum_scatter(g, 'dp', scatter_dimension=0, tiled=True)]
    all_gather x1 -> x0, blocking collectives: 53.9 us -> none  [per_device(): late = lax.all_gather(sums_one[:3].reshape(-1), ('dp', 'seq'))]
    psum x1 -> x0, waiting for transfers between devices: 31.6 us -> none  [reduce_rows(): return lax.psum(part, 'seq').astype(F32)]
    unnamed x7 -> x0, waiting for transfers between devices: 22.1 us -> none
    ppermute x1, waiting for transfers between devices: 0.01 us -> 14.9 us  [per_device(): grad_tokens = spread(g_own, lax.ppermute(g_rem, 'seq', swap).astype(F32))]
    convert_element_type x5 -> x1, other arithmetic: 5.72 us -> 0.21 us  [per_device(): mod_all = mod_all.reshape(-1, mod_rows * 128).astype(F32)]
    unnamed x34 -> x48, local copies, waits for them, and re-layouts: 7.57 us -> 10.7 us
  transfers between devices with their start and end apart: 10 -> 2, of which waited for: 5 -> 1; matrix products, arithmetic and copies ran while one was open for 6% -> 5% of each run, Pallas kernels for 23% -> 0%
where the time goes in v2:
time: 404 us; the launch traced here: 397 us
  Pallas kernels  342 us (85%)
  local copies, waits for them, and re-layouts  22.7 us (6%)
  waiting for transfers between devices  14.9 us (4%)
  other arithmetic  8.74 us (2%)
  between operations  6.14 us (2%)
    pallas_call x1, Pallas kernels, reduce_all(): pl.pallas_call(functools.partial(reduce_kernel, count), in_specs=[ANY] *...  180 us
    pallas_call x1, Pallas kernels, middle(): pl.pallas_call(middle_kernel, grid=(ff // tile,), in_specs=[whole(att_t.s...  51 us
    pallas_call x1, Pallas kernels, attend(): pl.pallas_call(attend_kernel, grid=(PAIRS,), in_specs=[part(0), part(1),...  41.7 us
    pallas_call x1, Pallas kernels, attend_back(): pl.pallas_call(attend_back_kernel, grid=(PAIRS,), in_specs=[part(0), part...  39 us
    ppermute x1, waiting for transfers between devices, per_device(): grad_tokens = spread(g_own, lax.ppermute(g_rem, 'seq', swap).astype(F32))  14.9 us
    pallas_call x1, Pallas kernels, tail(): pl.pallas_call(tail_kernel, grid=(2,), in_specs=[whole(tok_own.shape), wh...  11.5 us
    pallas_call x1, Pallas kernels, project(): pl.pallas_call(project_kernel, grid=(6,), in_specs=[whole(own.shape), who...  11 us
    unnamed x48, local copies, waits for them, and re-layouts  10.7 us
  transfers between devices with their start and end apart: 2, of which 1 were waited for; matrix products, arithmetic and copies ran while one was open for 5% of the time, Pallas kernels for 0%

profile of v2, /device:TPU:10, one launch (start us, length us, event | category | flops | bytes accessed | tf_op | source)
XLA Modules:
  0.0 396.9 jit_solution(14057469078131138614)
XLA Ops:
  0.6 0.0 copy-start
  0.7 2.5 dynamic-slice_bitcast_fusion.1
  3.2 0.5 collective-permute-start
  3.8 0.6 dynamic_slice.40
  7.6 0.1 multiply_sine_fusion.2
  7.7 0.0 copy-done.13
  7.7 0.7 convolution_reduce_fusion
  8.4 0.0 copy-done.11
  8.5 0.0 copy-start.16
  8.5 0.0 copy-start.19
  8.5 0.0 copy-start.20
  8.5 0.0 copy-start.8
  8.5 5.9 %copy.39 = bf16[768,2304]{0,1:T(8,128)(2,1)} copy(bf16[768,2304]{1,0:T(8,128)(2,1)} %param.23) | data formatting | bytes 7077888 | tf_op args[8]
  14.5 0.0 copy-done.19
  14.5 0.6 dynamic_slice.42
  15.1 0.6 dynamic_slice.43
  17.0 0.7 broadcast_compare_fusion
  17.6 0.3 copy.40
  17.9 0.3 copy.41
  18.3 0.6 stack.65.vec_ref
  18.9 0.6 stack.73.vec_ref
  19.5 0.1 fusion.19
  19.6 0.9 dynamic-slice_bitcast_fusion.cot_own
  20.6 1.2 multiply_sine_fusion
  21.8 0.9 and_select_fusion.span_ref
  22.7 0.0 collective-permute-done.rem_ref.tok_rem
  22.7 11.0 %project.1 = (bf16[768,1024]{1,0:T(8,128)(2,1)}, bf16[2304,1024]{1,0:T(8,128)(2,1)}) custom-call(bf16[512,768]{1,0:T(8,128)(2,1)} %get-tuple-element.71.own_ref.tok_own, bf16[512,768]{1,0:T(8,128)(2,1)} %collective-permute-done.rem_ref.tok_rem, f32[8,768]{1,0:T(8,128)} %stack.65.vec_ref, f32[32,1024]{1,0:T(8,128)} %get-tuple-element.84.cos_ref, ...), custom_call_target="tpu_custom_call" | custom-call | flops 3623878656 | bytes 14680064 | tf_op jit(solution)/shard_map/project/pallas_call | solution.py:134
  33.7 41.7 %attend.1 = (bf16[768,1024]{1,0:T(8,128)(2,1)}, bf16[12,1024,1024]{2,1,0:T(8,128)(2,1)}, f32[6,8,1024]{2,1,0:T(8,128)}, bf16[512,768]{1,0:T(8,128)(2,1)}) custom-call(bf16[2304,1024]{1,0:T(8,128)(2,1)} %get-tuple-element.38.q_ref.k_ref.v_ref, bf16[2304,1024]{1,0:T(8,128)(2,1)} %get-tuple-element.38.q_ref.k_ref.v_ref, ...), custom_call_target="tpu_custom_call" | custom-call | flops 12884901888 | bytes 31457280 | tf_op jit(solution)/shard_map/attend/pallas_call | solution.py:206
  75.4 51.0 %middle.1 = (bf16[512,768]{1,0:T(8,128)(2,1)}, bf16[512,768]{1,0:T(8,128)(2,1)}, f32[1024,768]{1,0:T(8,128)}, bf16[768,1024]{1,0:T(8,128)(2,1)}, bf16[768,768]{1...) custom-call(bf16[768,1024]{1,0:T(8,128)(2,1)} %get-tuple-element.39., ...), custom_call_target="tpu_custom_call" | custom-call | flops 32614907904 | bytes 41943040 | tf_op jit(solution)/shard_map/middle/pallas_call | solution.py:365
  126.4 39.0 %attend_back.1 = (bf16[3,768,1024]{2,1,0:T(8,128)(2,1)}, bf16[512,768]{1,0:T(8,128)(2,1)}) custom-call(bf16[2304,1024]{1,0:T(8,128)(2,1)} %get-tuple-element.38.q_ref.k_ref.v_ref, bf16[2304,1024]{1,0:T(8,128)(2,1)} %get-tuple-element.38.q_ref.k_ref.v_ref, bf16[2304,1024]{1,0:T(8,128)(2,1)} %get-tuple-element.38.q_ref.k_ref.v_ref, ...), custom_call_target="tpu_custom_call" | custom-call | flops 25769803776 | bytes 37748736 | tf_op jit(solution)/shard_map/attend_back/pallas_call | solution.py:495
  165.4 11.5 %tail.1 = (f32[512,768]{1,0:T(8,128)}, bf16[512,768]{1,0:T(8,128)(2,1)}, f32[8,768]{1,0:T(8,128)}) custom-call(bf16[512,768]{1,0:T(8,128)(2,1)} %get-tuple-element.71.own_ref.tok_own, bf16[512,768]{1,0:T(8,128)(2,1)} %collective-permute-done.rem_ref.tok_rem, bf16[2304,1024]{1,0:T(8,128)(2,1)} %bitcast.63, bf16[2304,768]{1,0:T(8,128)(2,1)} %bitcast.53, ...), custom_call_target="tpu_custom_call" | custom-call | flops 3623878656 | bytes 20971520 | tf_op jit(solution)/shard_map/tail/pallas_call | solution.py:557
  177.0 0.8 slice_reduce_fusion.2
  177.7 0.7 slice.99
  178.5 0.0 copy-start.14
  178.5 7.9 %weight_grad.1 = bf16[768,2304]{1,0:T(8,128)(2,1)} custom-call(bf16[768,1024]{1,0:T(8,128)(2,1)} %get-tuple-element.51.act_ref, bf16[2304,1024]{1,0:T(8,128)(2,1)} %bitcast.64), custom_call_target="tpu_custom_call" | custom-call | flops 3623878656 | bytes 12582912 | tf_op jit(solution)/shard_map/weight_grad/pallas_call | solution.py:590
  186.5 0.6 fusion.15.refs_4_
  187.1 0.6 fusion.4.refs_5_
  187.7 180.0 %reduce_all.1 = (f32[48,2304]{1,0:T(8,128)}, f32[48,768]{1,0:T(8,128)}, f32[48,3072]{1,0:T(8,128)}, f32[192,768]{1,0:T(8,128)}, bf16[4,2,2,2,48,128]{5,4,3,2,1,0:T(8,128)(2,1)}, /*index=5*/f32[48,128]{1,0:T(8,128)}) custom-call(bf16[4,2,2,48,2304]{4,3,2,1,0:T(8,128)(2,1)} %bitcast.54, bf16[4,2,2,48,768]{4,3,2,1,0:T(8,128)(2,1)} %bitcast.57, ...), custom_call_target="tpu_custom_call" | custom-call | tf_op jit(solution)/shard_map/reduce_all/pallas_call | solution.py:750
  367.7 1.1 copy.45
  368.8 0.8 copy.42
  369.6 0.2 convert_element_type.29
  369.9 0.2 slice.80
  370.0 0.5 copy-done.10
  370.6 0.6 dynamic_slice.46
  371.2 0.6 dynamic_slice.47
  371.8 0.6 dynamic_slice.49
  372.3 0.0 copy-done.17
  372.4 0.0 collective-permute-start.1
  372.4 0.7 dynamic-slice_reduce_fusion
  373.1 0.6 dynamic_slice.48
  373.7 0.1 select_bitcast_fusion.1
  373.8 1.3 pad_maximum_fusion.1
  375.1 0.1 multiply_cosine_fusion.1
  375.3 1.1 fusion.2
  376.3 14.9 %collective-permute-done.1 = bf16[512,768]{1,0:T(8,128)(2,1)S(1)} collective-permute-done((bf16[512,768]{1,0:T(8,128)(2,1)S(1)}, bf16[512,768]{1,0:T(8,128)(2,1)S(1)}, u32[]{:S(2)}, u32[]{:S(2)}) %collective-permute-start.1) | collective-permute-done | bytes 786464 | tf_op jit(solution)/shard_map/ppermute | solution.py:859
  391.2 0.2 fusion
  391.5 0.0 copy-start.1
  391.5 1.9 pad_maximum_fusion
  393.4 0.8 copy.50
  394.2 0.0 copy-done.9
  394.2 0.7 copy.51
  394.8 0.8 copy.52
  395.6 0.8 copy.53
  396.5 0.0 copy-done.1
  (54 shorter events, 0.2 us)
Async XLA Ops:
  0.6 7.1 %copy-start = (bf16[128,4608]{1,0:T(8,128)(2,1)S(1)}, bf16[128,4608]{1,0:T(8,128)(2,1)}, u32[]{:S(2)}) copy-start(bf16[128,4608]{1,0:T(8,128)(2,1)} %param.20) | copy-start | bytes 3538948
  0.7 3.1 copy-start.18
  0.7 7.0 %copy-start.12 = (f32[768]{0:T(1024)S(1)}, f32[768]{0:T(1024)}, u32[]{:S(2)}) copy-start(f32[768]{0:T(1024)} %param.22) | copy-start | bytes 9220
  0.7 7.0 %copy-start.13 = (f32[768]{0:T(1024)S(1)}, f32[768]{0:T(1024)}, u32[]{:S(2)}) copy-start(f32[768]{0:T(1024)} %param.25) | copy-start | bytes 9220
  0.7 7.7 %copy-start.11 = (f32[4608]{0:T(1024)S(1)}, f32[4608]{0:T(1024)}, u32[]{:S(2)}) copy-start(f32[4608]{0:T(1024)} %param.21) | copy-start | bytes 55300
  3.2 19.5 %collective-permute-start = (bf16[512,768]{1,0:T(8,128)(2,1)S(1)}, bf16[512,768]{1,0:T(8,128)(2,1)}, u32[]{:S(2)}, u32[]{:S(2)}) collective-permute-start(bf16[512,768]{1,0:T(8,128)(2,1)S(1)} %get-tuple-element.70), channel_id=1, source_target_pairs={{0,1},{1,0},{2,3},{3,2},{4,5},{5,4},{6,7},{7,6},{8,9},{9,8},{10,11... | collective-permute-start | bytes 2359304 | tf_op jit(solution)/shard_map/ppermute | solution.py:809
  8.5 6.0 %copy-start.16 = (f32[768]{0:T(1024)S(1)}, f32[768]{0:T(1024)}, u32[]{:S(2)}) copy-start(f32[768]{0:T(1024)} %param.29) | copy-start | bytes 9220
  8.5 6.0 %copy-start.19 = (s32[2]{0:T(128)S(1)}, s32[2]{0:T(128)}, u32[]{:S(2)}) copy-start(s32[2]{0:T(128)} %param.18) | copy-start | bytes 28
  8.5 6.6 %copy-start.20 = (s32[2]{0:T(128)S(1)}, s32[2]{0:T(128)}, u32[]{:S(2)}) copy-start(s32[2]{0:T(128)} %param.19) | copy-start | bytes 28
  8.5 11.1 %copy-start.8 = (bf16[2,512,768]{2,1,0:T(8,128)(2,1)S(1)}, bf16[2,512,768]{2,1,0:T(8,128)(2,1)}, u32[]{:S(2)}) copy-start(bf16[2,512,768]{2,1,0:T(8,128)(2,1)} %cot_ref.1) | copy-start | bytes 4718596
  165.4 13.0 %copy-start.15 = (f32[8,768]{1,0:T(8,128)S(1)}, f32[8,768]{1,0:T(8,128)}, u32[]{:S(2)}) copy-start(f32[8,768]{1,0:T(8,128)} %get-tuple-element.56) | copy-start | bytes 73732
  178.5 8.6 %copy-start.14 = (f32[1,3072]{1,0:T(1,128)S(1)}, f32[1,3072]{1,0:T(1,128)}, u32[]{:S(2)}) copy-start(f32[1,3072]{1,0:T(1,128)} %get-tuple-element.57) | copy-start | bytes 36868
  369.8 0.7 copy-start.10
  369.9 2.5 copy-start.17
  369.9 3.9 copy-start.3
  369.9 3.8 copy-start.4
  372.4 18.9 %collective-permute-start.1 = (bf16[512,768]{1,0:T(8,128)(2,1)S(1)}, bf16[512,768]{1,0:T(8,128)(2,1)S(1)}, u32[]{:S(2)}, u32[]{:S(2)}) collective-permute-start(bf16[512,768]{1,0:T(8,128)(2,1)S(1)} %copy-done.17), channel_id=1, source_target_pairs={{0,1},{1,0},{2,3},{3,2},{4,5},{5,4},{6,7},{7,6},{8,9},{9,8},{10,11... | collective-permute-start | bytes 2359304 | tf_op jit(solution)/shard_map/ppermute | solution.py:859
  373.8 17.4 %copy-start.2 = (f32[512,768]{1,0:T(8,128)S(1)}, f32[512,768]{1,0:T(8,128)}, u32[]{:S(2)}) copy-start(f32[512,768]{1,0:T(8,128)} %get-tuple-element.49) | copy-start | bytes 4718596
  391.5 1.9 copy-start.7
  391.5 2.7 copy-start.9
  391.5 5.0 %copy-start.1 = (bf16[128,4608]{1,0:T(8,128)(2,1)S(1)}, bf16[128,4608]{1,0:T(8,128)(2,1)}, u32[]{:S(2)}) copy-start(bf16[128,4608]{1,0:T(8,128)(2,1)} %param.20) | copy-start | bytes 3538948
  393.4 1.4 copy-start.6
  393.4 2.2 copy-start.5

commit v3 on v1

--- a/solution.py
+++ b/solution.py
@@ -46,13 +46,146 @@
     return pl.ds(pl.multiple_of(index * size, size), size)
 
 
-def params(mib=56):
-    return pltpu.CompilerParams(vmem_limit_bytes=mib * MIB)
+def params(mib=56, collective_id=None):
+    if collective_id is None:
+        return pltpu.CompilerParams(vmem_limit_bytes=mib * MIB)
+    return pltpu.CompilerParams(
+        vmem_limit_bytes=mib * MIB, collective_id=collective_id, has_side_effects=True
+    )
 
 
 def whole(shape):
     zeros = (0,) * len(shape)
     return pl.BlockSpec(shape, lambda *_: zeros)
+
+
+MESH = pl.DeviceIdType.MESH
+ANY = pl.BlockSpec(memory_space=pl.ANY)
+SEMS = [pltpu.SemaphoreType.DMA, pltpu.SemaphoreType.DMA]
+
+
+def greet(*partners):
+    barrier = pltpu.get_barrier_semaphore()
+    for partner in partners:
+        pl.semaphore_signal(barrier, inc=1, device_id=partner, device_id_type=MESH)
+    pl.semaphore_wait(barrier, len(partners))
+
+
+def remote(src, dst, send, recv, device):
+    return pltpu.make_async_remote_copy(
+        src_ref=src, dst_ref=dst, send_sem=send, recv_sem=recv, device_id=device, device_id_type=MESH
+    )
+
+
+def seq_partner():
+    return (lax.axis_index("dp"), 1 - lax.axis_index("seq"))
+
+
+def swap_start(src, dst, send, recv):
+    partner = seq_partner()
+    greet(partner)
+    remote(src, dst, send, recv, partner).start()
+
+
+def swap_wait(src, dst, send, recv):
+    remote(src, dst, send, recv, seq_partner()).wait()
+
+
+class Links:
+    def __init__(self, sems, zs):
+        self.sems, self.used, self.zs = sems, 0, zs
+        dp, self.x = lax.axis_index("dp"), lax.axis_index("seq")
+        self.z, self.y, self.c = dp // 4, lax.rem(dp // 2, 2), lax.rem(dp, 2)
+        self.core = (dp + 1 - 2 * self.c, self.x)
+        self.across = (dp + 2 - 4 * self.y, self.x)
+        self.facing = (dp, 1 - self.x)
+        self.far = [lax.rem(self.z + k, zs) for k in range(1, zs)]
+
+    def at_z(self, f):
+        return (f * 4 + 2 * self.y + self.c, self.x)
+
+    def take(self, count):
+        self.used += count
+        return self.used - count
+
+    def local(self, src, dst):
+        sem = self.take(1)
+        return lambda: pltpu.make_async_copy(src(), dst(), self.sems.at[sem])
+
+    def swap(self, src, dst, device):
+        sem = self.take(2)
+        return lambda: remote(src(), dst(), self.sems.at[sem], self.sems.at[sem + 1], device)
+
+    def spread(self, src, dst):
+        sem = self.take(2 * self.zs)
+
+        def make(f, slot):
+            return remote(
+                src(f), dst(slot), self.sems.at[sem + f], self.sems.at[sem + self.zs + slot], self.at_z(f)
+            )
+
+        def start():
+            for f in self.far:
+                make(f, self.z).start()
+
+        def wait():
+            for f in self.far:
+                make(f, self.z).wait_send()
+                make(f, f).wait_recv()
+
+        return start, wait
+
+    def gather(self, src, dst, goal):
+        sem = self.take(1 + self.zs)
+
+        def make(slot):
+            return remote(
+                src(), dst(slot), self.sems.at[sem], self.sems.at[sem + 1 + slot], self.at_z(goal)
+            )
+
+        def start():
+            pl.when(self.z != goal)(lambda: make(self.z).start())
+
+        def wait():
+            pl.when(self.z != goal)(lambda: make(self.z).wait_send())
+
+            @pl.when(self.z == goal)
+            def _():
+                for f in self.far:
+                    make(f).wait_recv()
+
+        return start, wait
+
+
+def add_to(dst, src, lead):
+    for index in lead:
+        dst[index] = dst[index] + src[index]
+
+
+def grid_of(*sizes):
+    return [()] if not sizes else [(i,) + r for i in range(sizes[0]) for r in grid_of(*sizes[1:])]
+
+
+def round_up(value, unit):
+    return -(-value // unit) * unit
+
+
+def early_mod_rows(width):
+    return round_up(4 * width // 128 + 1, 16)
+
+
+def early_sum_rows(width, ff):
+    return round_up((2 * width + ff) // 128, 8)
+
+
+def put_rows(ref, start, row):
+    for k in range(row.shape[1] // 128):
+        ref[start + k : start + k + 1, :] = row[:, k * 128 : (k + 1) * 128].astype(ref.dtype)
+
+
+def once(shape):
+    zeros = (0,) * len(shape)
+    return pl.BlockSpec(shape, lambda *_: zeros, pipeline_mode=pl.Buffered(1))
 
 
 def project_kernel(own_ref, rem_ref, vec_ref, cos_ref, sin_ref, w_ref, act_ref, out_ref):
@@ -122,7 +255,16 @@
     )(own, rem, vec, cos_t, sin_t, w_qkv_t)
 
 
-def attend_kernel(q_ref, k_ref, v_ref, att_ref, e_ref, linv_ref, q_mask, v_ext):
+def attend_kernel(
+    q_ref, k_ref, v_ref, cot_ref, att_ref, e_ref, linv_ref, cot_rem, q_mask, v_ext, send, recv
+):
+    step = pl.program_id(0)
+    cot_send = cot_ref.at[1 - lax.axis_index("seq")]
+
+    @pl.when(step == 0)
+    def _():
+        swap_start(cot_send, cot_rem, send, recv)
+
     tokens = q_ref.shape[1]
     tile = 256
     zero = jnp.zeros((HD, tokens), BF)
@@ -146,8 +288,12 @@
             linv_ref[0, h : h + 1, cols] = linv
             att_ref[h * HD : (h + 1) * HD, cols] = (mix[0:HD, :] * linv).astype(BF)
 
-
-def attend(qkv_t):
+    @pl.when(step == pl.num_programs(0) - 1)
+    def _():
+        swap_wait(cot_send, cot_rem, send, recv)
+
+
+def attend(qkv_t, cotangent):
     tokens = qkv_t.shape[1]
     width = HEADS * HD
 
@@ -157,29 +303,32 @@
     return pl.pallas_call(
         attend_kernel,
         grid=(PAIRS,),
-        in_specs=[part(0), part(1), part(2)],
+        in_specs=[part(0), part(1), part(2), ANY],
         out_specs=[
             part(0),
             pl.BlockSpec((2, tokens, tokens), lambda i: (i, 0, 0)),
             pl.BlockSpec((1, 8, tokens), lambda i: (i, 0, 0)),
+            ANY,
         ],
         out_shape=[
             jax.ShapeDtypeStruct((width, tokens), BF),
             jax.ShapeDtypeStruct((HEADS, tokens, tokens), BF),
             jax.ShapeDtypeStruct((PAIRS, 8, tokens), F32),
+            jax.ShapeDtypeStruct(cotangent.shape[1:], BF),
         ],
         scratch_shapes=[
             pltpu.VMEM((2, 2 * HD, tokens), BF),
             pltpu.VMEM((2, HD + 16, tokens), BF),
-        ],
-        compiler_params=params(),
+        ]
+        + SEMS,
+        compiler_params=params(collective_id=1),
         cost_estimate=pl.CostEstimate(
             flops=16 * tokens * tokens * width,
             bytes_accessed=30 << 20,
             transcendentals=HEADS * tokens * tokens,
         ),
         name="attend",
-    )(qkv_t, qkv_t, qkv_t)
+    )(qkv_t, qkv_t, qkv_t, cotangent)
 
 
 def gelu_both(u):
@@ -367,9 +516,271 @@
     )(att_t, tok_own, tok_rem, cot_own, cot_rem, span, vec, b_up, w_out, w_up, w_down)
 
 
+def middle_links_kernel(
+    zs,
+    att_ref,
+    tok_own,
+    tok_rem,
+    cot_own,
+    cot_rem,
+    span_ref,
+    vec_ref,
+    b_up_ref,
+    w_out_ref,
+    w_up_ref,
+    w_down_ref,
+    out_own,
+    out_rem,
+    dx_ref,
+    d_att_ref,
+    g_out_ref,
+    g_up_ref,
+    g_down_ref,
+    up_ref,
+    down_ref,
+    mod_ref,
+    sum_ref,
+    branch,
+    x_one,
+    act_two,
+    d_down,
+    down_acc,
+    d_act,
+    d_branch,
+    hidden,
+    d_up,
+    up_core,
+    up_side,
+    down_core,
+    down_y,
+    sems,
+):
+    step = pl.program_id(0)
+    steps = zs
+    tokens = att_ref.shape[1]
+    width = att_ref.shape[0]
+    half = tokens // 2
+    cut = width // 2
+    tile = 256
+    per_half = half // tile
+    gate_one = vec_ref[0:1, :]
+    mult_two = vec_ref[1:2, :]
+    shift_two = vec_ref[2:3, :]
+    gate_two = vec_ref[3:4, :]
+    b_down = vec_ref[4:5, :]
+    gain_two = vec_ref[5:6, :]
+    scale_two = vec_ref[6:7, :]
+
+    links = Links(sems, zs)
+    x, y, c = links.x, links.y, links.c
+    up_to_core = [
+        links.swap(lambda: g_up_ref.at[:, :, :, 1 - c], lambda j=j: up_core.at[j], links.core)
+        for j in range(steps - 1)
+    ]
+    down_to_core = [
+        links.swap(lambda: g_down_ref.at[:, 1 - c], lambda j=j: down_core.at[j], links.core)
+        for j in range(steps - 1)
+    ]
+    up_to_side = [
+        links.swap(lambda j=j: up_core.at[j, 1 - x], lambda j=j: up_side.at[j], links.facing)
+        for j in range(steps - 1)
+    ]
+    down_to_y = [
+        links.swap(lambda j=j: down_core.at[j, 1 - y], lambda j=j: down_y.at[j], links.across)
+        for j in range(steps - 1)
+    ]
+
+    @pl.when(step == 0)
+    def _():
+        greet(links.core, links.across, links.facing)
+        for part, (tok, cot) in enumerate(((tok_own, cot_own), (tok_rem, cot_rem))):
+            for t in range(per_half):
+                src = slice(t * tile, (t + 1) * tile)
+                dst = slice(part * half + t * tile, part * half + (t + 1) * tile)
+                br = mm(att_ref[:, dst], w_out_ref[...], TN)
+                branch[dst, :] = br
+                xv = tok[src, :].astype(F32) + gate_one * br
+                x_one[dst, :] = xv
+                n, _ = norm_parts(xv)
+                act_two[dst, :] = (n * mult_two + shift_two).astype(BF)
+                grad_out = cot[src, :].astype(F32) * span_ref[dst, :]
+                d_down[dst, :] = (gate_two * grad_out).astype(BF)
+                down_acc[dst, :] = jnp.zeros((tile, width), F32)
+                d_act[dst, :] = jnp.zeros((tile, width), F32)
+
+    bup = jnp.zeros((1, w_up_ref.shape[1]), F32)
+    for part in range(2):
+        rows = slice(part * half, (part + 1) * half)
+        up = mm(act_two[rows, :], w_up_ref[...]) + b_up_ref[...]
+        value, slope = gelu_both(up)
+        hidden[rows, :] = value.astype(BF)
+        d_up_low = (slope * mm(d_down[rows, :], w_down_ref[...], NT)).astype(BF)
+        bup += col_sum(d_up_low.astype(F32))
+        d_up[rows, :] = d_up_low
+    for j in range(steps):
+        pl.when(step == j)(lambda j=j: put_rows(sum_ref, 2 * width // 128 + j * bup.shape[1] // 128, bup))
+
+    for j in range(steps - 1):
+
+        @pl.when(step == j + 1)
+        def _(j=j):
+            up_to_core[j]().wait()
+            for h, a, b in grid_of(2, zs, 2):
+                up_core[j, h, a, b] = up_core[j, h, a, b] + g_up_ref[h, a, b, c]
+            up_to_side[j]().start()
+            down_to_core[j]().wait()
+            for b in range(2):
+                down_core[j, b] = down_core[j, b] + g_down_ref[b, c]
+            down_to_y[j]().start()
+
+    down_acc[...] += mm(hidden[...], w_down_ref[...])
+    d_act[...] += mm(d_up[...], w_up_ref[...], NT)
+    g_down = mm(hidden[...], d_down[...], TN).astype(BF)
+    g_down_ref[...] = g_down.reshape(g_down_ref.shape)
+    g_up = mm(act_two[...], d_up[...], TN).astype(BF)
+    for h in range(2):
+        g_up_ref[h] = g_up[:, h * cut : (h + 1) * cut].reshape(g_up_ref.shape[1:])
+
+    for j in range(steps - 1):
+
+        @pl.when(step == j)
+        def _(j=j):
+            up_to_core[j]().start()
+            down_to_core[j]().start()
+
+    @pl.when(step == steps - 1)
+    def _():
+        zero = jnp.zeros((1, width), F32)
+        s_gate_two, s_shift, s_pull, s_gate_one, s_bdown = zero, zero, zero, zero, zero
+        for part, (cot, out) in enumerate(((cot_own, out_own), (cot_rem, out_rem))):
+            for t in range(per_half):
+                src = slice(t * tile, (t + 1) * tile)
+                dst = slice(part * half + t * tile, part * half + (t + 1) * tile)
+                xv = x_one[dst, :]
+                down = down_acc[dst, :] + b_down
+                out[src, :] = (xv + gate_two * down).astype(BF)
+                grad_out = cot[src, :].astype(F32) * span_ref[dst, :]
+                s_gate_two += col_sum(grad_out * down)
+                s_bdown += col_sum(d_down[dst, :].astype(F32))
+                n, rstd = norm_parts(xv)
+                da = d_act[dst, :]
+                s_shift += col_sum(da)
+                s_pull += col_sum(da * n)
+                dx = grad_out + norm_pull(n, rstd, da * mult_two)
+                dx_ref[dst, :] = dx
+                s_gate_one += col_sum(dx * branch[dst, :])
+                d_branch[dst, :] = (gate_one * dx).astype(BF)
+        lines = width // 128
+        mod_ref[4 * lines :, :] = jnp.zeros((mod_ref.shape[0] - 4 * lines, 128), BF)
+        for k, row in enumerate((s_gate_one, s_shift, s_pull * gain_two, s_gate_two)):
+            put_rows(mod_ref, k * lines, row)
+        put_rows(mod_ref, 4 * lines, vec_ref[7:8, 0:128])
+        put_rows(sum_ref, 0, s_pull * (1.0 + scale_two))
+        put_rows(sum_ref, lines, s_bdown)
+        g_out = mm(att_ref[...], d_branch[...]).astype(BF)
+        for h in range(2):
+            g_out_ref[h] = g_out[:, h * cut : (h + 1) * cut].reshape(g_out_ref.shape[1:])
+        d_att_ref[...] = mm(w_out_ref[...], d_branch[...], NT).astype(BF)
+        for j in range(steps - 1):
+            up_to_side[j]().wait()
+            for a, b in grid_of(zs, 2):
+                up_ref[j, a, b] = up_core[j, x, a, b] + up_side[j, a, b]
+            down_to_y[j]().wait()
+            down_ref[j] = down_core[j, y] + down_y[j]
+
+
+def middle_links(
+    att_t, tok_own, tok_rem, cot_own, cot_rem, span, vec, b_up, w_out, w_up, w_down, zs
+):
+    width, tokens = att_t.shape
+    half = tokens // 2
+    cut = width // 2
+    ff = w_up.shape[1]
+    tile = ff // zs
+    rows = width // (4 * zs)
+    down_rows = tile // 4
+    halves = (2, zs, 2, 2, rows, cut)
+    owned = (2, 2, down_rows, width)
+    outs = [
+        ((half, width), BF),
+        ((half, width), BF),
+        ((tokens, width), F32),
+        ((width, tokens), BF),
+        (halves, BF),
+        (halves, BF),
+        (owned, BF),
+        ((zs - 1, zs, 2, rows, cut), BF),
+        ((zs - 1, down_rows, width), BF),
+        ((early_mod_rows(width), 128), BF),
+        ((early_sum_rows(width, ff), 128), F32),
+    ]
+    return pl.pallas_call(
+        functools.partial(middle_links_kernel, zs),
+        grid=(zs,),
+        in_specs=[
+            once(att_t.shape),
+            once(tok_own.shape),
+            once(tok_rem.shape),
+            once(cot_own.shape),
+            once(cot_rem.shape),
+            once(span.shape),
+            once(vec.shape),
+            pl.BlockSpec((1, tile), lambda i: (0, i)),
+            once(w_out.shape),
+            pl.BlockSpec((width, tile), lambda i: (0, i)),
+            pl.BlockSpec((tile, width), lambda i: (i, 0)),
+        ],
+        out_specs=[once(shape) for shape, _ in outs],
+        out_shape=[jax.ShapeDtypeStruct(*o) for o in outs],
+        scratch_shapes=[
+            pltpu.VMEM((tokens, width), F32),
+            pltpu.VMEM((tokens, width), F32),
+            pltpu.VMEM((tokens, width), BF),
+            pltpu.VMEM((tokens, width), BF),
+            pltpu.VMEM((tokens, width), F32),
+            pltpu.VMEM((tokens, width), F32),
+            pltpu.VMEM((tokens, width), BF),
+            pltpu.VMEM((tokens, tile), BF),
+            pltpu.VMEM((tokens, tile), BF),
+            pltpu.VMEM((zs - 1, 2, zs, 2, rows, cut), BF),
+            pltpu.VMEM((zs - 1, zs, 2, rows, cut), BF),
+            pltpu.VMEM((zs - 1, 2, down_rows, width), BF),
+            pltpu.VMEM((zs - 1, down_rows, width), BF),
+            pltpu.SemaphoreType.DMA((8 * (zs - 1),)),
+        ],
+        compiler_params=params(62, collective_id=4),
+        cost_estimate=pl.CostEstimate(
+            flops=12 * tokens * width * ff + 6 * tokens * width * width,
+            bytes_accessed=40 << 20,
+            transcendentals=tokens * ff,
+        ),
+        name="middle_links",
+    )(att_t, tok_own, tok_rem, cot_own, cot_rem, span, vec, b_up, w_out, w_up, w_down)
+
+
 def attend_back_kernel(
-    q_ref, k_ref, v_ref, att_ref, d_att_ref, e_ref, linv_ref, cos_ref, sin_ref, out_ref, do_mask
+    q_ref,
+    k_ref,
+    v_ref,
+    att_ref,
+    d_att_ref,
+    e_ref,
+    linv_ref,
+    cos_ref,
+    sin_ref,
+    give_ref,
+    out_ref,
+    take_ref,
+    do_mask,
+    send,
+    recv,
 ):
+    step = pl.program_id(0)
+
+    @pl.when(step == 0)
+    def _():
+        swap_start(give_ref, take_ref, send, recv)
+
     tokens = q_ref.shape[1]
     tile = 256
     zero = jnp.zeros((HD, tokens), BF)
@@ -408,8 +819,12 @@
         out_ref[1, h * HD : h * HD + HD // 2, :] = lead.astype(BF)
         out_ref[1, h * HD + HD // 2 : (h + 1) * HD, :] = trail.astype(BF)
 
-
-def attend_back(qkv_t, att_t, d_att_t, e, linv, cos_t, sin_t):
+    @pl.when(step == pl.num_programs(0) - 1)
+    def _():
+        swap_wait(give_ref, take_ref, send, recv)
+
+
+def attend_back(qkv_t, att_t, d_att_t, e, linv, cos_t, sin_t, give):
     tokens = qkv_t.shape[1]
     width = HEADS * HD
 
@@ -429,16 +844,20 @@
             pl.BlockSpec((1, 8, tokens), lambda i: (i, 0, 0)),
             whole(cos_t.shape),
             whole(sin_t.shape),
+            ANY,
         ],
-        out_specs=pl.BlockSpec((3, 2 * HD, tokens), lambda i: (0, i, 0)),
-        out_shape=jax.ShapeDtypeStruct((3, width, tokens), BF),
-        scratch_shapes=[pltpu.VMEM((2, 2 * HD, tokens), BF)],
-        compiler_params=params(),
+        out_specs=[pl.BlockSpec((3, 2 * HD, tokens), lambda i: (0, i, 0)), ANY],
+        out_shape=[
+            jax.ShapeDtypeStruct((3, width, tokens), BF),
+            jax.ShapeDtypeStruct(give.shape, give.dtype),
+        ],
+        scratch_shapes=[pltpu.VMEM((2, 2 * HD, tokens), BF)] + SEMS,
+        compiler_params=params(collective_id=2),
         cost_estimate=pl.CostEstimate(
             flops=32 * tokens * tokens * width, bytes_accessed=36 << 20, transcendentals=0
         ),
         name="attend_back",
-    )(qkv_t, qkv_t, qkv_t, att_t, d_att_t, e, linv, cos_t, sin_t)
+    )(qkv_t, qkv_t, qkv_t, att_t, d_att_t, e, linv, cos_t, sin_t, give)
 
 
 def tail_kernel(tok_own, tok_rem, d_proj_ref, w_ref, dx_ref, vec_ref, own_ref, rem_ref, sums_ref):
@@ -521,6 +940,568 @@
     )(act_t, d_proj_t)
 
 
+def gather_stages(links, ref):
+    z, y, c, x = links.z, links.y, links.c, links.x
+
+    def pair(mine, theirs, device):
+        sem = links.take(2)
+
+        def make(slot):
+            return remote(slot(), slot(), links.sems.at[sem], links.sems.at[sem + 1], device)
+
+        def wait():
+            make(mine).wait_send()
+            make(theirs).wait_recv()
+
+        return (lambda: make(mine).start()), wait
+
+    sem = links.take(2 * links.zs)
+
+    def make(f, slot):
+        block = ref.at[slot, :, :, x]
+        return remote(
+            block, block, links.sems.at[sem + f], links.sems.at[sem + links.zs + slot], links.at_z(f)
+        )
+
+    def far_start():
+        for f in links.far:
+            make(f, z).start()
+
+    def far_wait():
+        for f in links.far:
+            make(f, z).wait_send()
+            make(f, f).wait_recv()
+
+    return [
+        pair(lambda: ref.at[z, y, c, x], lambda: ref.at[z, y, 1 - c, x], links.core),
+        pair(lambda: ref.at[z, y, :, x], lambda: ref.at[z, 1 - y, :, x], links.across),
+        (far_start, far_wait),
+        pair(lambda: ref.at[:, :, :, x], lambda: ref.at[:, :, :, 1 - x], links.facing),
+    ]
+
+
+def sum_stages(links, ref, take, far):
+    swaps = [
+        links.swap(lambda: ref, lambda k=k: take.at[k], device)
+        for k, device in enumerate((links.core, links.across, links.facing))
+    ]
+    far_start, far_wait = links.spread(lambda f: ref, lambda slot: far.at[slot])
+
+    def finish(k):
+        swaps[k]().wait()
+        ref[...] += take[k]
+
+    def far_finish():
+        far_wait()
+        far[links.z] = ref[...]
+        total = far[0]
+        for f in range(1, links.zs):
+            total += far[f]
+        ref[...] = total
+
+    return [
+        (lambda: swaps[0]().start(), lambda: finish(0)),
+        (lambda: swaps[1]().start(), lambda: finish(1)),
+        (far_start, far_finish),
+        (lambda: swaps[2]().start(), lambda: finish(2)),
+    ]
+
+
+def back_kernel(zs, split, ins, outs, scratch):
+    (
+        q_ref,
+        k_ref,
+        v_ref,
+        att_ref,
+        d_att_ref,
+        e_ref,
+        linv_ref,
+        cos_ref,
+        sin_ref,
+        own_ref,
+        give_ref,
+        up_ref,
+        down_ref,
+        raw_up,
+        raw_out,
+        raw_down,
+        mod_ref,
+        sum_ref,
+        act_ref,
+        w_ref,
+        tok_own,
+        tok_rem,
+        dx_ref,
+        vec_ref,
+    ) = ins
+    result, grad_ref, s_qkv, s_out, s_up, s_down, *small_outs = outs
+    (
+        do_mask,
+        d_proj,
+        sems,
+        u_own,
+        u_core,
+        u_side,
+        u_sum,
+        u_y,
+        u_z,
+        u_last,
+        u_facing,
+        d_own,
+        d_core,
+        d_y,
+        d_sum,
+        d_z,
+        d_last,
+        d_facing,
+        q_raws,
+        q_cores,
+        q_ys,
+        q_zs,
+        q_lasts,
+        q_facings,
+        g_send,
+        g_take,
+        early_take,
+        early_far,
+        late_take,
+        late_far,
+        mod_early,
+        mod_late,
+        sum_early,
+        sum_late,
+    ) = scratch
+    step = pl.program_id(0)
+    tokens = q_ref.shape[1]
+    width = act_ref.shape[0]
+    half = tokens // 2
+    cut = width // 2
+    pieces = zs + 1
+    links = Links(sems, zs)
+    x, y, z, c = links.x, links.y, links.z, links.c
+
+    def at(k):
+        return pl.when(step == k)
+
+    raws = (raw_up, raw_out)
+    u_keep = [links.local(lambda r=r: r.at[:, :, :, c], lambda k=k: u_own.at[k]) for k, r in enumerate(raws)]
+    u_to_core = [
+        links.swap(lambda r=r: r.at[:, :, :, 1 - c], lambda k=k: u_core.at[k], links.core)
+        for k, r in enumerate(raws)
+    ]
+    u_to_side = [
+        links.swap(lambda k=k: u_own.at[k, 1 - x], lambda k=k: u_side.at[k], links.facing)
+        for k in range(2)
+    ]
+    u_load = [links.local(lambda j=j: up_ref.at[j, :, y], lambda j=j: u_sum.at[j, :, y]) for j in range(zs - 1)]
+
+    def u_y_src(j):
+        if j < zs - 1:
+            return up_ref.at[j, :, 1 - y]
+        return u_sum.at[j, :, 1 - y]
+
+    u_to_y = [
+        links.swap(lambda j=j: u_y_src(j), lambda j=j: u_y.at[j], links.across) for j in range(pieces)
+    ]
+    u_far = [
+        links.spread(lambda f, j=j: u_sum.at[j, f, y], lambda slot, j=j: u_z.at[j, slot])
+        for j in range(pieces)
+    ]
+    u_to_facing = [
+        links.swap(lambda j=j: u_last.at[j], lambda j=j: u_facing.at[j], links.facing)
+        for j in range(pieces)
+    ]
+    d_keep = links.local(lambda: raw_down.at[:, c], lambda: d_own)
+    d_to_core = links.swap(lambda: raw_down.at[:, 1 - c], lambda: d_core, links.core)
+    d_to_y = links.swap(lambda: d_own.at[1 - y], lambda: d_y, links.across)
+    d_load = links.local(lambda: down_ref, lambda: d_sum.at[0 : zs - 1])
+    d_far = [
+        links.gather(
+            lambda j=j: down_ref.at[j] if j < zs - 1 else d_sum.at[j], lambda slot: d_z.at[slot], j
+        )
+        for j in range(zs)
+    ]
+    d_to_facing = links.swap(lambda: d_last, lambda: d_facing, links.facing)
+    groups = range(len(split))
+    q_to_core = [
+        links.swap(lambda g=g: q_raws[g].at[:, :, 1 - c], lambda g=g: q_cores[g], links.core)
+        for g in groups
+    ]
+    q_to_y = [
+        links.swap(lambda g=g: q_cores[g].at[:, 1 - y], lambda g=g: q_ys[g], links.across)
+        for g in groups
+    ]
+    q_far = [
+        links.spread(lambda f, g=g: q_cores[g].at[f, y], lambda slot, g=g: q_zs[g].at[slot])
+        for g in groups
+    ]
+    q_to_facing = [
+        links.swap(lambda g=g: q_lasts[g], lambda g=g: q_facings[g], links.facing) for g in groups
+    ]
+    keep_out = links.local(lambda: own_ref, lambda: result.at[x])
+    out_sem = links.take(2)
+
+    def cross_out(slot):
+        return remote(give_ref, result.at[slot], sems.at[out_sem], sems.at[out_sem + 1], links.facing)
+
+    give_grad = links.swap(lambda: g_send, lambda: g_take, links.facing)
+    early = [
+        gather_stages(links, mod_early),
+        sum_stages(links, sum_early, early_take, early_far),
+    ]
+    late = [gather_stages(links, mod_late), sum_stages(links, sum_late, late_take, late_far)]
+
+    def begin(arrays, stage):
+        for stages in arrays:
+            stages[stage][0]()
+
+    def end(arrays, stage):
+        for stages in arrays:
+            stages[stage][1]()
+
+    def u_y_done(j):
+        u_to_y[j]().wait()
+        for a in range(zs):
+            u_sum[j, a, y] = u_sum[j, a, y] + u_y[j, a]
+        u_far[j][0]()
+
+    def u_z_done(j):
+        u_far[j][1]()
+        total = u_sum[j, z, y].astype(F32)
+        for f in links.far:
+            total += u_z[j, f].astype(F32)
+        u_last[j] = total.astype(BF)
+        u_to_facing[j]().start()
+
+    def u_done(j):
+        u_to_facing[j]().wait()
+        mine, other = u_last[j].astype(F32), u_facing[j].astype(F32)
+        out, start = (s_up, j * width) if j < zs else (s_out, 0)
+        out[:, start : start + cut] = jnp.where(x == 0, mine, other)
+        out[:, start + cut : start + width] = jnp.where(x == 0, other, mine)
+
+    def q_core_done(g):
+        q_to_core[g]().wait()
+        for a, b in grid_of(zs, 2):
+            q_cores[g][a, b] = q_cores[g][a, b] + q_raws[g][a, b, c]
+        q_to_y[g]().start()
+
+    def q_y_done(g):
+        q_to_y[g]().wait()
+        for a in range(zs):
+            q_cores[g][a, y] = q_cores[g][a, y] + q_ys[g][a]
+        q_far[g][0]()
+
+    def q_z_done(g):
+        q_far[g][1]()
+        total = q_cores[g][z, y].astype(F32)
+        for f in links.far:
+            total += q_zs[g][f].astype(F32)
+        q_lasts[g][...] = total.astype(BF)
+        q_to_facing[g]().start()
+
+    def q_done(g):
+        q_to_facing[g]().wait()
+        total = q_lasts[g][...].astype(F32) + q_facings[g][...].astype(F32)
+        first, size = split[g][0] * HD, (split[g][1] - split[g][0]) * HD
+        for p in range(3):
+            s_qkv[:, p * width + first : p * width + first + size] = total[:, p * size : (p + 1) * size]
+
+    def weight_grad_of(g):
+        first, size = split[g][0] * HD, (split[g][1] - split[g][0]) * HD
+        for p in range(3):
+            rows = slice(p * width + first, p * width + first + size)
+            part = mm(act_ref[...], d_proj[rows, :], NT).astype(BF)
+            q_raws[g][:, :, :, :, p * size : (p + 1) * size] = part.reshape(
+                q_raws[g].shape[:4] + (size,)
+            )
+        q_to_core[g]().start()
+
+
+    @at(0)
+    def _():
+        greet(links.core, links.across, links.facing, *[links.at_z(f) for f in links.far])
+        for k in range(2):
+            u_to_core[k]().start()
+            u_keep[k]().start()
+        d_to_core().start()
+        d_keep().start()
+        d_load().start()
+        for j in range(zs - 1):
+            u_load[j]().start()
+            u_to_y[j]().start()
+            d_far[j][0]()
+        mod_early[z, y, c, x] = mod_ref[...]
+        sum_early[...] = sum_ref[...]
+        begin(early, 0)
+        keep_out().start()
+        cross_out(x).start()
+
+    @at(1)
+    def _():
+        for k in range(2):
+            u_keep[k]().wait()
+            u_to_core[k]().wait()
+            for h, a, b in grid_of(2, zs, 2):
+                u_own[k, h, a, b] = u_own[k, h, a, b] + u_core[k, h, a, b]
+            u_to_side[k]().start()
+        d_keep().wait()
+        d_to_core().wait()
+        for b in range(2):
+            d_own[b] = d_own[b] + d_core[b]
+        d_to_y().start()
+        end(early, 0)
+        begin(early, 1)
+
+    @at(2)
+    def _():
+        for j in range(zs - 1):
+            u_load[j]().wait()
+            u_y_done(j)
+        end(early, 1)
+        begin(early, 2)
+
+    @at(3)
+    def _():
+        d_to_y().wait()
+        d_sum[zs - 1] = d_own[y] + d_y[...]
+        d_far[zs - 1][0]()
+        end(early, 2)
+        begin(early, 3)
+
+    @at(4)
+    def _():
+        weight_grad_of(0)
+        for k in range(2):
+            u_to_side[k]().wait()
+            for a, b in grid_of(zs, 2):
+                u_sum[zs - 1 + k, a, b] = u_own[k, x, a, b] + u_side[k, a, b]
+            u_to_y[zs - 1 + k]().start()
+        for j in range(zs - 1):
+            u_z_done(j)
+
+    @at(5)
+    def _():
+        q_core_done(0)
+        end(early, 3)
+        for k in range(2):
+            u_y_done(zs - 1 + k)
+        d_load().wait()
+        for j in range(zs):
+            d_far[j][1]()
+        total = d_sum[z].astype(F32)
+        for f in links.far:
+            total += d_z[f].astype(F32)
+        d_last[...] = total.astype(BF)
+        d_to_facing().start()
+
+
+    @pl.when(step < PAIRS)
+    def _():
+        tile = 256
+        zero = jnp.zeros((HD, tokens), BF)
+        v_nat = v_ref[...].T
+        cos = cos_ref[...]
+        sin = sin_ref[...]
+
+        def put(part, h, value):
+            low = value.astype(BF).astype(F32)
+            a, b = low[0 : HD // 2], low[HD // 2 :]
+            start = part * width + step * 2 * HD + h * HD
+            d_proj[pl.ds(pl.multiple_of(start, 32), 32), :] = (a * cos + b * sin).astype(BF)
+            d_proj[pl.ds(pl.multiple_of(start + 32, 32), 32), :] = (b * cos - a * sin).astype(BF)
+
+        for h in range(2):
+            rows = slice(h * HD, (h + 1) * HD)
+            linv = linv_ref[0, h : h + 1, :]
+            d_o = d_att_ref[rows, :].astype(F32)
+            d_os = (d_o * linv).astype(BF)
+            do_mask[h, rows, :] = d_os
+            do_mask[h, (1 - h) * HD : (2 - h) * HD, :] = zero
+            inner = col_sum(d_o * att_ref[rows, :].astype(F32)) * linv
+            d_values = mm(d_os, e_ref[h], NT)
+            start = 2 * width + step * 2 * HD + h * HD
+            d_proj[pl.ds(pl.multiple_of(start, HD), HD), :] = d_values.astype(BF)
+            d_keys = jnp.zeros((HD, tokens), F32)
+            d_queries = []
+            for t in range(tokens // tile):
+                cols = slice(t * tile, (t + 1) * tile)
+                d_probs = mm(v_nat, do_mask[h, :, cols])
+                d_s = (e_ref[h, :, cols].astype(F32) * (d_probs - inner[:, cols])).astype(BF)
+                d_queries.append(mm(k_ref[rows, :], d_s))
+                d_keys += mm(q_ref[rows, cols], d_s, NT)
+            put(0, h, jnp.concatenate(d_queries, axis=1) * HD**-0.5)
+            put(1, h, d_keys)
+
+
+    def finish(tok, cols):
+        d_act = mm(d_proj[:, cols], w_ref[...], TN)
+        n, rstd = norm_parts(tok[...].astype(F32))
+        grad = dx_ref[cols, :] + norm_pull(n, rstd, d_act * vec_ref[0:1, :])
+        return grad, col_sum(d_act), col_sum(d_act * n)
+
+    @at(PAIRS)
+    def _():
+        weight_grad_of(1)
+        for k in range(2):
+            u_z_done(zs - 1 + k)
+        q_y_done(0)
+        grad, shift, pull = finish(tok_rem, slice(half, 2 * half))
+        g_send[...] = grad.astype(BF)
+        give_grad().start()
+        q_core_done(1)
+        grad, shift_own, pull_own = finish(tok_own, slice(0, half))
+        grad_ref[x] = grad
+        shift += shift_own
+        pull += pull_own
+        lines = width // 128
+        mine = mod_late.at[z, y, c, x]
+        mine[2 * lines :, :] = jnp.zeros((mod_late.shape[4] - 2 * lines, 128), BF)
+        put_rows(mine, 0, shift)
+        put_rows(mine, lines, pull * vec_ref[2:3, :])
+        sum_late[lines:, :] = jnp.zeros((sum_late.shape[0] - lines, 128), F32)
+        put_rows(sum_late, 0, pull * (1.0 + vec_ref[3:4, :]))
+        begin(late, 0)
+        d_to_facing().wait()
+        s_down[...] = d_last[...].astype(F32) + d_facing[...].astype(F32)
+        end(late, 0)
+        begin(late, 1)
+        for j in range(pieces):
+            u_done(j)
+        q_z_done(0)
+        end(late, 1)
+        begin(late, 2)
+        q_y_done(1)
+        end(late, 2)
+        begin(late, 3)
+        keep_out().wait()
+        cross_out(x).wait_send()
+        cross_out(1 - x).wait_recv()
+        q_done(0)
+        q_z_done(1)
+        end(late, 3)
+        give_grad().wait()
+        grad_ref[1 - x] = g_take[...].astype(F32)
+        q_done(1)
+        for out, value in zip(small_outs, (mod_early, mod_late, sum_early, sum_late)):
+            out[...] = value[...]
+
+
+def back(ins, zs, ff):
+    (q, att, d_att, e, linv, cos_t, sin_t, own, give, up, down, raw_up, raw_out, raw_down) = ins[:14]
+    mod, sums, act_t, w_qkv_t, tok_own, tok_rem, dx, vec = ins[14:]
+    width, tokens = att.shape
+    half = tokens // 2
+    cut = width // 2
+    rows = width // (4 * zs)
+    down_rows = ff // (4 * zs)
+    pieces = zs + 1
+    split = ((0, 8), (8, HEADS))
+    sizes = [3 * (b - a) * HD for a, b in split]
+    last = PAIRS - 1
+
+    def part(k):
+        return pl.BlockSpec((2 * HD, tokens), lambda i: (jnp.minimum(i, last) + k * PAIRS, 0))
+
+    def vm(*shape, kind=BF):
+        return pltpu.VMEM(shape, kind)
+
+    lines = width // 128
+    mod_early = (zs, 2, 2, 2) + mod.shape
+    mod_late = (zs, 2, 2, 2, round_up(2 * lines, 16), 128)
+    sum_late = (round_up(lines, 8), 128)
+    outs = [
+        ((half, width), F32),
+        ((rows, 3 * width), F32),
+        ((rows, width), F32),
+        ((rows, ff), F32),
+        ((down_rows, width), F32),
+        (mod_early, BF),
+        (mod_late, BF),
+        (sums.shape, F32),
+        (sum_late, F32),
+    ]
+    outs[0] = ((2, half, width), F32)
+    in_specs = (
+        [part(0), part(1), part(2), part(0), part(0)]
+        + [
+            pl.BlockSpec((2, tokens, tokens), lambda i: (jnp.minimum(i, last), 0, 0)),
+            pl.BlockSpec((1, 8, tokens), lambda i: (jnp.minimum(i, last), 0, 0)),
+            once(cos_t.shape),
+            once(sin_t.shape),
+        ]
+        + [ANY] * 7
+        + [once(a.shape) for a in (mod, sums, act_t, w_qkv_t, tok_own, tok_rem, dx, vec)]
+    )
+    out_specs = [ANY] + [once(shape) for shape, _ in outs]
+    out_shape = [jax.ShapeDtypeStruct((2, half, width), BF)] + [
+        jax.ShapeDtypeStruct(*o) for o in outs
+    ]
+    scratch = [
+        vm(2, 2 * HD, tokens),
+        vm(3 * width, tokens),
+        pltpu.SemaphoreType.DMA((250,)),
+        vm(2, 2, zs, 2, rows, cut),
+        vm(2, 2, zs, 2, rows, cut),
+        vm(2, zs, 2, rows, cut),
+        vm(pieces, zs, 2, rows, cut),
+        vm(pieces, zs, rows, cut),
+        vm(pieces, zs, rows, cut),
+        vm(pieces, rows, cut),
+        vm(pieces, rows, cut),
+        vm(2, down_rows, width),
+        vm(2, down_rows, width),
+        vm(down_rows, width),
+        vm(zs, down_rows, width),
+        vm(zs, down_rows, width),
+        vm(down_rows, width),
+        vm(down_rows, width),
+        [vm(zs, 2, 2, rows, s) for s in sizes],
+        [vm(zs, 2, rows, s) for s in sizes],
+        [vm(zs, rows, s) for s in sizes],
+        [vm(zs, rows, s) for s in sizes],
+        [vm(rows, s) for s in sizes],
+        [vm(rows, s) for s in sizes],
+        vm(half, width),
+        vm(half, width),
+        vm(3, *sums.shape, kind=F32),
+        vm(zs, *sums.shape, kind=F32),
+        vm(3, *sum_late, kind=F32),
+        vm(zs, *sum_late, kind=F32),
+        vm(*mod_early),
+        vm(*mod_late),
+        vm(*sums.shape, kind=F32),
+        vm(*sum_late, kind=F32),
+    ]
+    flat, tree = jax.tree.flatten(scratch)
+    n_in, n_out = len(in_specs), len(out_specs)
+
+    def kernel(*refs):
+        back_kernel(
+            zs,
+            split,
+            refs[:n_in],
+            refs[n_in : n_in + n_out],
+            jax.tree.unflatten(tree, refs[n_in + n_out :]),
+        )
+
+    return pl.pallas_call(
+        kernel,
+        grid=(PAIRS + 1,),
+        in_specs=in_specs,
+        out_specs=out_specs,
+        out_shape=out_shape,
+        scratch_shapes=flat,
+        compiler_params=params(62, collective_id=5),
+        cost_estimate=pl.CostEstimate(
+            flops=32 * tokens * tokens * width + 12 * tokens * width * width,
+            bytes_accessed=60 << 20,
+            transcendentals=0,
+        ),
+        name="back",
+    )(q, q, q, att, d_att, e, linv, cos_t, sin_t, *ins[7:])
+
+
 def time_features(time_steps, pair_count):
     frequency = jnp.exp(-math.log(10000.0) * jnp.arange(pair_count, dtype=F32) / pair_count)
     angles = time_steps.astype(F32)[:, None] * frequency[None, :]
@@ -553,9 +1534,8 @@
         return lax.dynamic_index_in_dim(x, i, 0, keepdims=False)
 
     tok_own, tok_send = pick(tokens, rank), pick(tokens, 1 - rank)
-    cot_own, cot_send = pick(cotangent, rank), pick(cotangent, 1 - rank)
+    cot_own = pick(cotangent, rank)
     tok_rem = lax.ppermute(tok_send, "seq", swap)
-    cot_rem = lax.ppermute(cot_send, "seq", swap)
 
     here = jnp.arange(half, dtype=jnp.int32)
     place = jnp.concatenate([rank * half + here, (1 - rank) * half + here])
@@ -584,52 +1564,70 @@
             b_down,
             gain_two,
             scale_two,
-            zeros,
+            jnp.pad(jnp.concatenate([time_own // 32, time_own % 32]).astype(F32), (0, width - 2)),
         ]
     )
     w_qkv_t = w_qkv.T
 
+    dp, dps = lax.axis_index("dp"), lax.axis_size("dp")
+    ff = w_up.shape[1]
+    zs = dps // 4
+    linked = dps % 4 == 0 and width % (64 * zs) == 0 and ff == zs * width
+
     act_t, qkv_t = project(tok_own, tok_rem, vec_one, cos_t, sin_t, w_qkv_t)
-    att_t, e, linv = attend(qkv_t)
-    out_own, out_rem, dx, d_att_t, g_out, g_up, g_down, g_bup, sums_two = middle(
-        att_t, tok_own, tok_rem, cot_own, cot_rem, span, vec_two, b_up[None], w_out, w_up, w_down
-    )
-    d_proj = attend_back(qkv_t, att_t, d_att_t, e, linv, cos_t, sin_t)
-    d_proj_t = d_proj.reshape(3 * width, length)
-    g_own, g_rem, sums_one = tail(tok_own, tok_rem, d_proj_t, w_qkv_t, dx, vec_one)
-    g_qkv = weight_grad(act_t, d_proj_t)
-
-    def spread(own, other):
-        first = jnp.where(rank == 0, own, other)
-        second = jnp.where(rank == 0, other, own)
-        return jnp.stack([first, second])
-
-    output = spread(out_own, lax.ppermute(out_rem, "seq", swap))
-    grad_tokens = spread(g_own, lax.ppermute(g_rem, "seq", swap).astype(F32))
-
-    gate_sums = jnp.concatenate([sums_two[:6].reshape(-1), g_bup[0], time_own.astype(F32)])
-    early = lax.all_gather(gate_sums, ("dp", "seq"))
-    late = lax.all_gather(sums_one[:3].reshape(-1), ("dp", "seq"))
-    everyone = early[:, -1]
-    ff = w_up.shape[1]
-    features = jax.nn.silu(time_features(everyone, w_ada.shape[0] // 2))
-    d_mod = jnp.concatenate([late[:, : 2 * width], early[:, : 4 * width]], axis=1)
-    dp = lax.axis_index("dp")
+    att_t, e, linv, cot_rem = attend(qkv_t, cotangent)
+    if linked:
+        out_own, out_rem, dx, d_att_t, raw_out, raw_up, raw_down, up, down, mod, sums = middle_links(
+            att_t, tok_own, tok_rem, cot_own, cot_rem, span, vec_two, b_up[None], w_out, w_up, w_down, zs
+        )
+        ins = (qkv_t, att_t, d_att_t, e, linv, cos_t, sin_t, out_own, out_rem, up, down)
+        ins += (raw_up, raw_out, raw_down, mod, sums, act_t, w_qkv_t, tok_own, tok_rem, dx, vec_one)
+        output, grad_tokens, *shards, mod_early, mod_late, sum_early, sum_late = back(ins, zs, ff)
+        mod_early = mod_early.reshape(2 * dps, -1).astype(F32)
+        mod_late = mod_late.reshape(2 * dps, -1).astype(F32)
+        d_mod_all = jnp.concatenate([mod_late[:, : 2 * width], mod_early[:, : 4 * width]], axis=1)
+        time_all = 32.0 * mod_early[:, 4 * width] + mod_early[:, 4 * width + 1]
+        small = jnp.concatenate(
+            [sum_late.reshape(-1)[:width], sum_early.reshape(-1)[: 2 * width + ff]]
+        )
+    else:
+        out_own, out_rem, dx, d_att_t, g_out, g_up, g_down, g_bup, sums_two = middle(
+            att_t, tok_own, tok_rem, cot_own, cot_rem, span, vec_two, b_up[None], w_out, w_up, w_down
+        )
+        d_proj, out_back = attend_back(qkv_t, att_t, d_att_t, e, linv, cos_t, sin_t, out_rem)
+        d_proj_t = d_proj.reshape(3 * width, length)
+        g_own, g_rem, sums_one = tail(tok_own, tok_rem, d_proj_t, w_qkv_t, dx, vec_one)
+        g_qkv = weight_grad(act_t, d_proj_t)
+
+        def spread(own, other):
+            first = jnp.where(rank == 0, own, other)
+            second = jnp.where(rank == 0, other, own)
+            return jnp.stack([first, second])
+
+        output = spread(out_own, out_back)
+        grad_tokens = spread(g_own, lax.ppermute(g_rem, "seq", swap).astype(F32))
+        shards = [
+            lax.psum(lax.psum_scatter(g, "dp", scatter_dimension=0, tiled=True), "seq").astype(F32)
+            for g in (g_qkv, g_out, g_up, g_down)
+        ]
+        d_mod = jnp.concatenate([sums_one[:2].reshape(-1), sums_two[:4].reshape(-1)])
+        small = jnp.concatenate([sums_one[2], sums_two[4], sums_two[5], g_bup[0]])
+        d_mod_all = lax.all_gather(d_mod, ("dp", "seq"))
+        time_all = lax.all_gather(time_own[0].astype(F32), ("dp", "seq"))
+        small = lax.psum(small, ("dp", "seq"))
 
     def mine(x, axis=0):
-        size = x.shape[axis] // lax.axis_size("dp")
+        size = x.shape[axis] // dps
         return lax.dynamic_slice_in_dim(x, dp * size, size, axis)
 
-    s_w_ada = jnp.dot(mine(features, 1).T, d_mod, precision=lax.Precision.HIGHEST)
-    s_b_ada = jnp.sum(mine(d_mod, 1), axis=0)
-    s_gain_one = jnp.sum(mine(late[:, 2 * width :], 1), axis=0)
-    s_gain_two = jnp.sum(mine(early[:, 4 * width : 5 * width], 1), axis=0)
-    s_b_down = jnp.sum(mine(early[:, 5 * width : 6 * width], 1), axis=0)
-    s_b_up = jnp.sum(mine(early[:, 6 * width : 6 * width + ff], 1), axis=0)
-
-    def reduce_rows(g):
-        part = lax.psum_scatter(g, "dp", scatter_dimension=0, tiled=True)
-        return lax.psum(part, "seq").astype(F32)
+    features = jax.nn.silu(time_features(time_all, w_ada.shape[0] // 2))
+    s_w_ada = jnp.dot(mine(features, 1).T, d_mod_all, precision=lax.Precision.HIGHEST)
+    s_b_ada = jnp.sum(mine(d_mod_all, 1), axis=0)
+    s_gain_one = mine(small[:width])
+    s_gain_two = mine(small[width : 2 * width])
+    s_b_down = mine(small[2 * width : 3 * width])
+    s_b_up = mine(small[3 * width :])
+    s_qkv, s_out, s_up, s_down = shards
 
     return (
         output,
@@ -637,12 +1635,12 @@
         s_w_ada,
         s_b_ada,
         s_gain_one,
-        reduce_rows(g_qkv),
-        reduce_rows(g_out),
+        s_qkv,
+        s_out,
         s_gain_two,
-        reduce_rows(g_up),
+        s_up,
         s_b_up,
-        reduce_rows(g_down),
+        s_down,
         s_b_down,
     )
 

time: 483 us -> 269 us (0.56)
  waiting for transfers between devices: 204 us -> 0.01 us
  Pallas kernels: 159 us -> 230 us
  blocking collectives: 53.9 us -> 0 us
  other arithmetic: 19.9 us -> 3.8 us
  between operations: 17.4 us -> 5.77 us
  local copies, waits for them, and re-layouts: 17.7 us -> 24 us
  starting transfers between devices: 5.64 us -> 0.53 us
    reduce_scatter x4 -> x0, waiting for transfers between devices: 148 us -> none  [reduce_rows(): part = lax.psum_scatter(g, 'dp', scatter_dimension=0, tiled=True)]
    pallas_call x4 -> x2, Pallas kernels: 108 us -> 177 us  [the longest x1 113 us: back(): pl.pallas_call(kernel, grid=(PAIRS + 1,), in_specs=in_specs, out_specs=ou...]
    all_gather x1 -> x0, blocking collectives: 53.9 us -> none  [per_device(): late = lax.all_gather(sums_one[:3].reshape(-1), ('dp', 'seq'))]
    psum x1 -> x0, waiting for transfers between devices: 31.6 us -> none  [reduce_rows(): return lax.psum(part, 'seq').astype(F32)]
    unnamed x7 -> x0, waiting for transfers between devices: 22.1 us -> none
    unnamed x34 -> x49, local copies, waits for them, and re-layouts: 7.57 us -> 14.4 us
    another operation x4 -> x0, other arithmetic: 5.8 us -> none  [spread(): return jnp.stack([first, second])]
    convert_element_type x5 -> x1, other arithmetic: 5.72 us -> 0.08 us  [per_device(): jnp.concatenate([time_own // 32, time_own % 32]).astype(F32)]
  transfers between devices with their start and end apart: 10 -> 1, of which waited for: 5 -> 0; matrix products, arithmetic and copies ran while one was open for 6% -> 5% of each run, Pallas kernels for 23% -> 0%
where the time goes in v3:
time: 269 us; the launch traced here: 266 us
  Pallas kernels  230 us (86%)
  local copies, waits for them, and re-layouts  24 us (9%)
  between operations  5.77 us (2%)
  other arithmetic  3.8 us (1%)
    pallas_call x1, Pallas kernels, back(): pl.pallas_call(kernel, grid=(PAIRS + 1,), in_specs=in_specs, out_specs=ou...  113 us
    pallas_call x1, Pallas kernels, middle_links(): pl.pallas_call(functools.partial(middle_links_kernel, zs), grid=(zs,), in...  64.7 us
    pallas_call x1, Pallas kernels, attend(): pl.pallas_call(attend_kernel, grid=(PAIRS,), in_specs=[part(0), part(1),...  41.7 us
    unnamed x49, local copies, waits for them, and re-layouts  14.4 us
    pallas_call x1, Pallas kernels, project(): pl.pallas_call(project_kernel, grid=(6,), in_specs=[whole(own.shape), who...  11.1 us
  transfers between devices with their start and end apart: 1, of which 0 were waited for; matrix products, arithmetic and copies ran while one was open for 5% of the time, Pallas kernels for 0%

profile of v3, /device:TPU:10, one launch (start us, length us, event | category | flops | bytes accessed | tf_op | source)
XLA Modules:
  0.0 266.2 jit_solution(2209705028703327538)
XLA Ops:
  0.6 0.0 copy-start
  0.7 0.0 copy-start.16
  0.7 0.0 copy-start.12
  0.7 0.0 copy-start.13
  0.7 0.0 copy-start.11
  0.7 2.4 dynamic-slice_bitcast_fusion.1
  3.2 0.5 collective-permute-start
  3.7 0.0 copy-done.16
  3.7 0.6 dynamic_slice.40
  7.6 0.0 copy-done.12
  7.6 0.0 copy-done.13
  7.6 0.0 copy-done
  7.6 0.7 convolution_reduce_fusion
  8.3 0.0 copy-done.11
  8.4 0.0 copy-start.14
  8.4 0.0 copy-start.17
  8.4 0.0 copy-start.18
  8.4 0.0 copy-start.7
  8.4 5.9 %copy.42 = bf16[768,2304]{0,1:T(8,128)(2,1)} copy(bf16[768,2304]{1,0:T(8,128)(2,1)} %param.23) | data formatting | bytes 7077888 | tf_op args[8]
  14.3 0.1 add_convert_fusion.1
  14.5 0.0 copy-done.14
  14.5 0.0 copy-done.17
  14.5 0.6 dynamic_slice.42
  15.1 0.0 copy-done.18
  15.1 0.6 dynamic_slice.43
  17.0 0.7 broadcast_compare_fusion
  17.6 0.3 copy.43
  17.9 0.3 copy.44
  18.2 0.6 stack.50.vec_ref.refs_23_
  18.9 0.6 stack.59.vec_ref
  19.5 0.0 copy-done.7
  19.6 1.0 dynamic-slice_bitcast_fusion.cot_own
  20.5 1.2 multiply_sine_fusion
  21.8 0.9 and_select_fusion.span_ref
  22.7 0.0 collective-permute-done.rem_ref.tok_rem.refs_21_
  22.7 11.1 %project.1 = (bf16[768,1024]{1,0:T(8,128)(2,1)}, bf16[2304,1024]{1,0:T(8,128)(2,1)}) custom-call(bf16[512,768]{1,0:T(8,128)(2,1)} %get-tuple-element.67.own_ref.tok_own.refs_20_, bf16[512,768]{1,0:T(8,128)(2,1)} %collective-permute-done.rem_ref.tok_rem.refs_21_, f32[8,768]{1,0:T(8,128)} %stack.50.vec_ref.refs_23_, ...), custom_call_target="tpu_custom_call" | custom-call | flops 3623878656 | bytes 14680064 | tf_op jit(solution)/shard_map/project/pallas_call | solution.py:231
  33.8 41.7 %attend.1 = (bf16[768,1024]{1,0:T(8,128)(2,1)}, bf16[12,1024,1024]{2,1,0:T(8,128)(2,1)}, f32[6,8,1024]{2,1,0:T(8,128)}, bf16[512,768]{1,0:T(8,128)(2,1)}) custom-call(bf16[2304,1024]{1,0:T(8,128)(2,1)} %get-tuple-element.39.q_ref.k_ref.v_ref.refs_0_.refs_1_.refs_2_, bf16[2304,1024]{1,0:T(8,128)(2,1)} %get-tuple-element.39.q_ref.k_ref.v_ref.refs_0_.refs_1_.refs_2_, ...), custom_call_target="tpu_custom_call" | custom-call | flops 12884901888 | bytes 31457280 | tf_op jit(solution)/shard_map/attend/pallas_call | solution.py:303
  75.4 64.7 %middle_links.1 = (bf16[512,768]{1,0:T(8,128)(2,1)}, bf16[512,768]{1,0:T(8,128)(2,1)}, f32[1024,768]{1,0:T(8,128)}, bf16[768,1024]{1,0:T(8,128)(2,1)}, bf16[2,4,...) custom-call(bf16[768,1024]{1,0:T(8,128)(2,1)} %get-tuple-element.40., ...), custom_call_target="tpu_custom_call" | custom-call | flops 32614907904 | bytes 41943040 | tf_op jit(solution)/shard_map/middle_links/pallas_call | solution.py:717
  140.2 112.7 %back.1 = (bf16[2,512,768]{2,1,0:T(8,128)(2,1)}, f32[2,512,768]{2,1,0:T(8,128)}, f32[48,2304]{1,0:T(8,128)}, f32[48,768]{1,0:T(8,128)}, f32[48,3072]{1,0:T(8,128...) custom-call(bf16[2304,1024]{1,0:T(8,128)(2,1)} %get-tuple-element.39, ...), custom_call_target="tpu_custom_call" | custom-call | flops 33017561088 | bytes 62914560 | tf_op jit(solution)/shard_map/back/pallas_call | solution.py:1488
  252.9 0.0 copy-start.10
  252.9 0.0 copy-start.9
  252.9 1.1 copy.53
  254.0 0.1 fusion.18
  254.1 0.0 copy-done.10
  254.1 0.0 copy-done.9
  254.2 0.1 copy.47
  254.3 0.1 copy.48
  254.3 0.6 dynamic_slice.47
  254.9 0.6 dynamic_slice.49
  255.5 0.6 dynamic_slice.46
  256.1 0.1 multiply_cosine_fusion.1
  256.3 0.6 dynamic_slice.48
  256.9 0.7 fusion.2
  257.6 1.2 fusion
  258.8 0.0 copy-done.3
  258.8 1.1 copy.61
  260.0 1.3 copy-done.2
  261.3 1.7 copy.62
  262.9 0.0 copy-done.6
  263.0 0.8 copy.63
  263.7 0.7 copy.64
  264.4 0.8 copy.65
  265.2 0.0 copy-done.4
  265.2 0.8 copy.66
  (40 shorter events, 0.3 us)
Async XLA Ops:
  0.6 7.0 %copy-start = (bf16[128,4608]{1,0:T(8,128)(2,1)S(1)}, bf16[128,4608]{1,0:T(8,128)(2,1)}, u32[]{:S(2)}) copy-start(bf16[128,4608]{1,0:T(8,128)(2,1)} %param.20) | copy-start | bytes 3538948
  0.7 3.0 %copy-start.16 = (s32[2]{0:T(128)S(1)}, s32[2]{0:T(128)}, u32[]{:S(2)}) copy-start(s32[2]{0:T(128)} %param.17) | copy-start | bytes 28
  0.7 6.9 %copy-start.12 = (f32[768]{0:T(1024)S(1)}, f32[768]{0:T(1024)}, u32[]{:S(2)}) copy-start(f32[768]{0:T(1024)} %param.22) | copy-start | bytes 9220
  0.7 6.9 %copy-start.13 = (f32[768]{0:T(1024)S(1)}, f32[768]{0:T(1024)}, u32[]{:S(2)}) copy-start(f32[768]{0:T(1024)} %param.25) | copy-start | bytes 9220
  0.7 7.6 %copy-start.11 = (f32[4608]{0:T(1024)S(1)}, f32[4608]{0:T(1024)}, u32[]{:S(2)}) copy-start(f32[4608]{0:T(1024)} %param.21) | copy-start | bytes 55300
  3.2 19.5 %collective-permute-start = (bf16[512,768]{1,0:T(8,128)(2,1)S(1)}, bf16[512,768]{1,0:T(8,128)(2,1)}, u32[]{:S(2)}, u32[]{:S(2)}) collective-permute-start(bf16[512,768]{1,0:T(8,128)(2,1)S(1)} %get-tuple-element.66), channel_id=1, source_target_pairs={{0,1},{1,0},{2,3},{3,2},{4,5},{5,4},{6,7},{7,6},{8,9},{9,8},{10,11... | collective-permute-start | bytes 2359304 | tf_op jit(solution)/shard_map/ppermute | solution.py:1538
  8.4 6.1 %copy-start.14 = (f32[768]{0:T(1024)S(1)}, f32[768]{0:T(1024)}, u32[]{:S(2)}) copy-start(f32[768]{0:T(1024)} %param.29) | copy-start | bytes 9220
  8.4 6.1 %copy-start.17 = (s32[2]{0:T(128)S(1)}, s32[2]{0:T(128)}, u32[]{:S(2)}) copy-start(s32[2]{0:T(128)} %param.18) | copy-start | bytes 28
  8.4 6.7 %copy-start.18 = (s32[2]{0:T(128)S(1)}, s32[2]{0:T(128)}, u32[]{:S(2)}) copy-start(s32[2]{0:T(128)} %param.19) | copy-start | bytes 28
  8.4 11.1 %copy-start.7 = (bf16[2,512,768]{2,1,0:T(8,128)(2,1)S(1)}, bf16[2,512,768]{2,1,0:T(8,128)(2,1)}, u32[]{:S(2)}) copy-start(bf16[2,512,768]{2,1,0:T(8,128)(2,1)} %cot_ref.1) | copy-start | bytes 4718596
  252.9 1.2 copy-start.10
  252.9 1.2 copy-start.9
  252.9 2.6 copy-start.15
  254.0 4.8 %copy-start.3 = (bf16[2,512,768]{2,1,0:T(8,128)(2,1)S(1)}, bf16[2,512,768]{2,1,0:T(8,128)(2,1)}, u32[]{:S(2)}) copy-start(bf16[2,512,768]{2,1,0:T(8,128)(2,1)} %get-tuple-element.102) | copy-start | bytes 4718596
  258.8 2.5 copy-start.2
  261.3 1.7 copy-start.6
  261.3 2.4 copy-start.8
  261.3 4.7 %copy-start.1 = (bf16[128,4608]{1,0:T(8,128)(2,1)S(1)}, bf16[128,4608]{1,0:T(8,128)(2,1)}, u32[]{:S(2)}) copy-start(bf16[128,4608]{1,0:T(8,128)(2,1)} %param.20) | copy-start | bytes 3538948
  262.9 1.4 copy-start.5
  263.0 2.2 copy-start.4

commit v4 on v3

--- a/solution.py
+++ b/solution.py
@@ -276,17 +276,28 @@
     for h in range(2):
         v_ext[h, 0:HD, :] = v_ref[h * HD : (h + 1) * HD, :]
         v_ext[h, HD:, :] = jnp.ones((16, tokens), BF)
-    for h in range(2):
-        for t in range(tokens // tile):
-            cols = slice(t * tile, (t + 1) * tile)
-            s = mm(k_nat, q_mask[h, :, cols])
-            top = jnp.max(s, axis=0, keepdims=True)
-            e = jnp.exp(s - top).astype(BF)
-            e_ref[h, :, cols] = e
-            mix = mm(v_ext[h], e)
-            linv = 1.0 / mix[HD : HD + 1, :]
-            linv_ref[0, h : h + 1, cols] = linv
-            att_ref[h * HD : (h + 1) * HD, cols] = (mix[0:HD, :] * linv).astype(BF)
+    def score(h, cols):
+        return mm(k_nat, q_mask[h, :, cols])
+
+    def soften(h, cols, s):
+        e_ref[h, :, cols] = jnp.exp(s - jnp.max(s, axis=0, keepdims=True)).astype(BF)
+
+    def mix(h, cols):
+        mixed = mm(v_ext[h], e_ref[h, :, cols])
+        linv = 1.0 / mixed[HD : HD + 1, :]
+        linv_ref[0, h : h + 1, cols] = linv
+        att_ref[h * HD : (h + 1) * HD, cols] = (mixed[0:HD, :] * linv).astype(BF)
+
+    units = [(h, slice(t, t + tile)) for t in range(0, tokens, tile) for h in range(2)]
+    coming = score(*units[0])
+    for i, unit in enumerate(units):
+        here = coming
+        if i + 1 < len(units):
+            coming = score(*units[i + 1])
+        soften(*unit, here)
+        if i > 0:
+            mix(*units[i - 1])
+    mix(*units[-1])
 
     @pl.when(step == pl.num_programs(0) - 1)
     def _():
@@ -536,8 +547,12 @@
     g_out_ref,
     g_up_ref,
     g_down_ref,
-    up_ref,
-    down_ref,
+    up_last_ref,
+    up_one_ref,
+    up_two_ref,
+    down_last_ref,
+    down_one_ref,
+    down_two_ref,
     mod_ref,
     sum_ref,
     branch,
@@ -551,8 +566,12 @@
     d_up,
     up_core,
     up_side,
+    up_y,
+    up_z,
     down_core,
     down_y,
+    down_side,
+    down_z,
     sems,
 ):
     step = pl.program_id(0)
@@ -572,27 +591,63 @@
     scale_two = vec_ref[6:7, :]
 
     links = Links(sems, zs)
-    x, y, c = links.x, links.y, links.c
-    up_to_core = [
-        links.swap(lambda: g_up_ref.at[:, :, :, 1 - c], lambda j=j: up_core.at[j], links.core)
-        for j in range(steps - 1)
-    ]
-    down_to_core = [
-        links.swap(lambda: g_down_ref.at[:, 1 - c], lambda j=j: down_core.at[j], links.core)
-        for j in range(steps - 1)
-    ]
-    up_to_side = [
-        links.swap(lambda j=j: up_core.at[j, 1 - x], lambda j=j: up_side.at[j], links.facing)
-        for j in range(steps - 1)
-    ]
-    down_to_y = [
-        links.swap(lambda j=j: down_core.at[j, 1 - y], lambda j=j: down_y.at[j], links.across)
-        for j in range(steps - 1)
-    ]
+    x, y, z, c = links.x, links.y, links.z, links.c
+    tiles = range(steps - 1)
+
+    def swaps(src, dst, device):
+        return [links.swap(lambda j=j: src(j), lambda j=j: dst.at[j], device) for j in tiles]
+
+    up_to_core = swaps(lambda j: g_up_ref.at[:, :, :, 1 - c], up_core, links.core)
+    down_to_core = swaps(lambda j: g_down_ref.at[:, 1 - c], down_core, links.core)
+    up_to_side = swaps(lambda j: up_core.at[j, 1 - x], up_side, links.facing)
+    down_to_y = swaps(lambda j: down_core.at[j, 1 - y], down_y, links.across)
+    up_to_y = swaps(lambda j: up_core.at[j, x, :, 1 - y], up_y, links.across)
+    down_to_side = swaps(lambda j: down_core.at[j, y, 1 - x], down_side, links.facing)
+    down_far = links.gather(lambda: down_core.at[0, y, x], lambda slot: down_z.at[slot], 0)
+    up_far = links.spread(lambda f: up_core.at[0, x, f, y], lambda slot: up_z.at[slot])
+
+    def core_stage(j):
+        up_to_core[j]().start()
+        down_to_core[j]().start()
+
+    def first_stage(j):
+        up_to_core[j]().wait()
+        for h, a, b in grid_of(2, zs, 2):
+            up_core[j, h, a, b] = up_core[j, h, a, b] + g_up_ref[h, a, b, c]
+        up_to_side[j]().start()
+        down_to_core[j]().wait()
+        for b, h in grid_of(2, 2):
+            down_core[j, b, h] = down_core[j, b, h] + g_down_ref[b, c, h]
+        down_to_y[j]().start()
+
+    def first_done(j):
+        up_to_side[j]().wait()
+        for a, b in grid_of(zs, 2):
+            up_core[j, x, a, b] = up_core[j, x, a, b] + up_side[j, a, b]
+        down_to_y[j]().wait()
+        for h in range(2):
+            down_core[j, y, h] = down_core[j, y, h] + down_y[j, h]
+
+    def second_stage(j):
+        first_done(j)
+        up_to_y[j]().start()
+        down_to_side[j]().start()
+
+    def second_done(j):
+        up_to_y[j]().wait()
+        for a in range(zs):
+            up_core[j, x, a, y] = up_core[j, x, a, y] + up_y[j, a]
+        down_to_side[j]().wait()
+        down_core[j, y, x] = down_core[j, y, x] + down_side[j]
+
+    def third_stage():
+        second_done(0)
+        up_far[0]()
+        down_far[0]()
 
     @pl.when(step == 0)
     def _():
-        greet(links.core, links.across, links.facing)
+        greet(links.core, links.across, links.facing, *[links.at_z(f) for f in links.far])
         for part, (tok, cot) in enumerate(((tok_own, cot_own), (tok_rem, cot_rem))):
             for t in range(per_half):
                 src = slice(t * tile, (t + 1) * tile)
@@ -608,45 +663,65 @@
                 down_acc[dst, :] = jnp.zeros((tile, width), F32)
                 d_act[dst, :] = jnp.zeros((tile, width), F32)
 
-    bup = jnp.zeros((1, w_up_ref.shape[1]), F32)
-    for part in range(2):
-        rows = slice(part * half, (part + 1) * half)
+    chunk = tokens // 4
+
+    def one(k, bup):
+        rows = rows_of(chunk, k)
         up = mm(act_two[rows, :], w_up_ref[...]) + b_up_ref[...]
+        d_hidden = mm(d_down[rows, :], w_down_ref[...], NT)
         value, slope = gelu_both(up)
-        hidden[rows, :] = value.astype(BF)
-        d_up_low = (slope * mm(d_down[rows, :], w_down_ref[...], NT)).astype(BF)
-        bup += col_sum(d_up_low.astype(F32))
+        low = value.astype(BF)
+        hidden[rows, :] = low
+        d_up_low = (slope * d_hidden).astype(BF)
         d_up[rows, :] = d_up_low
+        down_acc[rows, :] += mm(low, w_down_ref[...])
+        d_act[rows, :] += mm(d_up_low, w_up_ref[...], NT)
+        return bup + col_sum(d_up_low.astype(F32))
+
+    bup = lax.fori_loop(0, 4, one, jnp.zeros((1, w_up_ref.shape[1]), F32))
     for j in range(steps):
         pl.when(step == j)(lambda j=j: put_rows(sum_ref, 2 * width // 128 + j * bup.shape[1] // 128, bup))
 
-    for j in range(steps - 1):
-
-        @pl.when(step == j + 1)
-        def _(j=j):
-            up_to_core[j]().wait()
-            for h, a, b in grid_of(2, zs, 2):
-                up_core[j, h, a, b] = up_core[j, h, a, b] + g_up_ref[h, a, b, c]
-            up_to_side[j]().start()
-            down_to_core[j]().wait()
-            for b in range(2):
-                down_core[j, b] = down_core[j, b] + g_down_ref[b, c]
-            down_to_y[j]().start()
-
-    down_acc[...] += mm(hidden[...], w_down_ref[...])
-    d_act[...] += mm(d_up[...], w_up_ref[...], NT)
-    g_down = mm(hidden[...], d_down[...], TN).astype(BF)
-    g_down_ref[...] = g_down.reshape(g_down_ref.shape)
-    g_up = mm(act_two[...], d_up[...], TN).astype(BF)
-    for h in range(2):
-        g_up_ref[h] = g_up[:, h * cut : (h + 1) * cut].reshape(g_up_ref.shape[1:])
-
-    for j in range(steps - 1):
-
-        @pl.when(step == j)
-        def _(j=j):
-            up_to_core[j]().start()
-            down_to_core[j]().start()
+    @pl.when(step == 1)
+    def _():
+        first_stage(0)
+
+    @pl.when(step == 2)
+    def _():
+        second_stage(0)
+        first_stage(1)
+
+    @pl.when(step == 3)
+    def _():
+        second_stage(1)
+        first_stage(2)
+
+    chunk_out = width // 3
+    g_down_flat = g_down_ref.reshape(width, width)
+    g_up_flat = g_up_ref.reshape(2, width, cut)
+
+    def grads(k, carry):
+        outs = rows_of(chunk_out, k)
+        g_down_flat[outs, :] = mm(hidden[:, outs], d_down[...], TN).astype(BF)
+        g_up = mm(act_two[:, outs], d_up[...], TN).astype(BF)
+        for h in range(2):
+            g_up_flat[h, outs, :] = g_up[:, h * cut : (h + 1) * cut]
+        return carry
+
+    lax.fori_loop(0, 3, grads, 0)
+
+    @pl.when(step == 0)
+    def _():
+        core_stage(0)
+
+    @pl.when(step == 1)
+    def _():
+        core_stage(1)
+
+    @pl.when(step == 2)
+    def _():
+        third_stage()
+        core_stage(2)
 
     @pl.when(step == steps - 1)
     def _():
@@ -681,12 +756,23 @@
         for h in range(2):
             g_out_ref[h] = g_out[:, h * cut : (h + 1) * cut].reshape(g_out_ref.shape[1:])
         d_att_ref[...] = mm(w_out_ref[...], d_branch[...], NT).astype(BF)
-        for j in range(steps - 1):
-            up_to_side[j]().wait()
-            for a, b in grid_of(zs, 2):
-                up_ref[j, a, b] = up_core[j, x, a, b] + up_side[j, a, b]
-            down_to_y[j]().wait()
-            down_ref[j] = down_core[j, y] + down_y[j]
+        up_far[1]()
+        total = up_core[0, x, z, y].astype(F32)
+        for f in links.far:
+            total += up_z[f].astype(F32)
+        up_last_ref[...] = total.astype(BF)
+        down_far[1]()
+        total = down_core[0, y, x].astype(F32)
+        for f in links.far:
+            total += down_z[f].astype(F32)
+        down_last_ref[...] = total.astype(BF)
+        second_done(1)
+        for a in range(zs):
+            up_one_ref[a] = up_core[1, x, a, y]
+        down_one_ref[...] = down_core[1, y, x]
+        first_done(2)
+        up_two_ref[...] = up_core[2, x]
+        down_two_ref[...] = down_core[2, y]
 
 
 def middle_links(
@@ -700,7 +786,8 @@
     rows = width // (4 * zs)
     down_rows = tile // 4
     halves = (2, zs, 2, 2, rows, cut)
-    owned = (2, 2, down_rows, width)
+    down_half = (down_rows // 2, width)
+    owned = (2, 2, 2) + down_half
     outs = [
         ((half, width), BF),
         ((half, width), BF),
@@ -709,8 +796,12 @@
         (halves, BF),
         (halves, BF),
         (owned, BF),
-        ((zs - 1, zs, 2, rows, cut), BF),
-        ((zs - 1, down_rows, width), BF),
+        ((rows, cut), BF),
+        ((zs, rows, cut), BF),
+        ((zs, 2, rows, cut), BF),
+        (down_half, BF),
+        (down_half, BF),
+        ((2,) + down_half, BF),
         ((early_mod_rows(width), 128), BF),
         ((early_sum_rows(width, ff), 128), F32),
     ]
@@ -744,9 +835,13 @@
             pltpu.VMEM((tokens, tile), BF),
             pltpu.VMEM((zs - 1, 2, zs, 2, rows, cut), BF),
             pltpu.VMEM((zs - 1, zs, 2, rows, cut), BF),
-            pltpu.VMEM((zs - 1, 2, down_rows, width), BF),
-            pltpu.VMEM((zs - 1, down_rows, width), BF),
-            pltpu.SemaphoreType.DMA((8 * (zs - 1),)),
+            pltpu.VMEM((zs - 1, zs, rows, cut), BF),
+            pltpu.VMEM((zs, rows, cut), BF),
+            pltpu.VMEM((zs - 1, 2, 2) + down_half, BF),
+            pltpu.VMEM((zs - 1, 2) + down_half, BF),
+            pltpu.VMEM((zs - 1,) + down_half, BF),
+            pltpu.VMEM((zs,) + down_half, BF),
+            pltpu.SemaphoreType.DMA((12 * (zs - 1) + 1 + 3 * zs,)),
         ],
         compiler_params=params(62, collective_id=4),
         cost_estimate=pl.CostEstimate(
@@ -1020,18 +1115,22 @@
         sin_ref,
         own_ref,
         give_ref,
-        up_ref,
-        down_ref,
+        up_last_ref,
+        up_one_ref,
+        up_two_ref,
+        down_last_ref,
+        down_one_ref,
+        down_two_ref,
         raw_up,
         raw_out,
         raw_down,
         mod_ref,
         sum_ref,
-        act_ref,
-        w_ref,
-        tok_own,
-        tok_rem,
-        dx_ref,
+        act_in,
+        w_in,
+        tok_own_in,
+        tok_rem_in,
+        dx_in,
         vec_ref,
     ) = ins
     result, grad_ref, s_qkv, s_out, s_up, s_down, *small_outs = outs
@@ -1040,16 +1139,20 @@
         d_proj,
         sems,
         u_own,
-        u_core,
-        u_side,
-        u_sum,
         u_y,
         u_z,
         u_last,
         u_facing,
+        w_own,
+        w_core,
+        w_y,
+        w_z,
+        w_last,
+        w_facing,
         d_own,
         d_core,
         d_y,
+        d_side,
         d_sum,
         d_z,
         d_last,
@@ -1070,56 +1173,85 @@
         mod_late,
         sum_early,
         sum_late,
+        act_ref,
+        w_ref,
+        tok_own,
+        tok_rem,
+        dx_ref,
+        g_own,
     ) = scratch
     step = pl.program_id(0)
     tokens = q_ref.shape[1]
     width = act_ref.shape[0]
     half = tokens // 2
     cut = width // 2
-    pieces = zs + 1
     links = Links(sems, zs)
     x, y, z, c = links.x, links.y, links.z, links.c
 
-    def at(k):
-        return pl.when(step == k)
-
-    raws = (raw_up, raw_out)
-    u_keep = [links.local(lambda r=r: r.at[:, :, :, c], lambda k=k: u_own.at[k]) for k, r in enumerate(raws)]
-    u_to_core = [
-        links.swap(lambda r=r: r.at[:, :, :, 1 - c], lambda k=k: u_core.at[k], links.core)
-        for k, r in enumerate(raws)
-    ]
-    u_to_side = [
-        links.swap(lambda k=k: u_own.at[k, 1 - x], lambda k=k: u_side.at[k], links.facing)
-        for k in range(2)
-    ]
-    u_load = [links.local(lambda j=j: up_ref.at[j, :, y], lambda j=j: u_sum.at[j, :, y]) for j in range(zs - 1)]
-
-    def u_y_src(j):
-        if j < zs - 1:
-            return up_ref.at[j, :, 1 - y]
-        return u_sum.at[j, :, 1 - y]
-
-    u_to_y = [
-        links.swap(lambda j=j: u_y_src(j), lambda j=j: u_y.at[j], links.across) for j in range(pieces)
-    ]
+    fetch = [
+        links.local(lambda p=p: p[0], lambda p=p: p[1])
+        for p in (
+            (act_in, act_ref),
+            (w_in, w_ref),
+            (tok_own_in, tok_own),
+            (tok_rem_in, tok_rem),
+            (dx_in, dx_ref),
+        )
+    ]
+    u_load = [
+        links.local(lambda: up_last_ref, lambda: u_last.at[0]),
+        links.local(lambda: up_one_ref.at[z], lambda: u_own.at[0, z]),
+        links.local(lambda: up_two_ref.at[:, y], lambda: u_own.at[1]),
+    ]
+    u_to_y = links.swap(lambda: up_two_ref.at[:, 1 - y], lambda: u_y, links.across)
     u_far = [
-        links.spread(lambda f, j=j: u_sum.at[j, f, y], lambda slot, j=j: u_z.at[j, slot])
-        for j in range(pieces)
+        links.spread(
+            lambda f, j=j: up_one_ref.at[f] if j == 0 else u_own.at[1, f],
+            lambda slot, j=j: u_z.at[j, slot],
+        )
+        for j in range(2)
     ]
     u_to_facing = [
         links.swap(lambda j=j: u_last.at[j], lambda j=j: u_facing.at[j], links.facing)
-        for j in range(pieces)
+        for j in range(3)
+    ]
+    raws = (raw_up, raw_out)
+    w_keep = [
+        links.local(lambda r=r: r.at[:, :, :, c], lambda k=k: w_own.at[k]) for k, r in enumerate(raws)
+    ]
+    w_to_core = [
+        links.swap(lambda r=r: r.at[:, :, :, 1 - c], lambda k=k: w_core.at[k], links.core)
+        for k, r in enumerate(raws)
+    ]
+    w_to_y = [
+        links.swap(lambda k=k: w_own.at[k, :, :, 1 - y], lambda k=k: w_y.at[k], links.across)
+        for k in range(2)
+    ]
+    w_far = [
+        links.spread(lambda f, k=k: w_own.at[k, :, f, y], lambda slot, k=k: w_z.at[k, slot])
+        for k in range(2)
+    ]
+    w_to_facing = [
+        links.swap(lambda k=k: w_last.at[k], lambda k=k: w_facing.at[k], links.facing)
+        for k in range(2)
     ]
     d_keep = links.local(lambda: raw_down.at[:, c], lambda: d_own)
     d_to_core = links.swap(lambda: raw_down.at[:, 1 - c], lambda: d_core, links.core)
     d_to_y = links.swap(lambda: d_own.at[1 - y], lambda: d_y, links.across)
-    d_load = links.local(lambda: down_ref, lambda: d_sum.at[0 : zs - 1])
+    d_to_side = [
+        links.swap(lambda: down_two_ref.at[1 - x], lambda: d_side.at[0], links.facing),
+        links.swap(lambda: d_own.at[y, 1 - x], lambda: d_side.at[1], links.facing),
+    ]
+    d_load = [
+        links.local(lambda: down_last_ref, lambda: d_last),
+        links.local(lambda: down_one_ref, lambda: d_sum.at[0]),
+        links.local(lambda: down_two_ref.at[x], lambda: d_sum.at[1]),
+    ]
     d_far = [
         links.gather(
-            lambda j=j: down_ref.at[j] if j < zs - 1 else d_sum.at[j], lambda slot: d_z.at[slot], j
+            lambda j=j: down_one_ref if j == 1 else d_sum.at[j - 1], lambda slot: d_z.at[slot], j
         )
-        for j in range(zs)
+        for j in range(1, zs)
     ]
     d_to_facing = links.swap(lambda: d_last, lambda: d_facing, links.facing)
     groups = range(len(split))
@@ -1145,6 +1277,8 @@
         return remote(give_ref, result.at[slot], sems.at[out_sem], sems.at[out_sem + 1], links.facing)
 
     give_grad = links.swap(lambda: g_send, lambda: g_take, links.facing)
+    keep_grad = links.local(lambda: g_own, lambda: grad_ref.at[x])
+    put_grad = links.local(lambda: g_own, lambda: grad_ref.at[1 - x])
     early = [
         gather_stages(links, mod_early),
         sum_stages(links, sum_early, early_take, early_far),
@@ -1159,26 +1293,49 @@
         for stages in arrays:
             stages[stage][1]()
 
-    def u_y_done(j):
-        u_to_y[j]().wait()
-        for a in range(zs):
-            u_sum[j, a, y] = u_sum[j, a, y] + u_y[j, a]
-        u_far[j][0]()
+    def sum_far(own, taken):
+        total = own.astype(F32)
+        for f in links.far:
+            total += taken(f).astype(F32)
+        return total.astype(BF)
 
     def u_z_done(j):
         u_far[j][1]()
-        total = u_sum[j, z, y].astype(F32)
-        for f in links.far:
-            total += u_z[j, f].astype(F32)
-        u_last[j] = total.astype(BF)
-        u_to_facing[j]().start()
+        u_last[j + 1] = sum_far(u_own[j, z], lambda f: u_z[j, f])
+        u_to_facing[j + 1]().start()
 
     def u_done(j):
         u_to_facing[j]().wait()
         mine, other = u_last[j].astype(F32), u_facing[j].astype(F32)
-        out, start = (s_up, j * width) if j < zs else (s_out, 0)
-        out[:, start : start + cut] = jnp.where(x == 0, mine, other)
-        out[:, start + cut : start + width] = jnp.where(x == 0, other, mine)
+        start = j * width
+        s_up[:, start : start + cut] = jnp.where(x == 0, mine, other)
+        s_up[:, start + cut : start + width] = jnp.where(x == 0, other, mine)
+
+    def w_core_done(k):
+        w_keep[k]().wait()
+        w_to_core[k]().wait()
+        for h, a, b in grid_of(2, zs, 2):
+            w_own[k, h, a, b] = w_own[k, h, a, b] + w_core[k, h, a, b]
+
+    def w_y_done(k):
+        w_to_y[k]().wait()
+        for h, a in grid_of(2, zs):
+            w_own[k, h, a, y] = w_own[k, h, a, y] + w_y[k, h, a]
+        w_far[k][0]()
+
+    def w_z_done(k):
+        w_far[k][1]()
+        for h in range(2):
+            w_last[k, h] = sum_far(w_own[k, h, z, y], lambda f: w_z[k, f, h])
+        w_to_facing[k]().start()
+
+    def w_done(k):
+        w_to_facing[k]().wait()
+        out, start = (s_up, (zs - 1) * width) if k == 0 else (s_out, 0)
+        for h in range(2):
+            out[:, start + h * cut : start + (h + 1) * cut] = w_last[k, h].astype(F32) + w_facing[
+                k, h
+            ].astype(F32)
 
     def q_core_done(g):
         q_to_core[g]().wait()
@@ -1194,10 +1351,7 @@
 
     def q_z_done(g):
         q_far[g][1]()
-        total = q_cores[g][z, y].astype(F32)
-        for f in links.far:
-            total += q_zs[g][f].astype(F32)
-        q_lasts[g][...] = total.astype(BF)
+        q_lasts[g][...] = sum_far(q_cores[g][z, y], lambda f: q_zs[g][f])
         q_to_facing[g]().start()
 
     def q_done(g):
@@ -1218,82 +1372,122 @@
         q_to_core[g]().start()
 
 
-    @at(0)
-    def _():
+    def due_00():
         greet(links.core, links.across, links.facing, *[links.at_z(f) for f in links.far])
-        for k in range(2):
-            u_to_core[k]().start()
-            u_keep[k]().start()
         d_to_core().start()
         d_keep().start()
-        d_load().start()
-        for j in range(zs - 1):
-            u_load[j]().start()
-            u_to_y[j]().start()
-            d_far[j][0]()
+        for k in range(2):
+            w_to_core[k]().start()
+            w_keep[k]().start()
+        u_far[0][0]()
+        d_far[0][0]()
+        u_to_y().start()
+        d_to_side[0]().start()
+        for load in u_load + d_load:
+            load().start()
         mod_early[z, y, c, x] = mod_ref[...]
         sum_early[...] = sum_ref[...]
         begin(early, 0)
         keep_out().start()
         cross_out(x).start()
-
-    @at(1)
-    def _():
-        for k in range(2):
-            u_keep[k]().wait()
-            u_to_core[k]().wait()
-            for h, a, b in grid_of(2, zs, 2):
-                u_own[k, h, a, b] = u_own[k, h, a, b] + u_core[k, h, a, b]
-            u_to_side[k]().start()
+        for load in fetch:
+            load().start()
+
+    def due_01():
         d_keep().wait()
         d_to_core().wait()
-        for b in range(2):
-            d_own[b] = d_own[b] + d_core[b]
+        for b, h in grid_of(2, 2):
+            d_own[b, h] = d_own[b, h] + d_core[b, h]
         d_to_y().start()
         end(early, 0)
         begin(early, 1)
 
-    @at(2)
-    def _():
-        for j in range(zs - 1):
-            u_load[j]().wait()
-            u_y_done(j)
+    def due_10():
+        w_core_done(0)
+        w_core_done(1)
+        w_to_y[0]().start()
+        u_load[0]().wait()
+        u_to_facing[0]().start()
+
+    def due_11():
+        u_load[2]().wait()
+        u_to_y().wait()
+        for a in range(zs):
+            u_own[1, a] = u_own[1, a] + u_y[a]
+        u_far[1][0]()
+        d_load[2]().wait()
+        d_to_side[0]().wait()
+        d_sum[1] = d_sum[1] + d_side[0]
+        d_far[1][0]()
         end(early, 1)
         begin(early, 2)
 
-    @at(3)
-    def _():
+    def due_20():
+        fetch[0]().wait()
+        weight_grad_of(0)
         d_to_y().wait()
-        d_sum[zs - 1] = d_own[y] + d_y[...]
-        d_far[zs - 1][0]()
+        for h in range(2):
+            d_own[y, h] = d_own[y, h] + d_y[h]
+        d_to_side[1]().start()
+        w_to_y[1]().start()
+
+    def due_21():
+        q_core_done(0)
+        w_y_done(0)
+
+    def due_30():
+        u_load[1]().wait()
+        u_z_done(0)
+        d_to_side[1]().wait()
+        d_sum[2] = d_own[y, x] + d_side[1]
+        d_far[2][0]()
         end(early, 2)
         begin(early, 3)
 
-    @at(4)
-    def _():
-        weight_grad_of(0)
-        for k in range(2):
-            u_to_side[k]().wait()
-            for a, b in grid_of(zs, 2):
-                u_sum[zs - 1 + k, a, b] = u_own[k, x, a, b] + u_side[k, a, b]
-            u_to_y[zs - 1 + k]().start()
+    def due_31():
+        w_y_done(1)
+        q_y_done(0)
+
+    def due_40():
+        weight_grad_of(1)
+        u_z_done(1)
+        end(early, 3)
+
+    def due_41():
+        q_core_done(1)
+        w_z_done(0)
+        u_done(0)
+        u_done(1)
+
+    def due_50():
+        for load in d_load[0:2]:
+            load().wait()
         for j in range(zs - 1):
-            u_z_done(j)
-
-    @at(5)
-    def _():
-        q_core_done(0)
-        end(early, 3)
-        for k in range(2):
-            u_y_done(zs - 1 + k)
-        d_load().wait()
-        for j in range(zs):
             d_far[j][1]()
-        total = d_sum[z].astype(F32)
-        for f in links.far:
-            total += d_z[f].astype(F32)
-        d_last[...] = total.astype(BF)
+
+        @pl.when(z > 0)
+        def _():
+            d_last[...] = sum_far(d_sum[jnp.maximum(z - 1, 0)], lambda f: d_z[f])
+
         d_to_facing().start()
+
+    def due_51():
+        q_y_done(1)
+        w_z_done(1)
+        u_done(2)
+
+    due = (
+        (due_00, due_01),
+        (due_10, due_11),
+        (due_20, due_21),
+        (due_30, due_31),
+        (due_40, due_41),
+        (due_50, due_51),
+    )
+
+    def do_due(h):
+        for k in range(PAIRS):
+            pl.when(step == k)(due[k][h])
 
 
     @pl.when(step < PAIRS)
@@ -1311,27 +1505,56 @@
             d_proj[pl.ds(pl.multiple_of(start, 32), 32), :] = (a * cos + b * sin).astype(BF)
             d_proj[pl.ds(pl.multiple_of(start + 32, 32), 32), :] = (b * cos - a * sin).astype(BF)
 
+        do_due(0)
+        inners, keys, values, queries = [], [], [], [[], []]
         for h in range(2):
             rows = slice(h * HD, (h + 1) * HD)
             linv = linv_ref[0, h : h + 1, :]
             d_o = d_att_ref[rows, :].astype(F32)
-            d_os = (d_o * linv).astype(BF)
-            do_mask[h, rows, :] = d_os
+            do_mask[h, rows, :] = (d_o * linv).astype(BF)
             do_mask[h, (1 - h) * HD : (2 - h) * HD, :] = zero
-            inner = col_sum(d_o * att_ref[rows, :].astype(F32)) * linv
-            d_values = mm(d_os, e_ref[h], NT)
-            start = 2 * width + step * 2 * HD + h * HD
-            d_proj[pl.ds(pl.multiple_of(start, HD), HD), :] = d_values.astype(BF)
-            d_keys = jnp.zeros((HD, tokens), F32)
-            d_queries = []
-            for t in range(tokens // tile):
-                cols = slice(t * tile, (t + 1) * tile)
-                d_probs = mm(v_nat, do_mask[h, :, cols])
-                d_s = (e_ref[h, :, cols].astype(F32) * (d_probs - inner[:, cols])).astype(BF)
-                d_queries.append(mm(k_ref[rows, :], d_s))
-                d_keys += mm(q_ref[rows, cols], d_s, NT)
-            put(0, h, jnp.concatenate(d_queries, axis=1) * HD**-0.5)
-            put(1, h, d_keys)
+            inners.append(col_sum(d_o * att_ref[rows, :].astype(F32)) * linv)
+
+        def ahead(h, cols):
+            return mm(v_nat, do_mask[h, :, cols])
+
+        def centre(h, cols, d_probs):
+            rows = slice(h * HD, (h + 1) * HD)
+            e = e_ref[h, :, cols]
+            part = mm(do_mask[h, rows, cols], e, NT)
+            if cols.start == 0:
+                values.append(part)
+            else:
+                values[h] += part
+            return (e.astype(F32) * (d_probs - inners[h][:, cols])).astype(BF)
+
+        def behind(h, cols, d_s):
+            rows = slice(h * HD, (h + 1) * HD)
+            queries[h].append(mm(k_ref[rows, :], d_s))
+            part = mm(q_ref[rows, cols], d_s, NT)
+            if cols.start == 0:
+                keys.append(part)
+            else:
+                keys[h] += part
+            if cols.stop == tokens:
+                put(0, h, jnp.concatenate(queries[h], axis=1) * HD**-0.5)
+                put(1, h, keys[h])
+                start = 2 * width + step * 2 * HD + h * HD
+                d_proj[pl.ds(pl.multiple_of(start, HD), HD), :] = values[h].astype(BF)
+
+        units = [(h, slice(t, t + tile)) for h in range(2) for t in range(0, tokens, tile)]
+        coming = ahead(*units[0])
+        for i, unit in enumerate(units):
+            if i == len(units) // 2:
+                do_due(1)
+            here = coming
+            if i + 1 < len(units):
+                coming = ahead(*units[i + 1])
+            d_s = centre(*unit, here)
+            if i > 0:
+                behind(*units[i - 1], held)
+            held = d_s
+        behind(*units[-1], held)
 
 
     def finish(tok, cols):
@@ -1340,18 +1563,19 @@
         grad = dx_ref[cols, :] + norm_pull(n, rstd, d_act * vec_ref[0:1, :])
         return grad, col_sum(d_act), col_sum(d_act * n)
 
-    @at(PAIRS)
-    def _():
-        weight_grad_of(1)
-        for k in range(2):
-            u_z_done(zs - 1 + k)
-        q_y_done(0)
+    @pl.when(step == PAIRS)
+    def _():
+        for load in fetch[1:]:
+            load().wait()
         grad, shift, pull = finish(tok_rem, slice(half, 2 * half))
         g_send[...] = grad.astype(BF)
         give_grad().start()
-        q_core_done(1)
+        weight_grad_of(2)
+        q_z_done(0)
+        q_core_done(2)
         grad, shift_own, pull_own = finish(tok_own, slice(0, half))
-        grad_ref[x] = grad
+        g_own[...] = grad
+        keep_grad().start()
         shift += shift_own
         pull += pull_own
         lines = width // 128
@@ -1362,41 +1586,48 @@
         sum_late[lines:, :] = jnp.zeros((sum_late.shape[0] - lines, 128), F32)
         put_rows(sum_late, 0, pull * (1.0 + vec_ref[3:4, :]))
         begin(late, 0)
-        d_to_facing().wait()
-        s_down[...] = d_last[...].astype(F32) + d_facing[...].astype(F32)
+        q_z_done(1)
         end(late, 0)
         begin(late, 1)
-        for j in range(pieces):
-            u_done(j)
-        q_z_done(0)
+        q_y_done(2)
         end(late, 1)
         begin(late, 2)
-        q_y_done(1)
+        for k in range(2):
+            w_done(k)
+        d_to_facing().wait()
+        mine, other = d_last[...].astype(F32), d_facing[...].astype(F32)
+        rows_half = mine.shape[0]
+        s_down[0:rows_half, :] = jnp.where(x == 0, mine, other)
+        s_down[rows_half:, :] = jnp.where(x == 0, other, mine)
         end(late, 2)
         begin(late, 3)
         keep_out().wait()
         cross_out(x).wait_send()
         cross_out(1 - x).wait_recv()
         q_done(0)
-        q_z_done(1)
+        q_done(1)
+        q_z_done(2)
         end(late, 3)
         give_grad().wait()
-        grad_ref[1 - x] = g_take[...].astype(F32)
-        q_done(1)
+        keep_grad().wait()
+        g_own[...] = g_take[...].astype(F32)
+        put_grad().start()
+        q_done(2)
+        put_grad().wait()
         for out, value in zip(small_outs, (mod_early, mod_late, sum_early, sum_late)):
             out[...] = value[...]
 
 
 def back(ins, zs, ff):
-    (q, att, d_att, e, linv, cos_t, sin_t, own, give, up, down, raw_up, raw_out, raw_down) = ins[:14]
-    mod, sums, act_t, w_qkv_t, tok_own, tok_rem, dx, vec = ins[14:]
+    q, att, d_att, e, linv, cos_t, sin_t = ins[:7]
+    mod, sums, vec = ins[-8], ins[-7], ins[-1]
     width, tokens = att.shape
     half = tokens // 2
     cut = width // 2
     rows = width // (4 * zs)
     down_rows = ff // (4 * zs)
-    pieces = zs + 1
-    split = ((0, 8), (8, HEADS))
+    down_half = (down_rows // 2, width)
+    split = ((0, 4), (4, 8), (8, HEADS))
     sizes = [3 * (b - a) * HD for a, b in split]
     last = PAIRS - 1
 
@@ -1422,6 +1653,7 @@
         (sum_late, F32),
     ]
     outs[0] = ((2, half, width), F32)
+    fetched = ins[-6:-1]
     in_specs = (
         [part(0), part(1), part(2), part(0), part(0)]
         + [
@@ -1430,10 +1662,12 @@
             once(cos_t.shape),
             once(sin_t.shape),
         ]
-        + [ANY] * 7
-        + [once(a.shape) for a in (mod, sums, act_t, w_qkv_t, tok_own, tok_rem, dx, vec)]
+        + [ANY] * (len(ins) - 15)
+        + [once(mod.shape), once(sums.shape)]
+        + [ANY] * 5
+        + [once(vec.shape)]
     )
-    out_specs = [ANY] + [once(shape) for shape, _ in outs]
+    out_specs = [ANY, ANY] + [once(shape) for shape, _ in outs[1:]]
     out_shape = [jax.ShapeDtypeStruct((2, half, width), BF)] + [
         jax.ShapeDtypeStruct(*o) for o in outs
     ]
@@ -1441,21 +1675,25 @@
         vm(2, 2 * HD, tokens),
         vm(3 * width, tokens),
         pltpu.SemaphoreType.DMA((250,)),
+        vm(2, zs, rows, cut),
+        vm(zs, rows, cut),
+        vm(2, zs, rows, cut),
+        vm(3, rows, cut),
+        vm(3, rows, cut),
         vm(2, 2, zs, 2, rows, cut),
         vm(2, 2, zs, 2, rows, cut),
+        vm(2, 2, zs, rows, cut),
         vm(2, zs, 2, rows, cut),
-        vm(pieces, zs, 2, rows, cut),
-        vm(pieces, zs, rows, cut),
-        vm(pieces, zs, rows, cut),
-        vm(pieces, rows, cut),
-        vm(pieces, rows, cut),
-        vm(2, down_rows, width),
-        vm(2, down_rows, width),
-        vm(down_rows, width),
-        vm(zs, down_rows, width),
-        vm(zs, down_rows, width),
-        vm(down_rows, width),
-        vm(down_rows, width),
+        vm(2, 2, rows, cut),
+        vm(2, 2, rows, cut),
+        vm(2, 2, *down_half),
+        vm(2, 2, *down_half),
+        vm(2, *down_half),
+        vm(2, *down_half),
+        vm(zs - 1, *down_half),
+        vm(zs, *down_half),
+        vm(*down_half),
+        vm(*down_half),
         [vm(zs, 2, 2, rows, s) for s in sizes],
         [vm(zs, 2, rows, s) for s in sizes],
         [vm(zs, rows, s) for s in sizes],
@@ -1473,6 +1711,8 @@
         vm(*sums.shape, kind=F32),
         vm(*sum_late, kind=F32),
     ]
+    scratch += [vm(*a.shape, kind=a.dtype) for a in fetched]
+    scratch += [vm(half, width, kind=F32)]
     flat, tree = jax.tree.flatten(scratch)
     n_in, n_out = len(in_specs), len(out_specs)
 
@@ -1572,15 +1812,15 @@
     dp, dps = lax.axis_index("dp"), lax.axis_size("dp")
     ff = w_up.shape[1]
     zs = dps // 4
-    linked = dps % 4 == 0 and width % (64 * zs) == 0 and ff == zs * width
+    linked = zs == 4 and dps == 16 and width % (64 * zs) == 0 and ff == zs * width
 
     act_t, qkv_t = project(tok_own, tok_rem, vec_one, cos_t, sin_t, w_qkv_t)
     att_t, e, linv, cot_rem = attend(qkv_t, cotangent)
     if linked:
-        out_own, out_rem, dx, d_att_t, raw_out, raw_up, raw_down, up, down, mod, sums = middle_links(
+        out_own, out_rem, dx, d_att_t, raw_out, raw_up, raw_down, *partial, mod, sums = middle_links(
             att_t, tok_own, tok_rem, cot_own, cot_rem, span, vec_two, b_up[None], w_out, w_up, w_down, zs
         )
-        ins = (qkv_t, att_t, d_att_t, e, linv, cos_t, sin_t, out_own, out_rem, up, down)
+        ins = (qkv_t, att_t, d_att_t, e, linv, cos_t, sin_t, out_own, out_rem, *partial)
         ins += (raw_up, raw_out, raw_down, mod, sums, act_t, w_qkv_t, tok_own, tok_rem, dx, vec_one)
         output, grad_tokens, *shards, mod_early, mod_late, sum_early, sum_late = back(ins, zs, ff)
         mod_early = mod_early.reshape(2 * dps, -1).astype(F32)

time: 269 us -> 222 us (0.83)
  Pallas kernels: 230 us -> 183 us
    pallas_call x1, Pallas kernels: 113 us -> 86.8 us  [back(): pl.pallas_call(kernel, grid=(PAIRS + 1,), in_specs=in_specs, out_specs=ou...]
    pallas_call x1, Pallas kernels: 41.7 us -> 23.9 us  [attend(): pl.pallas_call(attend_kernel, grid=(PAIRS,), in_specs=[part(0), part(1),...]
    pallas_call x1, Pallas kernels: 64.7 us -> 61.1 us  [middle_links(): pl.pallas_call(functools.partial(middle_links_kernel, zs), grid=(zs,), in...]
  transfers between devices with their start and end apart: 1 -> 1, of which waited for: 0 -> 0; matrix products, arithmetic and copies ran while one was open for 5% -> 6% of each run, Pallas kernels for 0% -> 0%
where the time goes in v4:
time: 222 us; the launch traced here: 219 us
  Pallas kernels  183 us (82%)
  local copies, waits for them, and re-layouts  24 us (11%)
  between operations  5.58 us (3%)
  other arithmetic  3.8 us (2%)
    pallas_call x1, Pallas kernels, back(): pl.pallas_call(kernel, grid=(PAIRS + 1,), in_specs=in_specs, out_specs=ou...  86.8 us
    pallas_call x1, Pallas kernels, middle_links(): pl.pallas_call(functools.partial(middle_links_kernel, zs), grid=(zs,), in...  61.1 us
    pallas_call x1, Pallas kernels, attend(): pl.pallas_call(attend_kernel, grid=(PAIRS,), in_specs=[part(0), part(1),...  23.9 us
    unnamed x49, local copies, waits for them, and re-layouts  14.4 us
    pallas_call x1, Pallas kernels, project(): pl.pallas_call(project_kernel, grid=(6,), in_specs=[whole(own.shape), who...  11.1 us
  transfers between devices with their start and end apart: 1, of which 0 were waited for; matrix products, arithmetic and copies ran while one was open for 6% of the time, Pallas kernels for 0%

profile of v4, /device:TPU:10, one launch (start us, length us, event | category | flops | bytes accessed | tf_op | source)
XLA Modules:
  0.0 218.8 jit_solution(15403627965443641550)
XLA Ops:
  0.6 0.0 copy-start
  0.7 0.0 copy-start.16
  0.7 0.0 copy-start.12
  0.7 0.0 copy-start.13
  0.7 0.0 copy-start.11
  0.7 2.4 %dynamic-slice_bitcast_fusion.1 = (bf16[512,768]{1,0:T(8,128)(2,1)S(1)}, bf16[512,768]{1,0:T(8,128)(2,1)}) fusion(bf16[2,512,768]{2,1,0:T(8,128)(2,1)} %param.15, s32[]{:T(128)S(6)} %select_n.50, s32[]{:T(128)S(6)} %select_n.49), kind=kLoop, calls=%fused_computation.2 | loop fusion | bytes 3145736 | tf_op jit(solution)/shard_map/jit(dynamic_index_in_dim)/squeeze | solution.py:1774
  3.2 0.5 collective-permute-start
  3.7 0.0 copy-done.16
  3.7 0.6 dynamic_slice.40
  7.6 0.0 copy-done.12
  7.6 0.0 copy-done.13
  7.6 0.0 copy-done
  7.6 0.7 convolution_reduce_fusion
  8.3 0.0 copy-done.11
  8.4 0.0 copy-start.14
  8.4 0.0 copy-start.17
  8.4 0.0 copy-start.18
  8.4 0.0 copy-start.7
  8.4 5.9 %copy.42 = bf16[768,2304]{0,1:T(8,128)(2,1)} copy(bf16[768,2304]{1,0:T(8,128)(2,1)} %param.23) | data formatting | bytes 7077888 | tf_op args[8]
  14.3 0.1 add_convert_fusion.1
  14.5 0.0 copy-done.14
  14.5 0.0 copy-done.17
  14.5 0.6 dynamic_slice.42
  15.1 0.0 copy-done.18
  15.1 0.6 dynamic_slice.43
  17.0 0.7 broadcast_compare_fusion
  17.6 0.3 copy.43
  17.9 0.3 copy.44
  18.2 0.6 stack.50.vec_ref.refs_27_
  18.9 0.6 stack.59.vec_ref
  19.5 0.0 copy-done.7
  19.6 1.0 dynamic-slice_bitcast_fusion.cot_own
  20.5 1.2 multiply_sine_fusion
  21.8 0.9 and_select_fusion.span_ref
  22.7 0.0 collective-permute-done.rem_ref.tok_rem.refs_25_
  22.7 11.1 %project.1 = (bf16[768,1024]{1,0:T(8,128)(2,1)}, bf16[2304,1024]{1,0:T(8,128)(2,1)}) custom-call(bf16[512,768]{1,0:T(8,128)(2,1)} %get-tuple-element.75.own_ref.tok_own.refs_24_, bf16[512,768]{1,0:T(8,128)(2,1)} %collective-permute-done.rem_ref.tok_rem.refs_25_, f32[8,768]{1,0:T(8,128)} %stack.50.vec_ref.refs_27_, ...), custom_call_target="tpu_custom_call" | custom-call | flops 3623878656 | bytes 14680064 | tf_op jit(solution)/shard_map/project/pallas_call | solution.py:231
  33.8 23.9 %attend.1 = (bf16[768,1024]{1,0:T(8,128)(2,1)}, bf16[12,1024,1024]{2,1,0:T(8,128)(2,1)}, f32[6,8,1024]{2,1,0:T(8,128)}, bf16[512,768]{1,0:T(8,128)(2,1)}) custom-call(bf16[2304,1024]{1,0:T(8,128)(2,1)} %get-tuple-element.43.q_ref.k_ref.v_ref.refs_0_.refs_1_.refs_2_, bf16[2304,1024]{1,0:T(8,128)(2,1)} %get-tuple-element.43.q_ref.k_ref.v_ref.refs_0_.refs_1_.refs_2_, ...), custom_call_target="tpu_custom_call" | custom-call | flops 12884901888 | bytes 31457280 | tf_op jit(solution)/shard_map/attend/pallas_call | solution.py:314
  57.7 61.1 %middle_links.1 = (bf16[512,768]{1,0:T(8,128)(2,1)}, bf16[512,768]{1,0:T(8,128)(2,1)}, f32[1024,768]{1,0:T(8,128)}, bf16[768,1024]{1,0:T(8,128)(2,1)}, bf16[2,4,...) custom-call(bf16[768,1024]{1,0:T(8,128)(2,1)} %get-tuple-element.44., ...), custom_call_target="tpu_custom_call" | custom-call | flops 32614907904 | bytes 41943040 | tf_op jit(solution)/shard_map/middle_links/pallas_call | solution.py:808
  118.8 86.8 %back.1 = (bf16[2,512,768]{2,1,0:T(8,128)(2,1)}, f32[2,512,768]{2,1,0:T(8,128)}, f32[48,2304]{1,0:T(8,128)}, f32[48,768]{1,0:T(8,128)}, f32[48,3072]{1,0:T(8,128...) custom-call(bf16[2304,1024]{1,0:T(8,128)(2,1)} %get-tuple-element.43, ...), custom_call_target="tpu_custom_call" | custom-call | flops 33017561088 | bytes 62914560 | tf_op jit(solution)/shard_map/back/pallas_call | solution.py:1728
  205.6 0.0 copy-start.10
  205.6 0.0 copy-start.9
  205.6 0.0 copy-start.15
  205.6 1.1 copy.53
  206.7 0.0 copy-start.3
  206.8 0.1 fusion.18
  206.8 0.0 copy-done.10
  206.9 0.0 copy-done.9
  206.9 0.1 copy.47
  207.0 0.1 copy.48
  207.1 0.6 dynamic_slice.47
  207.7 0.6 dynamic_slice.49
  208.3 0.0 copy-done.15
  208.3 0.6 dynamic_slice.46
  208.9 0.1 multiply_cosine_fusion.1
  209.0 0.6 dynamic_slice.48
  209.6 0.7 fusion.2
  210.3 1.2 fusion
  211.6 1.1 copy.61
  212.7 1.3 copy-done.2
  214.0 1.7 copy.62
  215.7 0.8 copy.63
  216.5 0.7 copy.64
  217.1 0.8 copy.65
  217.9 0.8 copy.66
  (40 shorter events, 0.3 us)
Async XLA Ops:
  0.6 7.0 %copy-start = (bf16[128,4608]{1,0:T(8,128)(2,1)S(1)}, bf16[128,4608]{1,0:T(8,128)(2,1)}, u32[]{:S(2)}) copy-start(bf16[128,4608]{1,0:T(8,128)(2,1)} %param.20) | copy-start | bytes 3538948
  0.7 3.0 %copy-start.16 = (s32[2]{0:T(128)S(1)}, s32[2]{0:T(128)}, u32[]{:S(2)}) copy-start(s32[2]{0:T(128)} %param.17) | copy-start | bytes 28
  0.7 6.9 %copy-start.12 = (f32[768]{0:T(1024)S(1)}, f32[768]{0:T(1024)}, u32[]{:S(2)}) copy-start(f32[768]{0:T(1024)} %param.22) | copy-start | bytes 9220
  0.7 6.9 %copy-start.13 = (f32[768]{0:T(1024)S(1)}, f32[768]{0:T(1024)}, u32[]{:S(2)}) copy-start(f32[768]{0:T(1024)} %param.25) | copy-start | bytes 9220
  0.7 7.6 %copy-start.11 = (f32[4608]{0:T(1024)S(1)}, f32[4608]{0:T(1024)}, u32[]{:S(2)}) copy-start(f32[4608]{0:T(1024)} %param.21) | copy-start | bytes 55300
  3.2 19.5 %collective-permute-start = (bf16[512,768]{1,0:T(8,128)(2,1)S(1)}, bf16[512,768]{1,0:T(8,128)(2,1)}, u32[]{:S(2)}, u32[]{:S(2)}) collective-permute-start(bf16[512,768]{1,0:T(8,128)(2,1)S(1)} %get-tuple-element.74), channel_id=1, source_target_pairs={{0,1},{1,0},{2,3},{3,2},{4,5},{5,4},{6,7},{7,6},{8,9},{9,8},{10,11... | collective-permute-start | bytes 2359304 | tf_op jit(solution)/shard_map/ppermute | solution.py:1778
  8.4 6.1 %copy-start.14 = (f32[768]{0:T(1024)S(1)}, f32[768]{0:T(1024)}, u32[]{:S(2)}) copy-start(f32[768]{0:T(1024)} %param.29) | copy-start | bytes 9220
  8.4 6.1 %copy-start.17 = (s32[2]{0:T(128)S(1)}, s32[2]{0:T(128)}, u32[]{:S(2)}) copy-start(s32[2]{0:T(128)} %param.18) | copy-start | bytes 28
  8.4 6.7 %copy-start.18 = (s32[2]{0:T(128)S(1)}, s32[2]{0:T(128)}, u32[]{:S(2)}) copy-start(s32[2]{0:T(128)} %param.19) | copy-start | bytes 28
  8.4 11.1 %copy-start.7 = (bf16[2,512,768]{2,1,0:T(8,128)(2,1)S(1)}, bf16[2,512,768]{2,1,0:T(8,128)(2,1)}, u32[]{:S(2)}) copy-start(bf16[2,512,768]{2,1,0:T(8,128)(2,1)} %cot_ref.1) | copy-start | bytes 4718596
  205.6 1.2 copy-start.10
  205.6 1.2 copy-start.9
  205.6 2.6 %copy-start.15 = (f32[8,128]{1,0:T(8,128)S(1)}, f32[8,128]{1,0:T(8,128)}, u32[]{:S(2)}) copy-start(f32[8,128]{1,0:T(8,128)} %get-tuple-element.68) | copy-start | bytes 12292
  206.7 4.8 %copy-start.3 = (bf16[2,512,768]{2,1,0:T(8,128)(2,1)S(1)}, bf16[2,512,768]{2,1,0:T(8,128)(2,1)}, u32[]{:S(2)}) copy-start(bf16[2,512,768]{2,1,0:T(8,128)(2,1)} %get-tuple-element.110) | copy-start | bytes 4718596
  211.6 2.5 %copy-start.2 = (f32[2,512,768]{2,1,0:T(8,128)S(1)}, f32[2,512,768]{2,1,0:T(8,128)}, u32[]{:S(2)}) copy-start(f32[2,512,768]{2,1,0:T(8,128)} %get-tuple-element.111) | copy-start | bytes 9437188
  214.0 1.7 copy-start.6
  214.0 2.4 %copy-start.8 = (f32[48,768]{1,0:T(8,128)S(1)}, f32[48,768]{1,0:T(8,128)}, u32[]{:S(2)}) copy-start(f32[48,768]{1,0:T(8,128)} %get-tuple-element.116) | copy-start | bytes 442372
  214.0 4.7 %copy-start.1 = (bf16[128,4608]{1,0:T(8,128)(2,1)S(1)}, bf16[128,4608]{1,0:T(8,128)(2,1)}, u32[]{:S(2)}) copy-start(bf16[128,4608]{1,0:T(8,128)(2,1)} %param.20) | copy-start | bytes 3538948
  215.7 1.4 copy-start.5
  215.7 2.2 %copy-start.4 = (f32[192,768]{1,0:T(8,128)S(1)}, f32[192,768]{1,0:T(8,128)}, u32[]{:S(2)}) copy-start(f32[192,768]{1,0:T(8,128)} %get-tuple-element.120) | copy-start | bytes 1769476

commit v5 on v4

--- a/solution.py
+++ b/solution.py
@@ -3,6 +3,7 @@
 
 import jax
 import jax.numpy as jnp
+import numpy as np
 from jax import lax
 from jax.experimental import pallas as pl
 from jax.experimental.pallas import tpu as pltpu
@@ -188,71 +189,222 @@
     return pl.BlockSpec(shape, lambda *_: zeros, pipeline_mode=pl.Buffered(1))
 
 
-def project_kernel(own_ref, rem_ref, vec_ref, cos_ref, sin_ref, w_ref, act_ref, out_ref):
+def split_three(x):
+    parts = []
+    for _ in range(3):
+        low = x.astype(BF)
+        parts.append(low)
+        x = x - low.astype(F32)
+    return parts
+
+
+def features_of(angles, is_sin):
+    raw = jnp.where(is_sin, jnp.sin(angles), jnp.cos(angles))
+    return raw / (1.0 + jnp.exp(-raw))
+
+
+def project_kernel(
+    time_ref,
+    start_ref,
+    extent_ref,
+    tokens_ref,
+    cos_ref,
+    sin_ref,
+    w_ada_ref,
+    b_ada_ref,
+    gain_one_ref,
+    gain_two_ref,
+    b_down_ref,
+    w_ref,
+    act_ref,
+    out_ref,
+    w_t_ref,
+    rem_ref,
+    vec_one_ref,
+    vec_two_ref,
+    span_ref,
+    cos_out,
+    sin_out,
+    own,
+    rem,
+    w_t,
+    qkv,
+    sems,
+):
     step = pl.program_id(0)
-    half, _ = own_ref.shape
-    tile = 256
+    half, width = own.shape
+    rows = w_t_ref.shape[0]
+    tile = 128
+    chunk = half // 2
+    x = lax.axis_index("seq")
+    keep = pltpu.make_async_copy(tokens_ref.at[x], own, sems.at[0])
+    cross = [
+        remote(
+            tokens_ref.at[1 - x, k * chunk : (k + 1) * chunk],
+            rem.at[k * chunk : (k + 1) * chunk],
+            sems.at[1 + k],
+            sems.at[3 + k],
+            seq_partner(),
+        )
+        for k in range(2)
+    ]
+    spans = (slice(0, half), slice(half, half + chunk), slice(half + chunk, 2 * half))
+    store = [
+        pltpu.make_async_copy(qkv.at[:, span], out_ref.at[:, span], sems.at[5 + k])
+        for k, span in enumerate(spans)
+    ]
+
+    def norm(src, first, size, start):
+        scale, shift = vec_one_ref[0:1, :], vec_one_ref[1:2, :]
+        for t in range(0, size, tile):
+            n, _ = norm_parts(src[first + t : first + t + tile, :].astype(F32))
+            act_ref[:, start + t : start + t + tile] = (n * scale + shift).astype(BF).T
 
     @pl.when(step == 0)
     def _():
-        scale = vec_ref[0:1, :]
-        shift = vec_ref[1:2, :]
-        for part, ref in enumerate((own_ref, rem_ref)):
-            for t in range(half // tile):
-                n, _ = norm_parts(ref[t * tile : (t + 1) * tile, :].astype(F32))
-                act = (n * scale + shift).astype(BF)
-                start = part * half + t * tile
-                act_ref[:, start : start + tile] = act.T
-
-    proj = mm(w_ref[...], act_ref[...])
-    heads = proj.shape[0] // HD
-    tokens = proj.shape[1]
-
-    @pl.when(step < 4)
-    def _():
-        factor = jnp.where(step < 2, HD**-0.5, 1.0)
-        cos = cos_ref[...] * factor
-        sin = sin_ref[...] * factor
-        for h in range(heads):
+        greet(seq_partner())
+        for copy in cross:
+            copy.start()
+        keep.start()
+        pairs = w_ada_ref.shape[0] // 2
+        time = time_ref[x]
+        lane = lax.broadcasted_iota(jnp.int32, (8, 2 * pairs), 1)
+        place = jnp.where(lane < pairs, lane, lane - pairs).astype(F32)
+        frequency = jnp.exp(-math.log(10000.0) * place / pairs)
+        cond = features_of(time.astype(F32) * frequency, lane >= pairs)
+        modulation = b_ada_ref[...].reshape(1, 6 * width)
+        for part in split_three(cond):
+            modulation = modulation + mm(part, w_ada_ref[...])[0:1, :]
+        pieces = [modulation[:, k * width : (k + 1) * width] for k in range(6)]
+        shift_one, scale_one, gate_one, shift_two, scale_two, gate_two = pieces
+        gain_one, gain_two = (ref[...].reshape(1, width) for ref in (gain_one_ref, gain_two_ref))
+        zeros = jnp.zeros((1, width), F32)
+        first = (gain_one * (1.0 + scale_one), shift_one, gain_one, scale_one)
+        for k, row in enumerate(first + (zeros,) * 4):
+            vec_one_ref[k : k + 1, :] = row
+        lanes = lax.broadcasted_iota(jnp.int32, (1, width), 1)
+        stamp = jnp.where(lanes == 0, time // 32, jnp.where(lanes == 1, lax.rem(time, 32), 0))
+        second = (
+            gate_one,
+            gain_two * (1.0 + scale_two),
+            shift_two,
+            gate_two,
+            b_down_ref[...].reshape(1, width),
+            gain_two,
+            scale_two,
+            stamp.astype(F32),
+        )
+        for k, row in enumerate(second):
+            vec_two_ref[k : k + 1, :] = row
+        begin, end = start_ref[x], start_ref[x] + extent_ref[x]
+        index = lax.broadcasted_iota(jnp.int32, (half, 1), 0)
+        for part, where in enumerate((x, 1 - x)):
+            place = index + where * half
+            inside = (place >= begin) & (place < end)
+            span_ref[part * half : (part + 1) * half, :] = jnp.where(inside, 2.0, 0.5)
+            cos_out[:, part * half : (part + 1) * half] = cos_ref[where]
+            sin_out[:, part * half : (part + 1) * half] = sin_ref[where]
+        keep.wait()
+        norm(own, 0, half, 0)
+
+    def rotated(proj, block, cols, factor):
+        cos, sin = cos_out[:, cols] * factor, sin_out[:, cols] * factor
+        parts = []
+        for h in range(rows // HD):
             a = proj[h * HD : h * HD + HD // 2]
             b = proj[h * HD + HD // 2 : (h + 1) * HD]
-            out_ref[h * HD : h * HD + HD // 2, :] = (a * cos - b * sin).astype(BF)
-            out_ref[h * HD + HD // 2 : (h + 1) * HD, :] = (b * cos + a * sin).astype(BF)
-
-    @pl.when(step >= 4)
-    def _():
-        out_ref[...] = proj.astype(BF)
-
-
-def project(own, rem, vec, cos_t, sin_t, w_qkv_t):
-    half, width = own.shape
-    tokens = 2 * half
+            parts += [(a * cos - b * sin).astype(BF), (b * cos + a * sin).astype(BF)]
+        qkv[block, cols] = jnp.concatenate(parts, axis=0)
+
+    @pl.when(step < 6)
+    def _():
+        block = rows_of(rows, step)
+        flipped = w_ref[...].T
+        w_t[block, :] = flipped
+        w_t_ref[...] = flipped
+        proj = mm(flipped, act_ref[:, spans[0]])
+
+        @pl.when(step < 4)
+        def _():
+            rotated(proj, block, spans[0], jnp.where(step < 2, HD**-0.5, 1.0))
+
+        @pl.when(step >= 4)
+        def _():
+            qkv[block, spans[0]] = proj.astype(BF)
+
+    for k in range(2):
+
+        @pl.when(step == 6 + k)
+        def _(k=k):
+            store[k].start()
+            cross[k].wait()
+            got = slice(k * chunk, (k + 1) * chunk)
+            rem_ref[got, :] = rem[got, :]
+            norm(rem, k * chunk, chunk, half + k * chunk)
+            cols = spans[1 + k]
+            for turn in range(6):
+                block = slice(turn * rows, (turn + 1) * rows)
+                proj = mm(w_t[block, :], act_ref[:, cols])
+                if turn < 4:
+                    rotated(proj, block, cols, HD**-0.5 if turn < 2 else 1.0)
+                else:
+                    qkv[block, cols] = proj.astype(BF)
+            if k == 1:
+                store[2].start()
+                for copy in store:
+                    copy.wait()
+
+
+def rotary_constants(length):
+    angles = np.arange(length, dtype=np.float32)[None, :] * np.exp(
+        -math.log(10000.0) * np.arange(HD // 2, dtype=np.float32) / np.float32(HD // 2)
+    ).astype(np.float32)[:, None]
+    angles = angles.reshape(HD // 2, 2, length // 2).transpose(1, 0, 2).astype(np.float64)
+    return np.cos(angles).astype(np.float32), np.sin(angles).astype(np.float32)
+
+
+def project(tokens, time_index, span_starts, span_lengths, w_ada, b_ada, gains, b_down, w_qkv):
+    _, half, width = tokens.shape
+    length = 2 * half
     blk = width // 2
+    cos_all, sin_all = rotary_constants(length)
+    smem = pl.BlockSpec(memory_space=pltpu.SMEM)
+    outs = [
+        ((width, length), BF),
+        ((3 * width, length), BF),
+        ((3 * width, width), BF),
+        ((half, width), BF),
+        ((8, width), F32),
+        ((8, width), F32),
+        ((length, 1), F32),
+        ((HD // 2, length), F32),
+        ((HD // 2, length), F32),
+    ]
+    out_specs = [once(shape) for shape, _ in outs]
+    out_specs[1] = ANY
+    out_specs[2] = pl.BlockSpec((blk, width), lambda i: (jnp.minimum(i, 5), 0))
+    rows = [b_ada, *gains, b_down]
     return pl.pallas_call(
         project_kernel,
-        grid=(6,),
-        in_specs=[
-            whole(own.shape),
-            whole(rem.shape),
-            whole(vec.shape),
-            whole(cos_t.shape),
-            whole(sin_t.shape),
-            pl.BlockSpec((blk, width), lambda i: (i, 0)),
+        grid=(8,),
+        in_specs=[smem, smem, smem, ANY, once(cos_all.shape), once(sin_all.shape), once(w_ada.shape)]
+        + [once(r.shape) for r in rows]
+        + [pl.BlockSpec((width, blk), lambda i: (0, jnp.minimum(i, 5)))],
+        out_specs=out_specs,
+        out_shape=[jax.ShapeDtypeStruct(*o) for o in outs],
+        scratch_shapes=[
+            pltpu.VMEM((half, width), BF),
+            pltpu.VMEM((half, width), BF),
+            pltpu.VMEM((3 * width, width), BF),
+            pltpu.VMEM((3 * width, length), BF),
+            pltpu.SemaphoreType.DMA((8,)),
         ],
-        out_specs=[
-            whole((width, tokens)),
-            pl.BlockSpec((blk, tokens), lambda i: (i, 0)),
-        ],
-        out_shape=[
-            jax.ShapeDtypeStruct((width, tokens), BF),
-            jax.ShapeDtypeStruct((3 * width, tokens), BF),
-        ],
-        compiler_params=params(),
+        compiler_params=params(collective_id=6),
         cost_estimate=pl.CostEstimate(
-            flops=6 * tokens * width * width, bytes_accessed=14 << 20, transcendentals=0
+            flops=6 * length * width * width, bytes_accessed=20 << 20, transcendentals=0
         ),
         name="project",
-    )(own, rem, vec, cos_t, sin_t, w_qkv_t)
+    )(time_index, span_starts, span_lengths, tokens, cos_all, sin_all, w_ada, *rows, w_qkv)
 
 
 def attend_kernel(
@@ -530,9 +682,9 @@
 def middle_links_kernel(
     zs,
     att_ref,
-    tok_own,
+    tokens_ref,
     tok_rem,
-    cot_own,
+    cot_ref,
     cot_rem,
     span_ref,
     vec_ref,
@@ -592,6 +744,7 @@
 
     links = Links(sems, zs)
     x, y, z, c = links.x, links.y, links.z, links.c
+    tok_own, cot_own = tokens_ref.at[x], cot_ref.at[x]
     tiles = range(steps - 1)
 
     def swaps(src, dst, device):
@@ -776,7 +929,7 @@
 
 
 def middle_links(
-    att_t, tok_own, tok_rem, cot_own, cot_rem, span, vec, b_up, w_out, w_up, w_down, zs
+    att_t, tok_all, tok_rem, cot_all, cot_rem, span, vec, b_up, w_out, w_up, w_down, zs
 ):
     width, tokens = att_t.shape
     half = tokens // 2
@@ -810,9 +963,9 @@
         grid=(zs,),
         in_specs=[
             once(att_t.shape),
-            once(tok_own.shape),
+            once(tok_all.shape),
             once(tok_rem.shape),
-            once(cot_own.shape),
+            once(cot_all.shape),
             once(cot_rem.shape),
             once(span.shape),
             once(vec.shape),
@@ -850,7 +1003,7 @@
             transcendentals=tokens * ff,
         ),
         name="middle_links",
-    )(att_t, tok_own, tok_rem, cot_own, cot_rem, span, vec, b_up, w_out, w_up, w_down)
+    )(att_t, tok_all, tok_rem, cot_all, cot_rem, span, vec, b_up, w_out, w_up, w_down)
 
 
 def attend_back_kernel(
@@ -1193,7 +1346,7 @@
         for p in (
             (act_in, act_ref),
             (w_in, w_ref),
-            (tok_own_in, tok_own),
+            (tok_own_in.at[x], tok_own),
             (tok_rem_in, tok_rem),
             (dx_in, dx_ref),
         )
@@ -1711,7 +1864,7 @@
         vm(*sums.shape, kind=F32),
         vm(*sum_late, kind=F32),
     ]
-    scratch += [vm(*a.shape, kind=a.dtype) for a in fetched]
+    scratch += [vm(*a.shape[-2:], kind=a.dtype) for a in fetched]
     scratch += [vm(half, width, kind=F32)]
     flat, tree = jax.tree.flatten(scratch)
     n_in, n_out = len(in_specs), len(out_specs)
@@ -1773,55 +1926,22 @@
     def pick(x, i):
         return lax.dynamic_index_in_dim(x, i, 0, keepdims=False)
 
-    tok_own, tok_send = pick(tokens, rank), pick(tokens, 1 - rank)
-    cot_own = pick(cotangent, rank)
-    tok_rem = lax.ppermute(tok_send, "seq", swap)
-
-    here = jnp.arange(half, dtype=jnp.int32)
-    place = jnp.concatenate([rank * half + here, (1 - rank) * half + here])
-    frequency = jnp.exp(-math.log(10000.0) * jnp.arange(HD // 2, dtype=F32) / (HD // 2))
-    angles = frequency[:, None] * place.astype(F32)[None, :]
-    cos_t, sin_t = jnp.cos(angles), jnp.sin(angles)
-    start, extent = pick(span_starts, rank), pick(span_lengths, rank)
-    span = jnp.where((place >= start) & (place < start + extent), 2.0, 0.5).astype(F32)[:, None]
-
     time_own = lax.dynamic_slice_in_dim(time_index, rank, 1)
-    cond_act = jax.nn.silu(time_features(time_own, w_ada.shape[0] // 2))
-    modulation = (
-        jnp.dot(cond_act, w_ada.astype(F32), precision=lax.Precision.HIGHEST)[0] + b_ada
-    )
-    shift_one, scale_one, gate_one, shift_two, scale_two, gate_two = jnp.split(modulation, 6)
-    zeros = jnp.zeros_like(shift_one)
-    vec_one = jnp.stack(
-        [gain_one * (1.0 + scale_one), shift_one, gain_one, scale_one, zeros, zeros, zeros, zeros]
-    )
-    vec_two = jnp.stack(
-        [
-            gate_one,
-            gain_two * (1.0 + scale_two),
-            shift_two,
-            gate_two,
-            b_down,
-            gain_two,
-            scale_two,
-            jnp.pad(jnp.concatenate([time_own // 32, time_own % 32]).astype(F32), (0, width - 2)),
-        ]
-    )
-    w_qkv_t = w_qkv.T
-
     dp, dps = lax.axis_index("dp"), lax.axis_size("dp")
     ff = w_up.shape[1]
     zs = dps // 4
     linked = zs == 4 and dps == 16 and width % (64 * zs) == 0 and ff == zs * width
 
-    act_t, qkv_t = project(tok_own, tok_rem, vec_one, cos_t, sin_t, w_qkv_t)
+    act_t, qkv_t, w_qkv_t, tok_rem, vec_one, vec_two, span, cos_t, sin_t = project(
+        tokens, time_index, span_starts, span_lengths, w_ada, b_ada, (gain_one, gain_two), b_down, w_qkv
+    )
     att_t, e, linv, cot_rem = attend(qkv_t, cotangent)
     if linked:
         out_own, out_rem, dx, d_att_t, raw_out, raw_up, raw_down, *partial, mod, sums = middle_links(
-            att_t, tok_own, tok_rem, cot_own, cot_rem, span, vec_two, b_up[None], w_out, w_up, w_down, zs
+            att_t, tokens, tok_rem, cotangent, cot_rem, span, vec_two, b_up[None], w_out, w_up, w_down, zs
         )
         ins = (qkv_t, att_t, d_att_t, e, linv, cos_t, sin_t, out_own, out_rem, *partial)
-        ins += (raw_up, raw_out, raw_down, mod, sums, act_t, w_qkv_t, tok_own, tok_rem, dx, vec_one)
+        ins += (raw_up, raw_out, raw_down, mod, sums, act_t, w_qkv_t, tokens, tok_rem, dx, vec_one)
         output, grad_tokens, *shards, mod_early, mod_late, sum_early, sum_late = back(ins, zs, ff)
         mod_early = mod_early.reshape(2 * dps, -1).astype(F32)
         mod_late = mod_late.reshape(2 * dps, -1).astype(F32)
@@ -1831,6 +1951,7 @@
             [sum_late.reshape(-1)[:width], sum_early.reshape(-1)[: 2 * width + ff]]
         )
     else:
+        tok_own, cot_own = pick(tokens, rank), pick(cotangent, rank)
         out_own, out_rem, dx, d_att_t, g_out, g_up, g_down, g_bup, sums_two = middle(
             att_t, tok_own, tok_rem, cot_own, cot_rem, span, vec_two, b_up[None], w_out, w_up, w_down
         )

time: 222 us -> 215 us (0.968)
  Pallas kernels: 183 us -> 197 us
  local copies, waits for them, and re-layouts: 24 us -> 11.7 us
  between operations: 5.58 us -> 0.77 us
  other arithmetic: 3.8 us -> 0.88 us
    pallas_call x1, Pallas kernels: 11.1 us -> 25.7 us  [project(): pl.pallas_call(project_kernel, grid=(8,), in_specs=[smem, smem, smem, ANY...]
    unnamed x49 -> x26, local copies, waits for them, and re-layouts: 14.4 us -> 8.43 us
    squeeze x2 -> x0, local copies, waits for them, and re-layouts: 3.43 us -> none  [pick(): return lax.dynamic_index_in_dim(x, i, 0, keepdims=False)]
  transfers between devices with their start and end apart: 1 -> 0, of which waited for: 0 -> 0; matrix products, arithmetic and copies ran while one was open for 6% -> 0% of each run, Pallas kernels for 0% -> 0%
where the time goes in v5:
time: 215 us; the launch traced here: 212 us
  Pallas kernels  197 us (92%)
  local copies, waits for them, and re-layouts  11.7 us (5%)
    pallas_call x1, Pallas kernels, back(): pl.pallas_call(kernel, grid=(PAIRS + 1,), in_specs=in_specs, out_specs=ou...  86.8 us
    pallas_call x1, Pallas kernels, middle_links(): pl.pallas_call(functools.partial(middle_links_kernel, zs), grid=(zs,), in...  61.5 us
    pallas_call x1, Pallas kernels, project(): pl.pallas_call(project_kernel, grid=(8,), in_specs=[smem, smem, smem, ANY...  25.7 us
    pallas_call x1, Pallas kernels, attend(): pl.pallas_call(attend_kernel, grid=(PAIRS,), in_specs=[part(0), part(1),...  22.9 us
    unnamed x26, local copies, waits for them, and re-layouts  8.43 us

profile of v5, /device:TPU:10, one launch (start us, length us, event | category | flops | bytes accessed | tf_op | source)
XLA Modules:
  0.0 211.6 jit_solution(14979772074739070679)
XLA Ops:
  0.6 25.7 %project.1 = (bf16[768,1024]{1,0:T(8,128)(2,1)}, bf16[2304,1024]{1,0:T(8,128)(2,1)}, bf16[2304,768]{1,0:T(8,128)(2,1)}, bf16[512,768]{1,0:T(8,128)(2,1)}, f32[8,...) custom-call(s32[2]{0:T(128)} %time_ref.1, s32[2]{0:T(128)} %start_ref.1, ...), custom_call_target="tpu_custom_call" | custom-call | flops 3623878656 | bytes 20971520 | tf_op jit(solution)/shard_map/project/pallas_call | solution.py:387
  26.4 22.9 %attend.1 = (bf16[768,1024]{1,0:T(8,128)(2,1)}, bf16[12,1024,1024]{2,1,0:T(8,128)(2,1)}, f32[6,8,1024]{2,1,0:T(8,128)}, bf16[512,768]{1,0:T(8,128)(2,1)}) custom-call(bf16[2304,1024]{1,0:T(8,128)(2,1)} %get-tuple-element.50.q_ref.k_ref.v_ref.refs_0_.refs_1_.refs_2_, bf16[2304,1024]{1,0:T(8,128)(2,1)} %get-tuple-element.50.q_ref.k_ref.v_ref.refs_0_.refs_1_.refs_2_, ...), custom_call_target="tpu_custom_call" | custom-call | flops 12884901888 | bytes 31457280 | tf_op jit(solution)/shard_map/attend/pallas_call | solution.py:466
  49.3 61.5 %middle_links.1 = (bf16[512,768]{1,0:T(8,128)(2,1)}, bf16[512,768]{1,0:T(8,128)(2,1)}, f32[1024,768]{1,0:T(8,128)}, bf16[768,1024]{1,0:T(8,128)(2,1)}, bf16[2,4,...) custom-call(bf16[768,1024]{1,0:T(8,128)(2,1)} %get-tuple-element.51., ...), custom_call_target="tpu_custom_call" | custom-call | flops 32614907904 | bytes 41943040 | tf_op jit(solution)/shard_map/middle_links/pallas_call | solution.py:961
  110.8 86.8 %back.1 = (bf16[2,512,768]{2,1,0:T(8,128)(2,1)}, f32[2,512,768]{2,1,0:T(8,128)}, f32[48,2304]{1,0:T(8,128)}, f32[48,768]{1,0:T(8,128)}, f32[48,3072]{1,0:T(8,128...) custom-call(bf16[2304,1024]{1,0:T(8,128)(2,1)} %get-tuple-element.50, ...), custom_call_target="tpu_custom_call" | custom-call | flops 33017561088 | bytes 62914560 | tf_op jit(solution)/shard_map/back/pallas_call | solution.py:1881
  197.7 0.0 copy-start.6
  197.7 0.8 slice_bitcast_fusion.1
  198.5 0.6 dynamic_slice.21
  199.0 0.6 dynamic_slice.23
  199.6 0.6 dynamic_slice.20
  200.2 1.0 copy.37
  201.3 0.0 copy-start.7
  201.3 0.0 copy-start.1
  201.3 0.0 copy-done.6
  201.4 0.7 fusion.2
  202.1 0.1 fusion.12
  202.2 0.1 copy.31
  202.2 0.1 copy.32
  202.3 0.1 multiply_cosine_fusion
  202.5 1.2 fusion
  203.7 0.0 copy-done.7
  203.7 0.6 dynamic_slice.22
  204.4 0.0 copy-done.1
  204.4 0.0 copy-start
  204.4 1.1 copy.45
  205.5 1.3 copy-done
  206.8 0.0 copy-start.4
  206.8 0.0 copy-start.5
  206.8 1.7 copy.46
  208.5 0.0 copy-done.4
  208.5 0.0 copy-start.3
  208.5 0.0 copy-start.2
  208.5 0.8 copy.47
  209.3 0.0 copy-done.5
  209.3 0.7 copy.48
  209.9 0.0 copy-done.3
  209.9 0.8 copy.49
  210.7 0.0 copy-done.2
  210.7 0.8 copy.50
  (6 shorter events, 0.1 us)
Async XLA Ops:
  197.7 3.6 %copy-start.6 = (bf16[4,2,2,2,16,128]{5,4,3,2,1,0:T(8,128)(2,1)S(1)}, bf16[4,2,2,2,16,128]{5,4,3,2,1,0:T(8,128)(2,1)}, u32[]{:S(2)}) copy-start(bf16[4,2,2,2,16,128]{5,4,3,2,1,0:T(8,128)(2,1)} %get-tuple-element.81) | copy-start | bytes 393220
  201.3 2.5 %copy-start.7 = (f32[40,128]{1,0:T(8,128)S(1)}, f32[40,128]{1,0:T(8,128)}, u32[]{:S(2)}) copy-start(f32[40,128]{1,0:T(8,128)} %get-tuple-element.85) | copy-start | bytes 61444
  201.3 3.1 %copy-start.1 = (bf16[2,512,768]{2,1,0:T(8,128)(2,1)S(1)}, bf16[2,512,768]{2,1,0:T(8,128)(2,1)}, u32[]{:S(2)}) copy-start(bf16[2,512,768]{2,1,0:T(8,128)(2,1)} %get-tuple-element.107) | copy-start | bytes 4718596
  204.4 2.5 %copy-start = (f32[2,512,768]{2,1,0:T(8,128)S(1)}, f32[2,512,768]{2,1,0:T(8,128)}, u32[]{:S(2)}) copy-start(f32[2,512,768]{2,1,0:T(8,128)} %get-tuple-element.108) | copy-start | bytes 9437188
  206.8 1.7 copy-start.4
  206.8 2.4 %copy-start.5 = (f32[48,768]{1,0:T(8,128)S(1)}, f32[48,768]{1,0:T(8,128)}, u32[]{:S(2)}) copy-start(f32[48,768]{1,0:T(8,128)} %get-tuple-element.113) | copy-start | bytes 442372
  208.5 1.4 copy-start.3
  208.5 2.2 %copy-start.2 = (f32[192,768]{1,0:T(8,128)S(1)}, f32[192,768]{1,0:T(8,128)}, u32[]{:S(2)}) copy-start(f32[192,768]{1,0:T(8,128)} %get-tuple-element.117) | copy-start | bytes 1769476

commit v6 on v5

--- a/solution.py
+++ b/solution.py
@@ -101,6 +101,9 @@
         self.across = (dp + 2 - 4 * self.y, self.x)
         self.facing = (dp, 1 - self.x)
         self.far = [lax.rem(self.z + k, zs) for k in range(1, zs)]
+        self.upper, self.lower = self.z // 2, lax.rem(self.z, 2)
+        self.near = self.at_z(2 * self.upper + 1 - self.lower)
+        self.beyond = self.at_z(2 * (1 - self.upper) + self.lower)
 
     def at_z(self, f):
         return (f * 4 + 2 * self.y + self.c, self.x)
@@ -136,31 +139,33 @@
 
         return start, wait
 
-    def gather(self, src, dst, goal):
-        sem = self.take(1 + self.zs)
-
-        def make(slot):
-            return remote(
-                src(), dst(slot), self.sems.at[sem], self.sems.at[sem + 1 + slot], self.at_z(goal)
-            )
+    def to_goal(self, src, dst, goal):
+        upper, lower = goal // 2, goal % 2
+        near = self.swap(src, lambda: dst().at[0], self.near)
+        beyond = self.swap(src, lambda: dst().at[1], self.beyond)
+        on_side = self.lower == lower
 
         def start():
-            pl.when(self.z != goal)(lambda: make(self.z).start())
-
-        def wait():
-            pl.when(self.z != goal)(lambda: make(self.z).wait_send())
-
-            @pl.when(self.z == goal)
+            pl.when(self.lower != lower)(lambda: near().start())
+
+        def middle():
+            pl.when(self.lower != lower)(lambda: near().wait_send())
+
+            @pl.when(on_side)
             def _():
-                for f in self.far:
-                    make(f).wait_recv()
-
-        return start, wait
-
-
-def add_to(dst, src, lead):
-    for index in lead:
-        dst[index] = dst[index] + src[index]
+                near().wait_recv()
+                src()[...] = src()[...] + dst()[0]
+                pl.when(self.upper != upper)(lambda: beyond().start())
+
+        def finish():
+            pl.when(on_side & (self.upper != upper))(lambda: beyond().wait_send())
+
+            @pl.when(on_side & (self.upper == upper))
+            def _():
+                beyond().wait_recv()
+                src()[...] = src()[...] + dst()[1]
+
+        return start, middle, finish
 
 
 def grid_of(*sizes):
@@ -750,14 +755,16 @@
     def swaps(src, dst, device):
         return [links.swap(lambda j=j: src(j), lambda j=j: dst.at[j], device) for j in tiles]
 
-    up_to_core = swaps(lambda j: g_up_ref.at[:, :, :, 1 - c], up_core, links.core)
+    up_to_core = swaps(lambda j: g_up_ref.at[:, :, :, :, 1 - c], up_core, links.core)
     down_to_core = swaps(lambda j: g_down_ref.at[:, 1 - c], down_core, links.core)
     up_to_side = swaps(lambda j: up_core.at[j, 1 - x], up_side, links.facing)
     down_to_y = swaps(lambda j: down_core.at[j, 1 - y], down_y, links.across)
-    up_to_y = swaps(lambda j: up_core.at[j, x, :, 1 - y], up_y, links.across)
+    up_to_y = swaps(lambda j: up_core.at[j, x, :, :, 1 - y], up_y, links.across)
     down_to_side = swaps(lambda j: down_core.at[j, y, 1 - x], down_side, links.facing)
-    down_far = links.gather(lambda: down_core.at[0, y, x], lambda slot: down_z.at[slot], 0)
-    up_far = links.spread(lambda f: up_core.at[0, x, f, y], lambda slot: up_z.at[slot])
+    h, b = links.upper, links.lower
+    down_goal = links.to_goal(lambda: down_core.at[0, y, x], lambda: down_z, 0)
+    up_near = links.swap(lambda: up_core.at[0, x, :, 1 - b, y], lambda: up_z.at[0:2], links.near)
+    up_beyond = links.swap(lambda: up_core.at[0, x, 1 - h, b, y], lambda: up_z.at[2], links.beyond)
 
     def core_stage(j):
         up_to_core[j]().start()
@@ -765,21 +772,21 @@
 
     def first_stage(j):
         up_to_core[j]().wait()
-        for h, a, b in grid_of(2, zs, 2):
-            up_core[j, h, a, b] = up_core[j, h, a, b] + g_up_ref[h, a, b, c]
+        for i in grid_of(2, 2, 2, 2):
+            up_core[(j, *i)] = up_core[(j, *i)] + g_up_ref[(*i, c)]
         up_to_side[j]().start()
         down_to_core[j]().wait()
-        for b, h in grid_of(2, 2):
-            down_core[j, b, h] = down_core[j, b, h] + g_down_ref[b, c, h]
+        for i, k in grid_of(2, 2):
+            down_core[j, i, k] = down_core[j, i, k] + g_down_ref[i, c, k]
         down_to_y[j]().start()
 
     def first_done(j):
         up_to_side[j]().wait()
-        for a, b in grid_of(zs, 2):
-            up_core[j, x, a, b] = up_core[j, x, a, b] + up_side[j, a, b]
+        for i in grid_of(2, 2, 2):
+            up_core[(j, x, *i)] = up_core[(j, x, *i)] + up_side[(j, *i)]
         down_to_y[j]().wait()
-        for h in range(2):
-            down_core[j, y, h] = down_core[j, y, h] + down_y[j, h]
+        for k in range(2):
+            down_core[j, y, k] = down_core[j, y, k] + down_y[j, k]
 
     def second_stage(j):
         first_done(j)
@@ -788,15 +795,22 @@
 
     def second_done(j):
         up_to_y[j]().wait()
-        for a in range(zs):
-            up_core[j, x, a, y] = up_core[j, x, a, y] + up_y[j, a]
+        for i in grid_of(2, 2):
+            up_core[(j, x, *i, y)] = up_core[(j, x, *i, y)] + up_y[(j, *i)]
         down_to_side[j]().wait()
         down_core[j, y, x] = down_core[j, y, x] + down_side[j]
 
     def third_stage():
         second_done(0)
-        up_far[0]()
-        down_far[0]()
+        up_near().start()
+        down_goal[0]()
+
+    def fourth_stage():
+        up_near().wait()
+        for k in range(2):
+            up_core[0, x, k, b, y] = up_core[0, x, k, b, y] + up_z[k]
+        up_beyond().start()
+        down_goal[1]()
 
     @pl.when(step == 0)
     def _():
@@ -853,12 +867,12 @@
     g_down_flat = g_down_ref.reshape(width, width)
     g_up_flat = g_up_ref.reshape(2, width, cut)
 
-    def grads(k, carry):
-        outs = rows_of(chunk_out, k)
+    def grads(turn, carry):
+        outs = rows_of(chunk_out, turn)
         g_down_flat[outs, :] = mm(hidden[:, outs], d_down[...], TN).astype(BF)
         g_up = mm(act_two[:, outs], d_up[...], TN).astype(BF)
-        for h in range(2):
-            g_up_flat[h, outs, :] = g_up[:, h * cut : (h + 1) * cut]
+        for k in range(2):
+            g_up_flat[k, outs, :] = g_up[:, k * cut : (k + 1) * cut]
         return carry
 
     lax.fori_loop(0, 3, grads, 0)
@@ -878,6 +892,7 @@
 
     @pl.when(step == steps - 1)
     def _():
+        fourth_stage()
         zero = jnp.zeros((1, width), F32)
         s_gate_two, s_shift, s_pull, s_gate_one, s_bdown = zero, zero, zero, zero, zero
         for part, (cot, out) in enumerate(((cot_own, out_own), (cot_rem, out_rem))):
@@ -906,22 +921,16 @@
         put_rows(sum_ref, 0, s_pull * (1.0 + scale_two))
         put_rows(sum_ref, lines, s_bdown)
         g_out = mm(att_ref[...], d_branch[...]).astype(BF)
-        for h in range(2):
-            g_out_ref[h] = g_out[:, h * cut : (h + 1) * cut].reshape(g_out_ref.shape[1:])
+        for k in range(2):
+            g_out_ref[k] = g_out[:, k * cut : (k + 1) * cut].reshape(g_out_ref.shape[1:])
         d_att_ref[...] = mm(w_out_ref[...], d_branch[...], NT).astype(BF)
-        up_far[1]()
-        total = up_core[0, x, z, y].astype(F32)
-        for f in links.far:
-            total += up_z[f].astype(F32)
-        up_last_ref[...] = total.astype(BF)
-        down_far[1]()
-        total = down_core[0, y, x].astype(F32)
-        for f in links.far:
-            total += down_z[f].astype(F32)
-        down_last_ref[...] = total.astype(BF)
+        up_beyond().wait()
+        up_last_ref[...] = up_core[0, x, h, b, y] + up_z[2]
+        down_goal[2]()
+        down_last_ref[...] = down_core[0, y, x]
         second_done(1)
-        for a in range(zs):
-            up_one_ref[a] = up_core[1, x, a, y]
+        for i, k in grid_of(2, 2):
+            up_one_ref[i, k] = up_core[1, x, i, k, y]
         down_one_ref[...] = down_core[1, y, x]
         first_done(2)
         up_two_ref[...] = up_core[2, x]
@@ -938,7 +947,7 @@
     tile = ff // zs
     rows = width // (4 * zs)
     down_rows = tile // 4
-    halves = (2, zs, 2, 2, rows, cut)
+    halves = (2, 2, 2, 2, 2, rows, cut)
     down_half = (down_rows // 2, width)
     owned = (2, 2, 2) + down_half
     outs = [
@@ -950,8 +959,8 @@
         (halves, BF),
         (owned, BF),
         ((rows, cut), BF),
-        ((zs, rows, cut), BF),
-        ((zs, 2, rows, cut), BF),
+        ((2, 2, rows, cut), BF),
+        ((2, 2, 2, rows, cut), BF),
         (down_half, BF),
         (down_half, BF),
         ((2,) + down_half, BF),
@@ -986,15 +995,15 @@
             pltpu.VMEM((tokens, width), BF),
             pltpu.VMEM((tokens, tile), BF),
             pltpu.VMEM((tokens, tile), BF),
-            pltpu.VMEM((zs - 1, 2, zs, 2, rows, cut), BF),
-            pltpu.VMEM((zs - 1, zs, 2, rows, cut), BF),
-            pltpu.VMEM((zs - 1, zs, rows, cut), BF),
-            pltpu.VMEM((zs, rows, cut), BF),
+            pltpu.VMEM((zs - 1, 2, 2, 2, 2, rows, cut), BF),
+            pltpu.VMEM((zs - 1, 2, 2, 2, rows, cut), BF),
+            pltpu.VMEM((zs - 1, 2, 2, rows, cut), BF),
+            pltpu.VMEM((3, rows, cut), BF),
             pltpu.VMEM((zs - 1, 2, 2) + down_half, BF),
             pltpu.VMEM((zs - 1, 2) + down_half, BF),
             pltpu.VMEM((zs - 1,) + down_half, BF),
-            pltpu.VMEM((zs,) + down_half, BF),
-            pltpu.SemaphoreType.DMA((12 * (zs - 1) + 1 + 3 * zs,)),
+            pltpu.VMEM((2,) + down_half, BF),
+            pltpu.SemaphoreType.DMA((12 * (zs - 1) + 8,)),
         ],
         compiler_params=params(62, collective_id=4),
         cost_estimate=pl.CostEstimate(
@@ -1266,7 +1275,6 @@
         linv_ref,
         cos_ref,
         sin_ref,
-        own_ref,
         give_ref,
         up_last_ref,
         up_one_ref,
@@ -1286,7 +1294,7 @@
         dx_in,
         vec_ref,
     ) = ins
-    result, grad_ref, s_qkv, s_out, s_up, s_down, *small_outs = outs
+    result, grad_ref, grad_take, s_qkv, s_out, s_up, s_down, *small_outs = outs
     (
         do_mask,
         d_proj,
@@ -1300,6 +1308,7 @@
         w_core,
         w_y,
         w_z,
+        w_far,
         w_last,
         w_facing,
         d_own,
@@ -1340,6 +1349,7 @@
     cut = width // 2
     links = Links(sems, zs)
     x, y, z, c = links.x, links.y, links.z, links.c
+    h, b = links.upper, links.lower
 
     fetch = [
         links.local(lambda p=p: p[0], lambda p=p: p[1])
@@ -1353,15 +1363,20 @@
     ]
     u_load = [
         links.local(lambda: up_last_ref, lambda: u_last.at[0]),
-        links.local(lambda: up_one_ref.at[z], lambda: u_own.at[0, z]),
-        links.local(lambda: up_two_ref.at[:, y], lambda: u_own.at[1]),
-    ]
-    u_to_y = links.swap(lambda: up_two_ref.at[:, 1 - y], lambda: u_y, links.across)
-    u_far = [
-        links.spread(
-            lambda f, j=j: up_one_ref.at[f] if j == 0 else u_own.at[1, f],
-            lambda slot, j=j: u_z.at[j, slot],
+        links.local(lambda: up_one_ref.at[:, b], lambda: u_own.at[0, :, b]),
+        links.local(lambda: up_two_ref.at[:, :, y], lambda: u_own.at[1]),
+    ]
+    u_to_y = links.swap(lambda: up_two_ref.at[:, :, 1 - y], lambda: u_y, links.across)
+    u_near = [
+        links.swap(
+            lambda j=j: up_one_ref.at[:, 1 - b] if j == 0 else u_own.at[1, :, 1 - b],
+            lambda j=j: u_z.at[j, 0:2],
+            links.near,
         )
+        for j in range(2)
+    ]
+    u_beyond = [
+        links.swap(lambda j=j: u_own.at[j, 1 - h, b], lambda j=j: u_z.at[j, 2], links.beyond)
         for j in range(2)
     ]
     u_to_facing = [
@@ -1370,18 +1385,26 @@
     ]
     raws = (raw_up, raw_out)
     w_keep = [
-        links.local(lambda r=r: r.at[:, :, :, c], lambda k=k: w_own.at[k]) for k, r in enumerate(raws)
+        links.local(lambda r=r: r.at[:, :, :, :, c], lambda k=k: w_own.at[k]) for k, r in enumerate(raws)
     ]
     w_to_core = [
-        links.swap(lambda r=r: r.at[:, :, :, 1 - c], lambda k=k: w_core.at[k], links.core)
+        links.swap(lambda r=r: r.at[:, :, :, :, 1 - c], lambda k=k: w_core.at[k], links.core)
         for k, r in enumerate(raws)
     ]
     w_to_y = [
-        links.swap(lambda k=k: w_own.at[k, :, :, 1 - y], lambda k=k: w_y.at[k], links.across)
+        links.swap(lambda k=k: w_own.at[k, :, :, :, 1 - y], lambda k=k: w_y.at[k], links.across)
         for k in range(2)
     ]
-    w_far = [
-        links.spread(lambda f, k=k: w_own.at[k, :, f, y], lambda slot, k=k: w_z.at[k, slot])
+    w_near = [
+        links.swap(
+            lambda k=k: w_own.at[k, :, :, 1 - b, y], lambda k=k: w_z.at[k], links.near
+        )
+        for k in range(2)
+    ]
+    w_beyond = [
+        links.swap(
+            lambda k=k: w_own.at[k, :, 1 - h, b, y], lambda k=k: w_far.at[k], links.beyond
+        )
         for k in range(2)
     ]
     w_to_facing = [
@@ -1400,38 +1423,35 @@
         links.local(lambda: down_one_ref, lambda: d_sum.at[0]),
         links.local(lambda: down_two_ref.at[x], lambda: d_sum.at[1]),
     ]
-    d_far = [
-        links.gather(
-            lambda j=j: down_one_ref if j == 1 else d_sum.at[j - 1], lambda slot: d_z.at[slot], j
-        )
-        for j in range(1, zs)
+    d_goal = [
+        links.to_goal(lambda j=j: d_sum.at[j - 1], lambda j=j: d_z.at[j - 1], j) for j in range(1, zs)
     ]
     d_to_facing = links.swap(lambda: d_last, lambda: d_facing, links.facing)
     groups = range(len(split))
     q_to_core = [
-        links.swap(lambda g=g: q_raws[g].at[:, :, 1 - c], lambda g=g: q_cores[g], links.core)
+        links.swap(lambda g=g: q_raws[g].at[:, :, :, 1 - c], lambda g=g: q_cores[g], links.core)
         for g in groups
     ]
     q_to_y = [
-        links.swap(lambda g=g: q_cores[g].at[:, 1 - y], lambda g=g: q_ys[g], links.across)
+        links.swap(lambda g=g: q_cores[g].at[:, :, 1 - y], lambda g=g: q_ys[g], links.across)
         for g in groups
     ]
-    q_far = [
-        links.spread(lambda f, g=g: q_cores[g].at[f, y], lambda slot, g=g: q_zs[g].at[slot])
+    q_near = [
+        links.swap(lambda g=g: q_cores[g].at[:, 1 - b, y], lambda g=g: q_zs[g].at[0:2], links.near)
+        for g in groups
+    ]
+    q_beyond = [
+        links.swap(lambda g=g: q_cores[g].at[1 - h, b, y], lambda g=g: q_zs[g].at[2], links.beyond)
         for g in groups
     ]
     q_to_facing = [
         links.swap(lambda g=g: q_lasts[g], lambda g=g: q_facings[g], links.facing) for g in groups
     ]
-    keep_out = links.local(lambda: own_ref, lambda: result.at[x])
-    out_sem = links.take(2)
-
-    def cross_out(slot):
-        return remote(give_ref, result.at[slot], sems.at[out_sem], sems.at[out_sem + 1], links.facing)
+    cross_out = links.swap(lambda: give_ref, lambda: result, links.facing)
 
     give_grad = links.swap(lambda: g_send, lambda: g_take, links.facing)
-    keep_grad = links.local(lambda: g_own, lambda: grad_ref.at[x])
-    put_grad = links.local(lambda: g_own, lambda: grad_ref.at[1 - x])
+    keep_grad = links.local(lambda: g_own, lambda: grad_ref)
+    put_grad = links.local(lambda: g_take, lambda: grad_take)
     early = [
         gather_stages(links, mod_early),
         sum_stages(links, sum_early, early_take, early_far),
@@ -1446,15 +1466,15 @@
         for stages in arrays:
             stages[stage][1]()
 
-    def sum_far(own, taken):
-        total = own.astype(F32)
-        for f in links.far:
-            total += taken(f).astype(F32)
-        return total.astype(BF)
-
-    def u_z_done(j):
-        u_far[j][1]()
-        u_last[j + 1] = sum_far(u_own[j, z], lambda f: u_z[j, f])
+    def u_near_done(j):
+        u_near[j]().wait()
+        for k in range(2):
+            u_own[j, k, b] = u_own[j, k, b] + u_z[j, k]
+        u_beyond[j]().start()
+
+    def u_beyond_done(j):
+        u_beyond[j]().wait()
+        u_last[j + 1] = u_own[j, h, b] + u_z[j, 2]
         u_to_facing[j + 1]().start()
 
     def u_done(j):
@@ -1467,44 +1487,55 @@
     def w_core_done(k):
         w_keep[k]().wait()
         w_to_core[k]().wait()
-        for h, a, b in grid_of(2, zs, 2):
-            w_own[k, h, a, b] = w_own[k, h, a, b] + w_core[k, h, a, b]
+        for i in grid_of(2, 2, 2, 2):
+            w_own[(k, *i)] = w_own[(k, *i)] + w_core[(k, *i)]
 
     def w_y_done(k):
         w_to_y[k]().wait()
-        for h, a in grid_of(2, zs):
-            w_own[k, h, a, y] = w_own[k, h, a, y] + w_y[k, h, a]
-        w_far[k][0]()
-
-    def w_z_done(k):
-        w_far[k][1]()
-        for h in range(2):
-            w_last[k, h] = sum_far(w_own[k, h, z, y], lambda f: w_z[k, f, h])
+        for i in grid_of(2, 2, 2):
+            w_own[(k, *i, y)] = w_own[(k, *i, y)] + w_y[(k, *i)]
+        w_near[k]().start()
+
+    def w_near_done(k):
+        w_near[k]().wait()
+        for i, j in grid_of(2, 2):
+            w_own[k, i, j, b, y] = w_own[k, i, j, b, y] + w_z[k, i, j]
+        w_beyond[k]().start()
+
+    def w_beyond_done(k):
+        w_beyond[k]().wait()
+        for i in range(2):
+            w_last[k, i] = w_own[k, i, h, b, y] + w_far[k, i]
         w_to_facing[k]().start()
 
     def w_done(k):
         w_to_facing[k]().wait()
         out, start = (s_up, (zs - 1) * width) if k == 0 else (s_out, 0)
-        for h in range(2):
-            out[:, start + h * cut : start + (h + 1) * cut] = w_last[k, h].astype(F32) + w_facing[
-                k, h
+        for i in range(2):
+            out[:, start + i * cut : start + (i + 1) * cut] = w_last[k, i].astype(F32) + w_facing[
+                k, i
             ].astype(F32)
 
     def q_core_done(g):
         q_to_core[g]().wait()
-        for a, b in grid_of(zs, 2):
-            q_cores[g][a, b] = q_cores[g][a, b] + q_raws[g][a, b, c]
-        q_to_y[g]().start()
+        for i in grid_of(2, 2, 2):
+            q_cores[g][i] = q_cores[g][i] + q_raws[g][(*i, c)]
 
     def q_y_done(g):
         q_to_y[g]().wait()
-        for a in range(zs):
-            q_cores[g][a, y] = q_cores[g][a, y] + q_ys[g][a]
-        q_far[g][0]()
-
-    def q_z_done(g):
-        q_far[g][1]()
-        q_lasts[g][...] = sum_far(q_cores[g][z, y], lambda f: q_zs[g][f])
+        for i in grid_of(2, 2):
+            q_cores[g][(*i, y)] = q_cores[g][(*i, y)] + q_ys[g][i]
+        q_near[g]().start()
+
+    def q_near_done(g):
+        q_near[g]().wait()
+        for k in range(2):
+            q_cores[g][k, b, y] = q_cores[g][k, b, y] + q_zs[g][k]
+        q_beyond[g]().start()
+
+    def q_beyond_done(g):
+        q_beyond[g]().wait()
+        q_lasts[g][...] = q_cores[g][h, b, y] + q_zs[g][2]
         q_to_facing[g]().start()
 
     def q_done(g):
@@ -1519,8 +1550,8 @@
         for p in range(3):
             rows = slice(p * width + first, p * width + first + size)
             part = mm(act_ref[...], d_proj[rows, :], NT).astype(BF)
-            q_raws[g][:, :, :, :, p * size : (p + 1) * size] = part.reshape(
-                q_raws[g].shape[:4] + (size,)
+            q_raws[g][:, :, :, :, :, p * size : (p + 1) * size] = part.reshape(
+                q_raws[g].shape[:5] + (size,)
             )
         q_to_core[g]().start()
 
@@ -1532,8 +1563,7 @@
         for k in range(2):
             w_to_core[k]().start()
             w_keep[k]().start()
-        u_far[0][0]()
-        d_far[0][0]()
+        u_near[0]().start()
         u_to_y().start()
         d_to_side[0]().start()
         for load in u_load + d_load:
@@ -1541,16 +1571,17 @@
         mod_early[z, y, c, x] = mod_ref[...]
         sum_early[...] = sum_ref[...]
         begin(early, 0)
-        keep_out().start()
-        cross_out(x).start()
+        cross_out().start()
         for load in fetch:
             load().start()
 
     def due_01():
+        d_load[1]().wait()
+        d_goal[0][0]()
         d_keep().wait()
         d_to_core().wait()
-        for b, h in grid_of(2, 2):
-            d_own[b, h] = d_own[b, h] + d_core[b, h]
+        for i, k in grid_of(2, 2):
+            d_own[i, k] = d_own[i, k] + d_core[i, k]
         d_to_y().start()
         end(early, 0)
         begin(early, 1)
@@ -1558,76 +1589,69 @@
     def due_10():
         w_core_done(0)
         w_core_done(1)
-        w_to_y[0]().start()
         u_load[0]().wait()
         u_to_facing[0]().start()
 
     def due_11():
         u_load[2]().wait()
         u_to_y().wait()
-        for a in range(zs):
-            u_own[1, a] = u_own[1, a] + u_y[a]
-        u_far[1][0]()
+        for i in grid_of(2, 2):
+            u_own[(1, *i)] = u_own[(1, *i)] + u_y[i]
+        u_near[1]().start()
+        u_load[1]().wait()
+        u_near_done(0)
+        d_goal[0][1]()
+        end(early, 1)
+        begin(early, 2)
+
+    def due_20():
+        fetch[0]().wait()
+        weight_grad_of(0)
         d_load[2]().wait()
         d_to_side[0]().wait()
         d_sum[1] = d_sum[1] + d_side[0]
-        d_far[1][0]()
-        end(early, 1)
-        begin(early, 2)
-
-    def due_20():
-        fetch[0]().wait()
-        weight_grad_of(0)
+        d_goal[1][0]()
+
+    def due_21():
         d_to_y().wait()
-        for h in range(2):
-            d_own[y, h] = d_own[y, h] + d_y[h]
+        for k in range(2):
+            d_own[y, k] = d_own[y, k] + d_y[k]
         d_to_side[1]().start()
-        w_to_y[1]().start()
-
-    def due_21():
+        w_to_y[0]().start()
         q_core_done(0)
+        u_near_done(1)
+        u_beyond_done(0)
+        end(early, 2)
+        begin(early, 3)
+
+    def due_30():
+        d_goal[1][1]()
+
+    def due_31():
         w_y_done(0)
-
-    def due_30():
-        u_load[1]().wait()
-        u_z_done(0)
+        q_to_y[0]().start()
+
+    def due_40():
+        weight_grad_of(1)
         d_to_side[1]().wait()
         d_sum[2] = d_own[y, x] + d_side[1]
-        d_far[2][0]()
-        end(early, 2)
-        begin(early, 3)
-
-    def due_31():
-        w_y_done(1)
-        q_y_done(0)
-
-    def due_40():
-        weight_grad_of(1)
-        u_z_done(1)
+        d_goal[2][0]()
+        u_beyond_done(1)
         end(early, 3)
 
     def due_41():
         q_core_done(1)
-        w_z_done(0)
+        w_near_done(0)
         u_done(0)
+
+    def due_50():
+        q_y_done(0)
+        q_to_y[1]().start()
+        d_goal[2][1]()
+
+    def due_51():
+        w_beyond_done(0)
         u_done(1)
-
-    def due_50():
-        for load in d_load[0:2]:
-            load().wait()
-        for j in range(zs - 1):
-            d_far[j][1]()
-
-        @pl.when(z > 0)
-        def _():
-            d_last[...] = sum_far(d_sum[jnp.maximum(z - 1, 0)], lambda f: d_z[f])
-
-        d_to_facing().start()
-
-    def due_51():
-        q_y_done(1)
-        w_z_done(1)
-        u_done(2)
 
     due = (
         (due_00, due_01),
@@ -1720,12 +1744,15 @@
     def _():
         for load in fetch[1:]:
             load().wait()
+        weight_grad_of(2)
         grad, shift, pull = finish(tok_rem, slice(half, 2 * half))
         g_send[...] = grad.astype(BF)
         give_grad().start()
-        weight_grad_of(2)
-        q_z_done(0)
+        q_y_done(1)
         q_core_done(2)
+        q_to_y[2]().start()
+        q_near_done(0)
+        w_to_y[1]().start()
         grad, shift_own, pull_own = finish(tok_own, slice(0, half))
         g_own[...] = grad
         keep_grad().start()
@@ -1739,33 +1766,46 @@
         sum_late[lines:, :] = jnp.zeros((sum_late.shape[0] - lines, 128), F32)
         put_rows(sum_late, 0, pull * (1.0 + vec_ref[3:4, :]))
         begin(late, 0)
-        q_z_done(1)
+        q_near_done(1)
+        q_beyond_done(0)
         end(late, 0)
         begin(late, 1)
+        d_load[0]().wait()
+        for j in range(zs - 1):
+            d_goal[j][2]()
+
+        @pl.when(z > 0)
+        def _():
+            d_last[...] = d_sum[jnp.maximum(z - 1, 0)]
+
+        d_to_facing().start()
         q_y_done(2)
         end(late, 1)
         begin(late, 2)
-        for k in range(2):
-            w_done(k)
+        q_beyond_done(1)
+        w_y_done(1)
+        q_near_done(2)
+        u_done(2)
+        end(late, 2)
+        begin(late, 3)
+        w_near_done(1)
+        w_done(0)
+        q_beyond_done(2)
+        w_beyond_done(1)
         d_to_facing().wait()
         mine, other = d_last[...].astype(F32), d_facing[...].astype(F32)
         rows_half = mine.shape[0]
         s_down[0:rows_half, :] = jnp.where(x == 0, mine, other)
         s_down[rows_half:, :] = jnp.where(x == 0, other, mine)
-        end(late, 2)
-        begin(late, 3)
-        keep_out().wait()
-        cross_out(x).wait_send()
-        cross_out(1 - x).wait_recv()
+        cross_out().wait()
         q_done(0)
         q_done(1)
-        q_z_done(2)
         end(late, 3)
         give_grad().wait()
+        put_grad().start()
         keep_grad().wait()
-        g_own[...] = g_take[...].astype(F32)
-        put_grad().start()
         q_done(2)
+        w_done(1)
         put_grad().wait()
         for out, value in zip(small_outs, (mod_early, mod_late, sum_early, sum_late)):
             out[...] = value[...]
@@ -1805,7 +1845,7 @@
         (sums.shape, F32),
         (sum_late, F32),
     ]
-    outs[0] = ((2, half, width), F32)
+    outs = [((half, width), F32), ((half, width), BF)] + outs[1:]
     fetched = ins[-6:-1]
     in_specs = (
         [part(0), part(1), part(2), part(0), part(0)]
@@ -1820,23 +1860,24 @@
         + [ANY] * 5
         + [once(vec.shape)]
     )
-    out_specs = [ANY, ANY] + [once(shape) for shape, _ in outs[1:]]
-    out_shape = [jax.ShapeDtypeStruct((2, half, width), BF)] + [
+    out_specs = [ANY, ANY, ANY] + [once(shape) for shape, _ in outs[2:]]
+    out_shape = [jax.ShapeDtypeStruct((half, width), BF)] + [
         jax.ShapeDtypeStruct(*o) for o in outs
     ]
     scratch = [
         vm(2, 2 * HD, tokens),
         vm(3 * width, tokens),
         pltpu.SemaphoreType.DMA((250,)),
-        vm(2, zs, rows, cut),
-        vm(zs, rows, cut),
-        vm(2, zs, rows, cut),
+        vm(2, 2, 2, rows, cut),
+        vm(2, 2, rows, cut),
+        vm(2, 3, rows, cut),
         vm(3, rows, cut),
         vm(3, rows, cut),
-        vm(2, 2, zs, 2, rows, cut),
-        vm(2, 2, zs, 2, rows, cut),
-        vm(2, 2, zs, rows, cut),
-        vm(2, zs, 2, rows, cut),
+        vm(2, 2, 2, 2, 2, rows, cut),
+        vm(2, 2, 2, 2, 2, rows, cut),
+        vm(2, 2, 2, 2, rows, cut),
+        vm(2, 2, 2, rows, cut),
+        vm(2, 2, rows, cut),
         vm(2, 2, rows, cut),
         vm(2, 2, rows, cut),
         vm(2, 2, *down_half),
@@ -1844,13 +1885,13 @@
         vm(2, *down_half),
         vm(2, *down_half),
         vm(zs - 1, *down_half),
-        vm(zs, *down_half),
+        vm(zs - 1, 2, *down_half),
         vm(*down_half),
         vm(*down_half),
-        [vm(zs, 2, 2, rows, s) for s in sizes],
-        [vm(zs, 2, rows, s) for s in sizes],
-        [vm(zs, rows, s) for s in sizes],
-        [vm(zs, rows, s) for s in sizes],
+        [vm(2, 2, 2, 2, rows, s) for s in sizes],
+        [vm(2, 2, 2, rows, s) for s in sizes],
+        [vm(2, 2, rows, s) for s in sizes],
+        [vm(3, rows, s) for s in sizes],
         [vm(rows, s) for s in sizes],
         [vm(rows, s) for s in sizes],
         vm(half, width),
@@ -1893,6 +1934,108 @@
         ),
         name="back",
     )(q, q, q, att, d_att, e, linv, cos_t, sin_t, *ins[7:])
+
+
+def iota2(shape, axis):
+    return lax.broadcasted_iota(jnp.int32, shape, axis)
+
+
+def finish_kernel(pairs, early_ref, late_ref, sum_early_ref, sum_late_ref, *refs):
+    sources, refs = refs[:8], refs[8:]
+    output, grad, *shards, w_ada, b_ada, gain_one, gain_two, b_down, b_up = refs[:12]
+    held, (wide, sems) = refs[12:20], refs[20:]
+    x = lax.axis_index("seq")
+    goals = [output.at[x], output.at[1 - x], grad.at[x], grad.at[1 - x], *shards]
+    loads = [
+        pltpu.make_async_copy(src, dst, sems.at[0, k])
+        for k, (src, dst) in enumerate(zip(sources, held))
+    ]
+    stores = [
+        pltpu.make_async_copy(wide if k == 3 else src, dst, sems.at[1, k])
+        for k, (src, dst) in enumerate(zip(held, goals))
+    ]
+    for copy in loads:
+        copy.start()
+    for k in range(8):
+        loads[k].wait()
+        if k == 3:
+            wide[...] = held[3][...].astype(F32)
+        stores[k].start()
+    dp = lax.axis_index("dp")
+    rows, lines = w_ada.shape[0], early_ref.shape[1]
+    width = gain_one.shape[0] * lax.axis_size("dp")
+    per_line = width // 128
+    stamp_line = 4 * per_line
+    blocks = []
+    for ref, first, count in ((late_ref, 0, 2 * per_line), (early_ref, 2 * per_line, 4 * per_line)):
+        seqs, period = ref.shape[0], ref.shape[1]
+        flat = ref[...].reshape(seqs * period, 128)
+        stamps = early_ref[...].reshape(seqs * lines, 128)
+        shape = (seqs * lines, seqs * period)
+        line, col = iota2(shape, 0), iota2(shape, 1)
+        pick = (line // lines == col // period) & (lax.rem(line, lines) == stamp_line)
+        time = mm(stamps, jnp.where(pick, 1.0, 0.0).astype(BF), TN)
+        time = 32.0 * time[0:1, :] + time[1:2, :]
+        shape = (rows, seqs * period)
+        index = dp * rows + iota2(shape, 0)
+        place = jnp.where(index < pairs, index, index - pairs).astype(F32)
+        angles = time * jnp.exp(-math.log(10000.0) * place / pairs)
+        cond = features_of(angles, index >= pairs)
+        shape = (period * rows, seqs * period)
+        same = iota2(shape, 0) // rows == lax.rem(iota2(shape, 1), period)
+        total = jnp.zeros((period * rows, 128), F32)
+        for part in split_three(cond):
+            spread = jnp.concatenate([part.astype(F32)] * period, axis=0)
+            total += mm(jnp.where(same, spread, 0.0).astype(BF), flat)
+        for k in range(count):
+            start = (first + k) * 128
+            w_ada[:, start : start + 128] = total[k * rows : (k + 1) * rows]
+        shape = (period, seqs * period)
+        same = iota2(shape, 0) == lax.rem(iota2(shape, 1), period)
+        sums = mm(jnp.where(same, 1.0, 0.0).astype(BF), flat)
+        blocks += [sums[k : k + 1] for k in range(count)]
+
+    def mine(parts, out):
+        row = jnp.concatenate(parts, axis=1)
+        size, full = out.shape[0], row.shape[1]
+        row = pltpu.roll(row, lax.rem(full - dp * size, full), 1)
+        out[...] = row[0, 0:size]
+
+    def lines_of(ref, first, count):
+        return [ref[first + k : first + k + 1, :] for k in range(count)]
+
+    mine(blocks, b_ada)
+    mine(lines_of(sum_late_ref, 0, per_line), gain_one)
+    mine(lines_of(sum_early_ref, 0, per_line), gain_two)
+    mine(lines_of(sum_early_ref, per_line, per_line), b_down)
+    mine(lines_of(sum_early_ref, 2 * per_line, b_up.shape[0] * lax.axis_size("dp") // 128), b_up)
+    for copy in stores:
+        copy.wait()
+
+
+def finish_all(big, mod_early, mod_late, sum_early, sum_late, cond_width, width, ff, dps):
+    seqs = 2 * dps
+    mod_early = mod_early.reshape(seqs, *mod_early.shape[-2:])
+    mod_late = mod_late.reshape(seqs, *mod_late.shape[-2:])
+    smalls = (mod_early, mod_late, sum_early, sum_late)
+    vmem = pl.BlockSpec(memory_space=pltpu.VMEM)
+    half = big[0].shape[0]
+    out_shape = [jax.ShapeDtypeStruct((2, half, width), kind) for kind in (BF, F32)]
+    out_shape += [jax.ShapeDtypeStruct(a.shape, a.dtype) for a in big[4:]]
+    out_shape += [jax.ShapeDtypeStruct((cond_width // dps, 6 * width), F32)]
+    out_shape += [
+        jax.ShapeDtypeStruct((n // dps,), F32) for n in (6 * width, width, width, width, ff)
+    ]
+    return pl.pallas_call(
+        functools.partial(finish_kernel, cond_width // 2),
+        in_specs=[vmem] * 4 + [ANY] * len(big),
+        out_specs=[ANY] * 6 + [vmem] * 6,
+        out_shape=out_shape,
+        scratch_shapes=[pltpu.VMEM(a.shape, a.dtype) for a in big]
+        + [pltpu.VMEM((half, width), F32), pltpu.SemaphoreType.DMA((2, len(big)))],
+        compiler_params=params(),
+        name="finish_all",
+    )(*smalls, *big)
 
 
 def time_features(time_steps, pair_count):
@@ -1940,15 +2083,21 @@
         out_own, out_rem, dx, d_att_t, raw_out, raw_up, raw_down, *partial, mod, sums = middle_links(
             att_t, tokens, tok_rem, cotangent, cot_rem, span, vec_two, b_up[None], w_out, w_up, w_down, zs
         )
-        ins = (qkv_t, att_t, d_att_t, e, linv, cos_t, sin_t, out_own, out_rem, *partial)
+        ins = (qkv_t, att_t, d_att_t, e, linv, cos_t, sin_t, out_rem, *partial)
         ins += (raw_up, raw_out, raw_down, mod, sums, act_t, w_qkv_t, tokens, tok_rem, dx, vec_one)
-        output, grad_tokens, *shards, mod_early, mod_late, sum_early, sum_late = back(ins, zs, ff)
-        mod_early = mod_early.reshape(2 * dps, -1).astype(F32)
-        mod_late = mod_late.reshape(2 * dps, -1).astype(F32)
-        d_mod_all = jnp.concatenate([mod_late[:, : 2 * width], mod_early[:, : 4 * width]], axis=1)
-        time_all = 32.0 * mod_early[:, 4 * width] + mod_early[:, 4 * width + 1]
-        small = jnp.concatenate(
-            [sum_late.reshape(-1)[:width], sum_early.reshape(-1)[: 2 * width + ff]]
+        taken, g_own, g_take, *shards, mod_early, mod_late, sum_early, sum_late = back(ins, zs, ff)
+        output, grad_tokens, *shards, s_w_ada, s_b_ada, s_gain_one, s_gain_two, s_b_down, s_b_up = (
+            finish_all(
+                (out_own, taken, g_own, g_take, *shards),
+                mod_early,
+                mod_late,
+                sum_early,
+                sum_late,
+                w_ada.shape[0],
+                width,
+                ff,
+                dps,
+            )
         )
     else:
         tok_own, cot_own = pick(tokens, rank), pick(cotangent, rank)
@@ -1977,17 +2126,18 @@
         time_all = lax.all_gather(time_own[0].astype(F32), ("dp", "seq"))
         small = lax.psum(small, ("dp", "seq"))
 
-    def mine(x, axis=0):
-        size = x.shape[axis] // dps
-        return lax.dynamic_slice_in_dim(x, dp * size, size, axis)
-
-    features = jax.nn.silu(time_features(time_all, w_ada.shape[0] // 2))
-    s_w_ada = jnp.dot(mine(features, 1).T, d_mod_all, precision=lax.Precision.HIGHEST)
-    s_b_ada = jnp.sum(mine(d_mod_all, 1), axis=0)
-    s_gain_one = mine(small[:width])
-    s_gain_two = mine(small[width : 2 * width])
-    s_b_down = mine(small[2 * width : 3 * width])
-    s_b_up = mine(small[3 * width :])
+        def mine(x, axis=0):
+            size = x.shape[axis] // dps
+            return lax.dynamic_slice_in_dim(x, dp * size, size, axis)
+
+        features = jax.nn.silu(time_features(time_all, w_ada.shape[0] // 2))
+        s_w_ada = jnp.dot(mine(features, 1).T, d_mod_all, precision=lax.Precision.HIGHEST)
+        s_b_ada = jnp.sum(mine(d_mod_all, 1), axis=0)
+        s_gain_one = mine(small[:width])
+        s_gain_two = mine(small[width : 2 * width])
+        s_b_down = mine(small[2 * width : 3 * width])
+        s_b_up = mine(small[3 * width :])
+
     s_qkv, s_out, s_up, s_down = shards
 
     return (

time: 215 us -> 206 us (0.958)
  local copies, waits for them, and re-layouts: 11.7 us -> 0 us
  Pallas kernels: 197 us -> 202 us
    unnamed x26 -> x0, local copies, waits for them, and re-layouts: 8.43 us -> none
    pallas_call x0 -> x1, Pallas kernels: none -> 7.49 us  [finish_all(): pl.pallas_call(functools.partial(finish_kernel, cond_width // 2), in_spec...]
    dynamic_slice x4 -> x0, local copies, waits for them, and re-layouts: 2.38 us -> none  [mine(): return lax.dynamic_slice_in_dim(x, dp * size, size, axis)]
where the time goes in v6:
time: 206 us; the launch traced here: 203 us
  Pallas kernels  202 us (98%)
    pallas_call x1, Pallas kernels, back(): pl.pallas_call(kernel, grid=(PAIRS + 1,), in_specs=in_specs, out_specs=ou...  84.7 us
    pallas_call x1, Pallas kernels, middle_links(): pl.pallas_call(functools.partial(middle_links_kernel, zs), grid=(zs,), in...  61.5 us
    pallas_call x1, Pallas kernels, project(): pl.pallas_call(project_kernel, grid=(8,), in_specs=[smem, smem, smem, ANY...  25.8 us
    pallas_call x1, Pallas kernels, attend(): pl.pallas_call(attend_kernel, grid=(PAIRS,), in_specs=[part(0), part(1),...  22.9 us
    pallas_call x1, Pallas kernels, finish_all(): pl.pallas_call(functools.partial(finish_kernel, cond_width // 2), in_spec...  7.49 us

profile of v6, /device:TPU:10, one launch (start us, length us, event | category | flops | bytes accessed | tf_op | source)
XLA Modules:
  0.0 203.2 jit_solution(9096003307436028521)
XLA Ops:
  0.6 25.8 %project.1 = (bf16[768,1024]{1,0:T(8,128)(2,1)}, bf16[2304,1024]{1,0:T(8,128)(2,1)}, bf16[2304,768]{1,0:T(8,128)(2,1)}, bf16[512,768]{1,0:T(8,128)(2,1)}, f32[8,...) custom-call(s32[2]{0:T(128)} %time_ref.1, s32[2]{0:T(128)} %start_ref.1, ...), custom_call_target="tpu_custom_call" | custom-call | flops 3623878656 | bytes 20971520 | tf_op jit(solution)/shard_map/project/pallas_call | solution.py:392
  26.4 22.9 %attend.1 = (bf16[768,1024]{1,0:T(8,128)(2,1)}, bf16[12,1024,1024]{2,1,0:T(8,128)(2,1)}, f32[6,8,1024]{2,1,0:T(8,128)}, bf16[512,768]{1,0:T(8,128)(2,1)}) custom-call(bf16[2304,1024]{1,0:T(8,128)(2,1)} %get-tuple-element.63.q_ref.k_ref.v_ref.refs_0_.refs_1_.refs_2_, bf16[2304,1024]{1,0:T(8,128)(2,1)} %get-tuple-element.63.q_ref.k_ref.v_ref.refs_0_.refs_1_.refs_2_, ...), custom_call_target="tpu_custom_call" | custom-call | flops 12884901888 | bytes 31457280 | tf_op jit(solution)/shard_map/attend/pallas_call | solution.py:471
  49.4 61.5 %middle_links.1 = (bf16[512,768]{1,0:T(8,128)(2,1)}, bf16[512,768]{1,0:T(8,128)(2,1)}, f32[1024,768]{1,0:T(8,128)}, bf16[768,1024]{1,0:T(8,128)(2,1)}, bf16[2,2,...) custom-call(bf16[768,1024]{1,0:T(8,128)(2,1)} %get-tuple-element.64., ...), custom_call_target="tpu_custom_call" | custom-call | flops 32614907904 | bytes 41943040 | tf_op jit(solution)/shard_map/middle_links/pallas_call | solution.py:970
  110.8 84.7 %back.1 = (bf16[512,768]{1,0:T(8,128)(2,1)}, f32[512,768]{1,0:T(8,128)}, bf16[512,768]{1,0:T(8,128)(2,1)}, f32[48,2304]{1,0:T(8,128)}, f32[48,768]{1,0:T(8,128)}...) custom-call(bf16[2304,1024]{1,0:T(8,128)(2,1)} %get-tuple-element.63, ...), custom_call_target="tpu_custom_call" | custom-call | flops 33017561088 | bytes 62914560 | tf_op jit(solution)/shard_map/back/pallas_call | solution.py:1922
  195.6 7.5 %finish_all.1 = (bf16[2,512,768]{2,1,0:T(8,128)(2,1)}, f32[2,512,768]{2,1,0:T(8,128)}, f32[48,2304]{1,0:T(8,128)}, f32[48,768]{1,0:T(8,128)}, f32[48,3072]{1,0:T...) custom-call(bf16[32,32,128]{2,1,0:T(8,128)(2,1)} %bitcast.3, ...), custom_call_target="tpu_custom_call" | custom-call | tf_op jit(solution)/shard_map/finish_all/pallas_call | solution.py:2029

commit v7 on v6

--- a/solution.py
+++ b/solution.py
@@ -830,7 +830,7 @@
                 down_acc[dst, :] = jnp.zeros((tile, width), F32)
                 d_act[dst, :] = jnp.zeros((tile, width), F32)
 
-    chunk = tokens // 4
+    chunk = tokens // 2
 
     def one(k, bup):
         rows = rows_of(chunk, k)
@@ -845,7 +845,7 @@
         d_act[rows, :] += mm(d_up_low, w_up_ref[...], NT)
         return bup + col_sum(d_up_low.astype(F32))
 
-    bup = lax.fori_loop(0, 4, one, jnp.zeros((1, w_up_ref.shape[1]), F32))
+    bup = lax.fori_loop(0, 2, one, jnp.zeros((1, w_up_ref.shape[1]), F32))
     for j in range(steps):
         pl.when(step == j)(lambda j=j: put_rows(sum_ref, 2 * width // 128 + j * bup.shape[1] // 128, bup))
 
@@ -860,6 +860,7 @@
 
     @pl.when(step == 3)
     def _():
+        third_stage()
         second_stage(1)
         first_stage(2)
 
@@ -887,7 +888,6 @@
 
     @pl.when(step == 2)
     def _():
-        third_stage()
         core_stage(2)
 
     @pl.when(step == steps - 1)
@@ -1598,6 +1598,7 @@
         for i in grid_of(2, 2):
             u_own[(1, *i)] = u_own[(1, *i)] + u_y[i]
         u_near[1]().start()
+        w_to_y[0]().start()
         u_load[1]().wait()
         u_near_done(0)
         d_goal[0][1]()
@@ -1617,41 +1618,53 @@
         for k in range(2):
             d_own[y, k] = d_own[y, k] + d_y[k]
         d_to_side[1]().start()
-        w_to_y[0]().start()
         q_core_done(0)
+        q_to_y[0]().start()
         u_near_done(1)
         u_beyond_done(0)
         end(early, 2)
         begin(early, 3)
 
     def due_30():
+        w_y_done(0)
+        w_to_y[1]().start()
         d_goal[1][1]()
 
     def due_31():
-        w_y_done(0)
-        q_to_y[0]().start()
-
-    def due_40():
-        weight_grad_of(1)
         d_to_side[1]().wait()
         d_sum[2] = d_own[y, x] + d_side[1]
         d_goal[2][0]()
+
+    def due_40():
+        weight_grad_of(1)
+        w_near_done(0)
+        q_y_done(0)
         u_beyond_done(1)
         end(early, 3)
 
     def due_41():
         q_core_done(1)
-        w_near_done(0)
-        u_done(0)
-
-    def due_50():
-        q_y_done(0)
         q_to_y[1]().start()
         d_goal[2][1]()
+        u_done(0)
+
+    def due_50():
+        w_beyond_done(0)
+        w_y_done(1)
+        q_near_done(0)
+        u_done(1)
 
     def due_51():
-        w_beyond_done(0)
-        u_done(1)
+        d_load[0]().wait()
+        for j in range(zs - 1):
+            d_goal[j][2]()
+
+        @pl.when(z > 0)
+        def _():
+            d_last[...] = d_sum[jnp.maximum(z - 1, 0)]
+
+        d_to_facing().start()
+        q_beyond_done(0)
 
     due = (
         (due_00, due_01),
@@ -1748,11 +1761,10 @@
         grad, shift, pull = finish(tok_rem, slice(half, 2 * half))
         g_send[...] = grad.astype(BF)
         give_grad().start()
-        q_y_done(1)
         q_core_done(2)
         q_to_y[2]().start()
-        q_near_done(0)
-        w_to_y[1]().start()
+        q_y_done(1)
+        w_near_done(1)
         grad, shift_own, pull_own = finish(tok_own, slice(0, half))
         g_own[...] = grad
         keep_grad().start()
@@ -1767,45 +1779,33 @@
         put_rows(sum_late, 0, pull * (1.0 + vec_ref[3:4, :]))
         begin(late, 0)
         q_near_done(1)
-        q_beyond_done(0)
+        w_beyond_done(1)
+        q_y_done(2)
         end(late, 0)
         begin(late, 1)
-        d_load[0]().wait()
-        for j in range(zs - 1):
-            d_goal[j][2]()
-
-        @pl.when(z > 0)
-        def _():
-            d_last[...] = d_sum[jnp.maximum(z - 1, 0)]
-
-        d_to_facing().start()
-        q_y_done(2)
+        u_done(2)
+        w_done(0)
+        q_done(0)
         end(late, 1)
         begin(late, 2)
         q_beyond_done(1)
-        w_y_done(1)
         q_near_done(2)
-        u_done(2)
         end(late, 2)
         begin(late, 3)
-        w_near_done(1)
-        w_done(0)
-        q_beyond_done(2)
-        w_beyond_done(1)
         d_to_facing().wait()
         mine, other = d_last[...].astype(F32), d_facing[...].astype(F32)
         rows_half = mine.shape[0]
         s_down[0:rows_half, :] = jnp.where(x == 0, mine, other)
         s_down[rows_half:, :] = jnp.where(x == 0, other, mine)
+        q_beyond_done(2)
         cross_out().wait()
-        q_done(0)
+        w_done(1)
         q_done(1)
         end(late, 3)
         give_grad().wait()
         put_grad().start()
         keep_grad().wait()
         q_done(2)
-        w_done(1)
         put_grad().wait()
         for out, value in zip(small_outs, (mod_early, mod_late, sum_early, sum_late)):
             out[...] = value[...]

time: 206 us -> 202 us (0.981)
  Pallas kernels: 202 us -> 198 us
    pallas_call x1, Pallas kernels: 61.5 us -> 57.6 us  [middle_links(): pl.pallas_call(functools.partial(middle_links_kernel, zs), grid=(zs,), in...]
where the time goes in v7:
time: 202 us; the launch traced here: 199 us
  Pallas kernels  198 us (98%)
    pallas_call x1, Pallas kernels, back(): pl.pallas_call(kernel, grid=(PAIRS + 1,), in_specs=in_specs, out_specs=ou...  84.3 us
    pallas_call x1, Pallas kernels, middle_links(): pl.pallas_call(functools.partial(middle_links_kernel, zs), grid=(zs,), in...  57.6 us
    pallas_call x1, Pallas kernels, project(): pl.pallas_call(project_kernel, grid=(8,), in_specs=[smem, smem, smem, ANY...  25.8 us
    pallas_call x1, Pallas kernels, attend(): pl.pallas_call(attend_kernel, grid=(PAIRS,), in_specs=[part(0), part(1),...  22.9 us
    pallas_call x1, Pallas kernels, finish_all(): pl.pallas_call(functools.partial(finish_kernel, cond_width // 2), in_spec...  7.49 us

profile of v7, /device:TPU:10, one launch (start us, length us, event | category | flops | bytes accessed | tf_op | source)
XLA Modules:
  0.0 198.9 jit_solution(13010396845859923087)
XLA Ops:
  0.6 25.8 %project.1 = (bf16[768,1024]{1,0:T(8,128)(2,1)}, bf16[2304,1024]{1,0:T(8,128)(2,1)}, bf16[2304,768]{1,0:T(8,128)(2,1)}, bf16[512,768]{1,0:T(8,128)(2,1)}, f32[8,...) custom-call(s32[2]{0:T(128)} %time_ref.1, s32[2]{0:T(128)} %start_ref.1, ...), custom_call_target="tpu_custom_call" | custom-call | flops 3623878656 | bytes 20971520 | tf_op jit(solution)/shard_map/project/pallas_call | solution.py:392
  26.4 22.9 %attend.1 = (bf16[768,1024]{1,0:T(8,128)(2,1)}, bf16[12,1024,1024]{2,1,0:T(8,128)(2,1)}, f32[6,8,1024]{2,1,0:T(8,128)}, bf16[512,768]{1,0:T(8,128)(2,1)}) custom-call(bf16[2304,1024]{1,0:T(8,128)(2,1)} %get-tuple-element.63.q_ref.k_ref.v_ref.refs_0_.refs_1_.refs_2_, bf16[2304,1024]{1,0:T(8,128)(2,1)} %get-tuple-element.63.q_ref.k_ref.v_ref.refs_0_.refs_1_.refs_2_, ...), custom_call_target="tpu_custom_call" | custom-call | flops 12884901888 | bytes 31457280 | tf_op jit(solution)/shard_map/attend/pallas_call | solution.py:471
  49.4 57.6 %middle_links.1 = (bf16[512,768]{1,0:T(8,128)(2,1)}, bf16[512,768]{1,0:T(8,128)(2,1)}, f32[1024,768]{1,0:T(8,128)}, bf16[768,1024]{1,0:T(8,128)(2,1)}, bf16[2,2,...) custom-call(bf16[768,1024]{1,0:T(8,128)(2,1)} %get-tuple-element.64., ...), custom_call_target="tpu_custom_call" | custom-call | flops 32614907904 | bytes 41943040 | tf_op jit(solution)/shard_map/middle_links/pallas_call | solution.py:970
  107.0 84.3 %back.1 = (bf16[512,768]{1,0:T(8,128)(2,1)}, f32[512,768]{1,0:T(8,128)}, bf16[512,768]{1,0:T(8,128)(2,1)}, f32[48,2304]{1,0:T(8,128)}, f32[48,768]{1,0:T(8,128)}...) custom-call(bf16[2304,1024]{1,0:T(8,128)(2,1)} %get-tuple-element.63, ...), custom_call_target="tpu_custom_call" | custom-call | flops 33017561088 | bytes 62914560 | tf_op jit(solution)/shard_map/back/pallas_call | solution.py:1922
  191.3 7.5 %finish_all.1 = (bf16[2,512,768]{2,1,0:T(8,128)(2,1)}, f32[2,512,768]{2,1,0:T(8,128)}, f32[48,2304]{1,0:T(8,128)}, f32[48,768]{1,0:T(8,128)}, f32[48,3072]{1,0:T...) custom-call(bf16[32,32,128]{2,1,0:T(8,128)(2,1)} %bitcast.3, ...), custom_call_target="tpu_custom_call" | custom-call | tf_op jit(solution)/shard_map/finish_all/pallas_call | solution.py:2029

commit v8 on v7

--- a/solution.py
+++ b/solution.py
@@ -1571,7 +1571,6 @@
         mod_early[z, y, c, x] = mod_ref[...]
         sum_early[...] = sum_ref[...]
         begin(early, 0)
-        cross_out().start()
         for load in fetch:
             load().start()
 
@@ -1604,6 +1603,7 @@
         d_goal[0][1]()
         end(early, 1)
         begin(early, 2)
+        cross_out().start()
 
     def due_20():
         fetch[0]().wait()

time: 202 us -> 210 us (1.040)
  Pallas kernels: 198 us -> 208 us
    pallas_call x1, Pallas kernels: 84.3 us -> 93.7 us  [back(): pl.pallas_call(kernel, grid=(PAIRS + 1,), in_specs=in_specs, out_specs=ou...]
where the time goes in v8:
time: 210 us; the launch traced here: 208 us
  Pallas kernels  208 us (99%)
    pallas_call x1, Pallas kernels, back(): pl.pallas_call(kernel, grid=(PAIRS + 1,), in_specs=in_specs, out_specs=ou...  93.7 us
    pallas_call x1, Pallas kernels, middle_links(): pl.pallas_call(functools.partial(middle_links_kernel, zs), grid=(zs,), in...  57.6 us
    pallas_call x1, Pallas kernels, project(): pl.pallas_call(project_kernel, grid=(8,), in_specs=[smem, smem, smem, ANY...  25.8 us
    pallas_call x1, Pallas kernels, attend(): pl.pallas_call(attend_kernel, grid=(PAIRS,), in_specs=[part(0), part(1),...  22.9 us
    pallas_call x1, Pallas kernels, finish_all(): pl.pallas_call(functools.partial(finish_kernel, cond_width // 2), in_spec...  7.49 us

profile of v8, /device:TPU:10, one launch (start us, length us, event | category | flops | bytes accessed | tf_op | source)
XLA Modules:
  0.0 208.4 jit_solution(12858398369583717955)
XLA Ops:
  0.6 25.8 %project.1 = (bf16[768,1024]{1,0:T(8,128)(2,1)}, bf16[2304,1024]{1,0:T(8,128)(2,1)}, bf16[2304,768]{1,0:T(8,128)(2,1)}, bf16[512,768]{1,0:T(8,128)(2,1)}, f32[8,...) custom-call(s32[2]{0:T(128)} %time_ref.1, s32[2]{0:T(128)} %start_ref.1, ...), custom_call_target="tpu_custom_call" | custom-call | flops 3623878656 | bytes 20971520 | tf_op jit(solution)/shard_map/project/pallas_call | solution.py:392
  26.4 22.9 %attend.1 = (bf16[768,1024]{1,0:T(8,128)(2,1)}, bf16[12,1024,1024]{2,1,0:T(8,128)(2,1)}, f32[6,8,1024]{2,1,0:T(8,128)}, bf16[512,768]{1,0:T(8,128)(2,1)}) custom-call(bf16[2304,1024]{1,0:T(8,128)(2,1)} %get-tuple-element.63.q_ref.k_ref.v_ref.refs_0_.refs_1_.refs_2_, bf16[2304,1024]{1,0:T(8,128)(2,1)} %get-tuple-element.63.q_ref.k_ref.v_ref.refs_0_.refs_1_.refs_2_, ...), custom_call_target="tpu_custom_call" | custom-call | flops 12884901888 | bytes 31457280 | tf_op jit(solution)/shard_map/attend/pallas_call | solution.py:471
  49.4 57.6 %middle_links.1 = (bf16[512,768]{1,0:T(8,128)(2,1)}, bf16[512,768]{1,0:T(8,128)(2,1)}, f32[1024,768]{1,0:T(8,128)}, bf16[768,1024]{1,0:T(8,128)(2,1)}, bf16[2,2,...) custom-call(bf16[768,1024]{1,0:T(8,128)(2,1)} %get-tuple-element.64., ...), custom_call_target="tpu_custom_call" | custom-call | flops 32614907904 | bytes 41943040 | tf_op jit(solution)/shard_map/middle_links/pallas_call | solution.py:970
  107.0 93.7 %back.1 = (bf16[512,768]{1,0:T(8,128)(2,1)}, f32[512,768]{1,0:T(8,128)}, bf16[512,768]{1,0:T(8,128)(2,1)}, f32[48,2304]{1,0:T(8,128)}, f32[48,768]{1,0:T(8,128)}...) custom-call(bf16[2304,1024]{1,0:T(8,128)(2,1)} %get-tuple-element.63, ...), custom_call_target="tpu_custom_call" | custom-call | flops 33017561088 | bytes 62914560 | tf_op jit(solution)/shard_map/back/pallas_call | solution.py:1922
  200.7 7.5 %finish_all.1 = (bf16[2,512,768]{2,1,0:T(8,128)(2,1)}, f32[2,512,768]{2,1,0:T(8,128)}, f32[48,2304]{1,0:T(8,128)}, f32[48,768]{1,0:T(8,128)}, f32[48,3072]{1,0:T...) custom-call(bf16[32,32,128]{2,1,0:T(8,128)(2,1)} %bitcast.3, ...), custom_call_target="tpu_custom_call" | custom-call | tf_op jit(solution)/shard_map/finish_all/pallas_call | solution.py:2029
